TPU v7x, 256 devices: a whole 4x4x8 slice. The times are simulated.
256 devices in a mesh: dp: 32 (over x, y, core), pack: 8 (over z).
Axes of the slice: x: 4, y: 4, z: 8, core: 2. Of those that a mesh axis runs over, the one named last changes fastest.
Arguments:
- queries: bfloat16 [40960, 2560], P(('dp', 'pack')), may hold values from -6 to 6
- keys: bfloat16 [40960, 512], P(('dp', 'pack')), may hold values from -6 to 6
- values: bfloat16 [40960, 512], P(('dp', 'pack')), may hold values from -6 to 6
- out_grad: bfloat16 [40960, 2560], P(('dp', 'pack')), may hold values from -6 to 6
- pair_weight: float32 [32, 2], P('dp'), may hold values from 0.3 to 3
- lengths: int32 [32, 2, 3], P('dp'), may hold values from 1 to 640, as said below
- route_dest: int32 [40960], P(('dp', 'pack')), may hold values from 0 to 31, as said below
- route_slot: int32 [40960], P(('dp', 'pack')), may hold values from 0 to 159
Outputs:
- attended: bfloat16 [40960, 2560], P(('dp', 'pack'))
- query_grad: bfloat16 [40960, 2560], P(('dp', 'pack'))
- key_grad: bfloat16 [40960, 512], P(('dp', 'pack'))
- value_grad: bfloat16 [40960, 512], P(('dp', 'pack'))
Inputs may be any that keep to these rules, and one draw needn't show every extreme that they name: `route_dest`: for each pack index the rows of all data ranks fill each data rank's 160 slots exactly once; at most 10 rows of one device go to one data rank, and every device sends exactly 10 to one of them. The lengths of one data rank sum to 1280.
All inputs are finite; a program needn't handle non-finite values.
Results may differ from a plain program's by a relative error of at most 0.018.
Values may be sent and summed in bfloat16 or wider, within the bound.
No kernel may reach another device: no remote copies, remote signals or barrier semaphores. Data moves between devices by JAX's collectives and lax.ppermute only.
A program may use at most 128 MiB of HBM per device.

v0:
```python
import functools
import math

import jax
import jax.numpy as jnp
from jax import lax
from jax.experimental import pallas as pl
from jax.experimental.pallas import tpu as pltpu
from jax.sharding import PartitionSpec as P

HEAD_DIM = 128
HEADS = 20
KV_HEADS = 4
GROUP = 5
CAP = 10
MAIN = 8
SPARE = CAP - MAIN

QUERY_WIDTH = HEADS * HEAD_DIM
KV_WIDTH = KV_HEADS * HEAD_DIM
GROUP_WIDTH = GROUP * HEAD_DIM
PAIR_WIDTH = 2 * HEAD_DIM
SCALING = HEAD_DIM ** (-0.5)
EXPONENT = SCALING * math.log2(math.e)
MASKED = -1e30
VMEM_LIMIT = 60 * 1024 * 1024


def dot(left, right, contract=((1,), (0,))):
    return lax.dot_general(left, right, (contract, ((), ())), preferred_element_type=jnp.float32)


def low(x):
    return x.astype(jnp.bfloat16)


def iota(shape, dim):
    return lax.broadcasted_iota(jnp.int32, shape, dim)


def one_hot(condition):
    return jnp.where(condition, 1.0, 0.0).astype(jnp.bfloat16)


def compiler_params(**extra):
    return pltpu.CompilerParams(vmem_limit_bytes=VMEM_LIMIT, **extra)


def send_kernel(dest_ref, slot_ref, keys_ref, values_ref, send_ref, p1_ref, p2_ref, p1t_ref, p2t_ref):
    rows = keys_ref.shape[0]
    slots = send_ref.shape[0]
    dest_row = dest_ref[...]
    place_row = slot_ref[...] + 1
    down = iota((rows, rows), 0)
    across = iota((rows, rows), 1)
    dest_col = jnp.sum(
        jnp.where(down == across, dest_row.astype(jnp.float32), 0.0), axis=1, keepdims=True
    ).astype(jnp.int32)
    same = dest_col == dest_row
    rank_row = jnp.sum(
        jnp.where(same & (down < across), 1.0, 0.0), axis=0, keepdims=True
    ).astype(jnp.int32)
    rank_col = jnp.sum(
        jnp.where(same & (across < down), 1.0, 0.0), axis=1, keepdims=True
    ).astype(jnp.int32)

    def keys_of(dest, rank):
        first = dest * MAIN + rank
        return (
            jnp.where(rank < MAIN, first, -MAIN),
            jnp.where(rank < MAIN, -MAIN, first - MAIN),
        )

    main_row, spare_row = keys_of(dest_row, rank_row)
    main_col, spare_col = keys_of(dest_col, rank_col)
    slot_down = iota((slots, rows), 0)
    slot_across = iota((rows, slots), 1)
    p1 = slot_down == main_row
    p1_low = one_hot(p1)
    p1_ref[...] = p1_low
    p1t_ref[...] = one_hot(slot_across == main_col)
    place = place_row.astype(jnp.float32)
    place_main = jnp.sum(jnp.where(p1, place, 0.0), axis=1, keepdims=True)
    place_spare = jnp.zeros((slots, 1), jnp.float32)
    spare = jnp.zeros((slots, PAIR_WIDTH), jnp.float32)
    for g in range(KV_HEADS):
        p2 = slot_down == spare_row + SPARE * g
        p2_low = one_hot(p2)
        p2_ref[g] = p2_low
        p2t_ref[g] = one_hot(slot_across == spare_col + SPARE * g)
        place_spare += jnp.sum(jnp.where(p2, place, 0.0), axis=1, keepdims=True)
        source = keys_ref if g < 2 else values_ref
        columns = source[:, (g % 2) * PAIR_WIDTH : (g % 2 + 1) * PAIR_WIDTH]
        send_ref[:, g * PAIR_WIDTH : (g + 1) * PAIR_WIDTH] = low(dot(p1_low, columns))
        spare += dot(p2_low, columns)
    send_ref[:, 4 * PAIR_WIDTH : 5 * PAIR_WIDTH] = low(spare)
    lane = iota((slots, HEAD_DIM), 1)
    send_ref[:, 5 * PAIR_WIDTH :] = low(
        jnp.where(lane == 0, place_main, jnp.where(lane == 1, place_spare, 0.0))
    )


def receive_kernel(recv_ref, kv_ref, r1_ref, r2_ref, r1t_ref, r2t_ref):
    rows = kv_ref.shape[0]
    slots = recv_ref.shape[0]
    tile = recv_ref[:, 5 * PAIR_WIDTH :].astype(jnp.float32)
    lane = iota((slots, HEAD_DIM), 1)
    main_col = jnp.sum(jnp.where(lane == 0, tile, 0.0), axis=1, keepdims=True)
    spare_col = jnp.sum(jnp.where(lane == 1, tile, 0.0), axis=1, keepdims=True)
    diagonal = iota((slots, slots), 0) == iota((slots, slots), 1)
    main_row = jnp.sum(jnp.where(diagonal, main_col, 0.0), axis=0, keepdims=True).astype(jnp.int32)
    spare_row = jnp.sum(jnp.where(diagonal, spare_col, 0.0), axis=0, keepdims=True).astype(jnp.int32)
    main_col = main_col.astype(jnp.int32)
    spare_col = spare_col.astype(jnp.int32)
    place_across = iota((slots, rows), 1) + 1
    place_down = iota((rows, slots), 0) + 1
    part_down = (iota((slots, rows), 0) & (MAIN - 1)) >> 1
    part_across = (iota((rows, slots), 1) & (MAIN - 1)) >> 1
    r1_ref[...] = one_hot(place_across == main_col)
    r1t = one_hot(place_down == main_row)
    r1t_ref[...] = r1t
    spare = recv_ref[:, 4 * PAIR_WIDTH : 5 * PAIR_WIDTH]
    for g in range(KV_HEADS):
        r2_ref[g] = one_hot((place_across == spare_col) & (part_down == g))
        r2t = one_hot((place_down == spare_row) & (part_across == g))
        r2t_ref[g] = r2t
        columns = slice(g * PAIR_WIDTH, (g + 1) * PAIR_WIDTH)
        kv_ref[:, columns] = low(dot(r1t, recv_ref[:, columns]) + dot(r2t, spare))


def pack_kernel(source_ref, m1_ref, m2_ref, send_ref):
    width = source_ref.shape[1] // KV_HEADS
    m1 = m1_ref[...]
    spare = jnp.zeros((send_ref.shape[0], width), jnp.float32)
    for g in range(KV_HEADS):
        columns = slice(g * width, (g + 1) * width)
        part = low(source_ref[:, columns])
        send_ref[:, columns] = low(dot(m1, part))
        spare += dot(m2_ref[g], part)
    send_ref[:, KV_HEADS * width :] = low(spare)


def unpack_kernel(recv_ref, m1_ref, m2_ref, out_ref):
    width = out_ref.shape[1] // KV_HEADS
    m1 = m1_ref[...]
    spare = recv_ref[:, KV_HEADS * width :]
    for g in range(KV_HEADS):
        columns = slice(g * width, (g + 1) * width)
        out_ref[:, columns] = low(dot(m1, recv_ref[:, columns]) + dot(m2_ref[g], spare))


def unpack_kv_kernel(recv_ref, m1_ref, m2_ref, key_ref, value_ref):
    m1 = m1_ref[...]
    spare = recv_ref[:, KV_HEADS * PAIR_WIDTH :]
    for g in range(KV_HEADS):
        both = low(
            dot(m1, recv_ref[:, g * PAIR_WIDTH : (g + 1) * PAIR_WIDTH]) + dot(m2_ref[g], spare)
        )
        key_ref[:, g * HEAD_DIM : (g + 1) * HEAD_DIM] = both[:, :HEAD_DIM]
        value_ref[:, g * HEAD_DIM : (g + 1) * HEAD_DIM] = both[:, HEAD_DIM:]


def ends_of(info_ref):
    ends = [info_ref[0]]
    for k in range(1, 6):
        ends.append(ends[-1] + info_ref[k])
    return ends


def forward_kernel(
    info_ref, main_ref, spare_ref, key_ref, value_ref, r1t_ref, r2t_ref, r1_ref, r2_ref,
    query_ref, attended_ref, prob_ref, send_ref, bias, spare_sum,
):
    g = pl.program_id(0)
    rows = query_ref.shape[0]
    keys = key_ref.shape[0]

    @pl.when(g == 0)
    def _():
        e0, e1, e2, e3, e4, _ = ends_of(info_ref)
        place = info_ref[6] * rows + iota((rows, 1), 0)
        first = jnp.where(place >= e2, e2, 0)
        rejected = (place >= e1) & (place < e2)
        hidden_from = jnp.where(place >= e4, e3, jnp.where(rejected, e0, 0))
        hidden_to = jnp.where(place >= e4, e4, jnp.where(rejected, e1, 0))
        other = iota((rows, keys), 1)
        seen = (other >= first) & (other <= place) & ((other < hidden_from) | (other >= hidden_to))
        bias[...] = jnp.where(seen, 0.0, MASKED)
        spare_sum[...] = jnp.zeros_like(spare_sum)

    query = low(dot(r1t_ref[...], main_ref[...]) + dot(r2t_ref[0], spare_ref[...]))
    query_ref[...] = query
    key = key_ref[...]
    value = value_ref[...]
    parts = []
    for h in range(GROUP):
        score = dot(query[:, h * HEAD_DIM : (h + 1) * HEAD_DIM], key, ((1,), (1,))) + bias[...]
        highest = jnp.max(score, axis=1, keepdims=True)
        raised = jnp.exp2((score - highest) * EXPONENT)
        total = jnp.sum(raised, axis=1, keepdims=True)
        prob = low(raised * (1.0 / total))
        prob_ref[h * rows : (h + 1) * rows, :] = prob
        parts.append(low(dot(prob, value)))
    attended = jnp.concatenate(parts, axis=1)
    attended_ref[...] = attended
    send_ref[:, pl.ds(pl.multiple_of(g * GROUP_WIDTH, GROUP_WIDTH), GROUP_WIDTH)] = low(
        dot(r1_ref[...], attended)
    )
    spare_sum[...] += dot(r2_ref[0], attended)

    @pl.when(g == KV_HEADS - 1)
    def _():
        send_ref[:, KV_HEADS * GROUP_WIDTH :] = low(spare_sum[...])


def backward_kernel(
    info_ref, weight_ref, main_ref, spare_ref, key_ref, value_ref, r1t_ref, r2t_ref, r1_ref, r2_ref,
    query_ref, attended_ref, prob_ref, kv_ref, send_ref, spare_sum,
):
    g = pl.program_id(0)
    rows = query_ref.shape[0]

    @pl.when(g == 0)
    def _():
        spare_sum[...] = jnp.zeros_like(spare_sum)

    _, e1, e2, _, e4, _ = ends_of(info_ref)
    place = info_ref[6] * rows + iota((rows, 1), 0)
    weight = jnp.where(place >= e2, weight_ref[1], weight_ref[0])
    rejected = ((place >= e1) & (place < e2)) | (place >= e4)
    factor = jnp.where(rejected, -weight, weight)
    grad = dot(r1t_ref[...], main_ref[...]) + dot(r2t_ref[0], spare_ref[...])
    cotangent = low(factor * grad)
    query = query_ref[...]
    attended = attended_ref[...]
    key = key_ref[...]
    value = value_ref[...]
    parts = []
    key_sum = jnp.zeros((HEAD_DIM, key.shape[0]), jnp.float32)
    value_sum = jnp.zeros((HEAD_DIM, key.shape[0]), jnp.float32)
    for h in range(GROUP):
        columns = slice(h * HEAD_DIM, (h + 1) * HEAD_DIM)
        cot = cotangent[:, columns]
        delta = jnp.sum(
            cot.astype(jnp.float32) * attended[:, columns].astype(jnp.float32), axis=1, keepdims=True
        )
        prob = prob_ref[h * rows : (h + 1) * rows, :]
        dscore = low(prob.astype(jnp.float32) * (dot(cot, value, ((1,), (1,))) - delta))
        parts.append(low(SCALING * dot(dscore, key)))
        key_sum += dot(query[:, columns].T, dscore)
        value_sum += dot(cot.T, prob)
    kv_ref[:, :HEAD_DIM] = low((SCALING * key_sum).T)
    kv_ref[:, HEAD_DIM:] = low(value_sum.T)
    query_grad = jnp.concatenate(parts, axis=1)
    send_ref[:, pl.ds(pl.multiple_of(g * GROUP_WIDTH, GROUP_WIDTH), GROUP_WIDTH)] = low(
        dot(r1_ref[...], query_grad)
    )
    spare_sum[...] += dot(r2_ref[0], query_grad)

    @pl.when(g == KV_HEADS - 1)
    def _():
        send_ref[:, KV_HEADS * GROUP_WIDTH :] = low(spare_sum[...])


def shape(dims, kind=jnp.bfloat16):
    return jax.ShapeDtypeStruct(dims, kind)


def cost(flops, moved, exps=0):
    return pl.CostEstimate(flops=int(flops), bytes_accessed=int(moved), transcendentals=int(exps))


def body(queries, keys, values, out_grad, pair_weight, lengths, route_dest, route_slot):
    rows = queries.shape[0]
    ranks = lax.axis_size("dp")
    packs = lax.axis_size("pack")
    seq = rows * packs
    slots = ranks * MAIN
    wide = (KV_HEADS + 1) * GROUP_WIDTH
    narrow = (KV_HEADS + 1) * PAIR_WIDTH
    fence = lax.optimization_barrier

    def exchange(block):
        moved = lax.all_to_all(
            block.reshape(ranks, MAIN, block.shape[1]), "dp", split_axis=0, concat_axis=0, tiled=True
        )
        return moved.reshape(block.shape)

    maps = (
        shape((slots, rows)),
        shape((KV_HEADS, slots, rows)),
        shape((rows, slots)),
        shape((KV_HEADS, rows, slots)),
    )

    def pack(source, m1, m2):
        width = source.shape[1]
        return pl.pallas_call(
            pack_kernel,
            out_shape=shape((slots, width // KV_HEADS * (KV_HEADS + 1))),
            compiler_params=compiler_params(),
            cost_estimate=cost(400 * slots * rows * width, 5 * slots * width),
        )(source, m1, m2)

    kv_send, p1, p2, p1t, p2t = pl.pallas_call(
        send_kernel,
        out_shape=(shape((slots, narrow + HEAD_DIM)), *maps),
        compiler_params=compiler_params(),
        cost_estimate=cost(4 * slots * rows * 2 * KV_WIDTH, 6 * slots * 2 * KV_WIDTH),
    )(route_dest.reshape(1, rows), route_slot.reshape(1, rows), keys, values)

    kv_recv = exchange(kv_send)
    query_send = pack(queries, p1, p2)
    grad_send = pack(out_grad, p1, p2)
    kv_recv, query_send, grad_send = fence((kv_recv, query_send, grad_send))

    kv_own, r1, r2, r1t, r2t = pl.pallas_call(
        receive_kernel,
        out_shape=(shape((rows, 2 * KV_WIDTH)), *maps),
        compiler_params=compiler_params(),
        cost_estimate=cost(4 * slots * rows * 2 * KV_WIDTH, 6 * slots * 2 * KV_WIDTH),
    )(kv_recv)
    kv_all = lax.all_gather(kv_own, "pack", axis=0, tiled=True)

    query_recv = exchange(query_send)
    query_recv, grad_send = fence((query_recv, grad_send))
    grad_recv = exchange(grad_send)

    info = jnp.concatenate(
        [lengths.reshape(6), lax.axis_index("pack").astype(jnp.int32).reshape(1)]
    )
    smem = pl.BlockSpec(memory_space=pltpu.SMEM)
    main_spec = pl.BlockSpec((slots, GROUP_WIDTH), lambda g: (0, g))
    spare_spec = pl.BlockSpec((slots, GROUP_WIDTH), lambda g: (0, KV_HEADS))
    key_spec = pl.BlockSpec((seq, HEAD_DIM), lambda g: (0, g))
    value_spec = pl.BlockSpec((seq, HEAD_DIM), lambda g: (0, KV_HEADS + g))
    map_specs = [
        pl.BlockSpec((rows, slots), lambda g: (0, 0)),
        pl.BlockSpec((1, rows, slots), lambda g: (g, 0, 0)),
        pl.BlockSpec((slots, rows), lambda g: (0, 0)),
        pl.BlockSpec((1, slots, rows), lambda g: (g, 0, 0)),
    ]
    row_spec = pl.BlockSpec((rows, GROUP_WIDTH), lambda g: (0, g))
    prob_spec = pl.BlockSpec((GROUP * rows, seq), lambda g: (g, 0))
    send_spec = pl.BlockSpec((slots, wide), lambda g: (0, 0))
    work = HEADS * rows * seq * HEAD_DIM
    query_rows, attended, probs, attended_send = pl.pallas_call(
        forward_kernel,
        grid=(KV_HEADS,),
        in_specs=[smem, main_spec, spare_spec, key_spec, value_spec, *map_specs],
        out_specs=(row_spec, row_spec, prob_spec, send_spec),
        out_shape=(
            shape((rows, QUERY_WIDTH)),
            shape((rows, QUERY_WIDTH)),
            shape((HEADS * rows, seq)),
            shape((slots, wide)),
        ),
        scratch_shapes=[
            pltpu.VMEM((rows, seq), jnp.float32),
            pltpu.VMEM((slots, GROUP_WIDTH), jnp.float32),
        ],
        compiler_params=compiler_params(dimension_semantics=("arbitrary",)),
        cost_estimate=cost(4 * work, 2 * HEADS * rows * seq, HEADS * rows * seq),
    )(info, query_recv, query_recv, kv_all, kv_all, r1t, r2t, r1, r2)

    grad_recv, attended_send = fence((grad_recv, attended_send))
    attended_back = exchange(attended_send)

    kv_part, qgrad_send = pl.pallas_call(
        backward_kernel,
        grid=(KV_HEADS,),
        in_specs=[
            smem, smem, main_spec, spare_spec, key_spec, value_spec, *map_specs,
            row_spec, row_spec, prob_spec,
        ],
        out_specs=(pl.BlockSpec((seq, PAIR_WIDTH), lambda g: (0, g)), send_spec),
        out_shape=(shape((seq, 2 * KV_WIDTH)), shape((slots, wide))),
        scratch_shapes=[pltpu.VMEM((slots, GROUP_WIDTH), jnp.float32)],
        compiler_params=compiler_params(dimension_semantics=("arbitrary",)),
        cost_estimate=cost(8 * work, 2 * HEADS * rows * seq),
    )(
        info, pair_weight.reshape(2), grad_recv, grad_recv, kv_all, kv_all, r1t, r2t, r1, r2,
        query_rows, attended, probs,
    )

    kv_grad = lax.psum_scatter(kv_part, "pack", scatter_dimension=0, tiled=True)
    attended_back, qgrad_send = fence((attended_back, qgrad_send))
    qgrad_back = exchange(qgrad_send)

    def unpack(block):
        return pl.pallas_call(
            unpack_kernel,
            out_shape=shape((rows, QUERY_WIDTH)),
            compiler_params=compiler_params(),
            cost_estimate=cost(400 * slots * rows * QUERY_WIDTH, 4 * slots * QUERY_WIDTH),
        )(block, p1t, p2t)

    kv_grad_send = pack(kv_grad, r1, r2)
    qgrad_back, kv_grad_send = fence((qgrad_back, kv_grad_send))
    kv_back = exchange(kv_grad_send)
    key_grad, value_grad = pl.pallas_call(
        unpack_kv_kernel,
        out_shape=(shape((rows, KV_WIDTH)), shape((rows, KV_WIDTH))),
        compiler_params=compiler_params(),
        cost_estimate=cost(4 * slots * rows * 2 * KV_WIDTH, 4 * slots * 2 * KV_WIDTH),
    )(kv_back, p1t, p2t)
    return unpack(attended_back), unpack(qgrad_back), key_grad, value_grad


def solution(mesh):
    rows = P(("dp", "pack"), None)
    flat = P(("dp", "pack"))
    return jax.shard_map(
        body,
        mesh=mesh,
        in_specs=(rows, rows, rows, rows, P("dp", None), P("dp", None, None), flat, flat),
        out_specs=(rows, rows, rows, rows),
        check_vma=False,
    )
```

profile of v0, /device:TPU:1, one launch (start us, length us, event | category | flops | bytes accessed | tf_op | source)
XLA Modules:
  0.0 193.7 jit_solution(14921366034209346561)
XLA Ops:
  7.2 2.7 %shard_map.111 = (bf16[256,1408]{1,0:T(8,128)(2,1)}, bf16[256,160]{1,0:T(8,128)(2,1)}, bf16[4,256,160]{2,1,0:T(8,128)(2,1)}, bf16[160,256]{1,0:T(8,128)(2,1)}, bf16[4,160,256]{2,1,0:T(8,128)(2,1)}) custom-call(s32[1,160]{1,0:T(1,128)} %bitcast.29, s32[1,160]{1,0:T(1,128)} %bitcast.30, bf16[160,512]{1,0:T(8,128)(2,1)} %keys_ref.1, bf16[160,512]{1,0:T(8,128)(2,1)} %values_ref.1), custom_call_target="tpu_custom_call" | custom-call | flops 167772160 | bytes 1572864 | tf_op jit(solution)/shard_map/pallas_call | solution.py:305
  9.8 8.6 %all-to-all-start = ((bf16[32,8,1408]{2,1,0:T(8,128)(2,1)}), bf16[32,8,1408]{2,1,0:T(8,128)(2,1)S(1)}, u32[]{:S(2)}, u32[]{:S(2)}) async-start(bf16[32,8,1408]{2,1,0:T(8,128)(2,1)} %bitcast.26), calls=%async_computation | async-start | bytes 1441792 | tf_op jit(solution)/shard_map/all_to_all | solution.py:284
  18.4 0.0 all-gather.2.cloned.1.call-start
  18.5 3.5 %shard_map.113 = bf16[256,3200]{1,0:T(8,128)(2,1)} custom-call(bf16[160,2560]{1,0:T(8,128)(2,1)} %source_ref.3, bf16[256,160]{1,0:T(8,128)(2,1)} %get-tuple-element.34.m1_ref, bf16[4,256,160]{2,1,0:T(8,128)(2,1)} %get-tuple-element.35.m2_ref), custom_call_target="tpu_custom_call" | custom-call | flops 41943040000 | bytes 3276800 | tf_op jit(solution)/shard_map/pallas_call | solution.py:298
  22.0 3.5 %shard_map.112 = bf16[256,3200]{1,0:T(8,128)(2,1)} custom-call(bf16[160,2560]{1,0:T(8,128)(2,1)} %source_ref.2, bf16[256,160]{1,0:T(8,128)(2,1)} %get-tuple-element.34.m1_ref, bf16[4,256,160]{2,1,0:T(8,128)(2,1)} %get-tuple-element.35.m2_ref), custom_call_target="tpu_custom_call" | custom-call | flops 41943040000 | bytes 3276800 | tf_op jit(solution)/shard_map/pallas_call | solution.py:298
  25.5 6.5 %all-to-all-done = bf16[32,8,1408]{2,1,0:T(8,128)(2,1)S(1)} async-done(((bf16[32,8,1408]{2,1,0:T(8,128)(2,1)}), bf16[32,8,1408]{2,1,0:T(8,128)(2,1)S(1)}, u32[]{:S(2)}, u32[]{:S(2)}) %all-to-all-start) | async-done | bytes 720928 | tf_op jit(solution)/shard_map/all_to_all | solution.py:284
  32.0 0.0 copy-start.1
  32.0 0.9 copy-done.1
  32.9 2.5 %shard_map.114 = (bf16[160,1024]{1,0:T(8,128)(2,1)}, bf16[256,160]{1,0:T(8,128)(2,1)}, bf16[4,256,160]{2,1,0:T(8,128)(2,1)}, bf16[160,256]{1,0:T(8,128)(2,1)}, bf16[4,160,256]{2,1,0:T(8,128)(2,1)}) custom-call(bf16[256,1408]{1,0:T(8,128)(2,1)} %bitcast.20), custom_call_target="tpu_custom_call" | custom-call | flops 167772160 | bytes 1572864 | tf_op jit(solution)/shard_map/pallas_call | solution.py:317
  35.3 0.0 all-gather.2.cloned.1.call-update
  35.4 27.8 %all_to_all.30 = bf16[32,8,3200]{2,1,0:T(8,128)(2,1)} all-to-all(bf16[32,8,3200]{2,1,0:T(8,128)(2,1)} %bitcast.25), channel_id=1, replica_groups=mesh['dp'=32,'pack'=8] {'dp'}, dimensions={0} | all-to-all | bytes 3276800 | tf_op jit(solution)/shard_map/all_to_all | solution.py:284
  63.2 0.0 copy-start.5
  63.2 3.9 %all-to-all-start.2 = ((bf16[32,8,3200]{2,1,0:T(8,128)(2,1)}), bf16[32,8,3200]{2,1,0:T(8,128)(2,1)S(1)}, u32[]{:S(2)}, u32[]{:S(2)}) async-start(bf16[32,8,3200]{2,1,0:T(8,128)(2,1)} %bitcast.6), calls=%async_computation.2 | async-start | bytes 3276800 | tf_op jit(solution)/shard_map/all_to_all | solution.py:284
  67.1 0.0 copy-done.5
  67.1 0.1 reshape.67
  67.2 0.6 pad_add_fusion.info_ref
  67.8 6.1 %all-gather.2.cloned.1.call-done.key_ref.value_ref = bf16[1280,1024]{1,0:T(8,128)(2,1)} async-done(((bf16[160,1024]{1,0:T(8,128)(2,1)}), bf16[1280,1024]{1,0:T(8,128)(2,1)}) %all-gather.2.cloned.1.call-update) | async-done | bytes 2621456 | tf_op jit(solution)/shard_map/all_gather | solution.py:323
  73.9 18.0 %shard_map.115 = (bf16[160,2560]{1,0:T(8,128)(2,1)}, bf16[160,2560]{1,0:T(8,128)(2,1)}, bf16[3200,1280]{1,0:T(8,128)(2,1)}, bf16[256,3200]{1,0:T(8,128)(2,1)}) custom-call(s32[7]{0:T(128)} %pad_add_fusion.info_ref, bf16[256,3200]{1,0:T(8,128)(2,1)} %bitcast.18, bf16[256,3200]{1,0:T(8,128)(2,1)} %bitcast.19, ...), custom_call_target="tpu_custom_call" | custom-call | flops 2097152000 | bytes 8192000 | tf_op jit(solution)/shard_map/pallas_call | solution.py:347
  91.8 0.0 all-to-all-done.2
  91.8 0.0 copy-start
  91.8 1.2 copy-done
  93.0 10.5 %all-to-all-start.3 = ((bf16[32,8,3200]{2,1,0:T(8,128)(2,1)}), bf16[32,8,3200]{2,1,0:T(8,128)(2,1)S(1)}, u32[]{:S(2)}, u32[]{:S(2)}) async-start(bf16[32,8,3200]{2,1,0:T(8,128)(2,1)} %bitcast.23), calls=%async_computation.3 | async-start | bytes 3276800 | tf_op jit(solution)/shard_map/all_to_all | solution.py:284
  103.5 0.0 reduce-scatter.2.cloned.1.call-start
  103.5 14.7 %shard_map.116 = (bf16[1280,1024]{1,0:T(8,128)(2,1)}, bf16[256,3200]{1,0:T(8,128)(2,1)}) custom-call(s32[7]{0:T(128)} %pad_add_fusion.info_ref, f32[2]{0:T(128)} %bitcast.28, bf16[256,3200]{1,0:T(8,128)(2,1)} %bitcast.16, bf16[256,3200]{1,0:T(8,128)(2,1)} %bitcast.17, bf16[1280,1024]{1,0:T(8,128)(2,1)} %all-gather.2.cloned.1.call-done.key_ref.value_ref, ...), custom_call_target="tpu_custom_call" | custom-call | flops 4194304000 | bytes 8192000 | tf_op jit(solution)/shard_map/pallas_call | solution.py:369
  118.2 0.0 reduce-scatter.2.cloned.1.call-update
  118.3 8.6 %all-to-all-done.3 = bf16[32,8,3200]{2,1,0:T(8,128)(2,1)S(1)} async-done(((bf16[32,8,3200]{2,1,0:T(8,128)(2,1)}), bf16[32,8,3200]{2,1,0:T(8,128)(2,1)S(1)}, u32[]{:S(2)}, u32[]{:S(2)}) %all-to-all-start.3) | async-done | bytes 1638432 | tf_op jit(solution)/shard_map/all_to_all | solution.py:284
  126.9 0.0 copy-start.3
  126.9 1.2 copy-done.3
  128.1 4.3 %all-to-all-start.4 = ((bf16[32,8,3200]{2,1,0:T(8,128)(2,1)}), bf16[32,8,3200]{2,1,0:T(8,128)(2,1)S(1)}, u32[]{:S(2)}, u32[]{:S(2)}) async-start(bf16[32,8,3200]{2,1,0:T(8,128)(2,1)} %bitcast.12), calls=%async_computation.4 | async-start | bytes 3276800 | tf_op jit(solution)/shard_map/all_to_all | solution.py:284
  132.4 3.1 %shard_map.117 = bf16[160,2560]{1,0:T(8,128)(2,1)} custom-call(bf16[256,3200]{1,0:T(8,128)(2,1)} %bitcast.22, bf16[160,256]{1,0:T(8,128)(2,1)} %get-tuple-element.54.m1_ref, bf16[4,160,256]{2,1,0:T(8,128)(2,1)} %get-tuple-element.55.m2_ref), custom_call_target="tpu_custom_call" | custom-call | flops 41943040000 | bytes 2621440 | tf_op jit(solution)/shard_map/pallas_call | solution.py:391
  135.5 21.7 %reduce-scatter.2.cloned.1.call-done.source_ref = bf16[160,1024]{1,0:T(8,128)(2,1)} async-done(((bf16[1280,1024]{1,0:T(8,128)(2,1)}), bf16[160,1024]{1,0:T(8,128)(2,1)}) %reduce-scatter.2.cloned.1.call-update) | async-done | bytes 327696 | tf_op jit(solution)/shard_map/reduce_scatter | solution.py:386
  157.2 2.5 %shard_map.118 = bf16[256,1280]{1,0:T(8,128)(2,1)} custom-call(bf16[160,1024]{1,0:T(8,128)(2,1)} %reduce-scatter.2.cloned.1.call-done.source_ref, bf16[256,160]{1,0:T(8,128)(2,1)} %get-tuple-element.44.r1_ref.m1_ref, bf16[4,256,160]{2,1,0:T(8,128)(2,1)} %get-tuple-element.45.r2_ref.m2_ref), custom_call_target="tpu_custom_call" | custom-call | flops 16777216000 | bytes 1310720 | tf_op jit(solution)/shard_map/pallas_call | solution.py:298
  159.6 0.0 all-to-all-done.4
  159.6 0.0 copy-start.4
  159.6 11.2 %all-to-all-start.5 = ((bf16[32,8,1280]{2,1,0:T(8,128)(2,1)}), bf16[32,8,1280]{2,1,0:T(8,128)(2,1)S(1)}, u32[]{:S(2)}, u32[]{:S(2)}) async-start(bf16[32,8,1280]{2,1,0:T(8,128)(2,1)} %bitcast.27), calls=%async_computation.6 | async-start | bytes 1310720 | tf_op jit(solution)/shard_map/all_to_all | solution.py:284
  170.8 0.0 copy-done.4
  170.8 3.1 %shard_map.119 = bf16[160,2560]{1,0:T(8,128)(2,1)} custom-call(bf16[256,3200]{1,0:T(8,128)(2,1)} %bitcast.24, bf16[160,256]{1,0:T(8,128)(2,1)} %get-tuple-element.54.m1_ref, bf16[4,160,256]{2,1,0:T(8,128)(2,1)} %get-tuple-element.55.m2_ref), custom_call_target="tpu_custom_call" | custom-call | flops 41943040000 | bytes 2621440 | tf_op jit(solution)/shard_map/pallas_call | solution.py:391
  173.9 9.8 %all-to-all-done.5 = bf16[32,8,1280]{2,1,0:T(8,128)(2,1)S(1)} async-done(((bf16[32,8,1280]{2,1,0:T(8,128)(2,1)}), bf16[32,8,1280]{2,1,0:T(8,128)(2,1)S(1)}, u32[]{:S(2)}, u32[]{:S(2)}) %all-to-all-start.5) | async-done | bytes 655392 | tf_op jit(solution)/shard_map/all_to_all | solution.py:284
  183.7 0.0 copy-start.2
  183.7 0.9 copy-done.2
  184.6 2.3 %shard_map.120 = (bf16[160,512]{1,0:T(8,128)(2,1)}, bf16[160,512]{1,0:T(8,128)(2,1)}) custom-call(bf16[256,1280]{1,0:T(8,128)(2,1)} %bitcast.21, bf16[160,256]{1,0:T(8,128)(2,1)} %get-tuple-element.54.m1_ref, bf16[4,160,256]{2,1,0:T(8,128)(2,1)} %get-tuple-element.55.m2_ref), custom_call_target="tpu_custom_call" | custom-call | flops 167772160 | bytes 1048576 | tf_op jit(solution)/shard_map/pallas_call | solution.py:401
Async XLA Ops:
  9.8 22.2 %all-to-all-start = ((bf16[32,8,1408]{2,1,0:T(8,128)(2,1)}), bf16[32,8,1408]{2,1,0:T(8,128)(2,1)S(1)}, u32[]{:S(2)}, u32[]{:S(2)}) async-start(bf16[32,8,1408]{2,1,0:T(8,128)(2,1)} %bitcast.26), calls=%async_computation | async-start | bytes 1441792 | tf_op jit(solution)/shard_map/all_to_all | solution.py:284
  18.4 55.4 %all-gather.2.cloned.1.call-start = ((), (), s32[]{:S(2)}) async-start(), calls=%async_computation.7 | async-start | bytes 2949120 | tf_op jit(solution)/shard_map/all_gather | solution.py:323
  32.0 0.9 copy-start.1
  63.2 3.9 %copy-start.5 = (s32[1,2,3]{2,1,0:T(2,128)S(1)}, s32[1,2,3]{2,1,0:T(2,128)}, u32[]{:S(2)}) copy-start(s32[1,2,3]{2,1,0:T(2,128)} %param.13) | copy-start | bytes 76
  63.2 28.6 %all-to-all-start.2 = ((bf16[32,8,3200]{2,1,0:T(8,128)(2,1)}), bf16[32,8,3200]{2,1,0:T(8,128)(2,1)S(1)}, u32[]{:S(2)}, u32[]{:S(2)}) async-start(bf16[32,8,3200]{2,1,0:T(8,128)(2,1)} %bitcast.6), calls=%async_computation.2 | async-start | bytes 3276800 | tf_op jit(solution)/shard_map/all_to_all | solution.py:284
  91.8 1.2 copy-start
  93.0 33.9 %all-to-all-start.3 = ((bf16[32,8,3200]{2,1,0:T(8,128)(2,1)}), bf16[32,8,3200]{2,1,0:T(8,128)(2,1)S(1)}, u32[]{:S(2)}, u32[]{:S(2)}) async-start(bf16[32,8,3200]{2,1,0:T(8,128)(2,1)} %bitcast.23), calls=%async_computation.3 | async-start | bytes 3276800 | tf_op jit(solution)/shard_map/all_to_all | solution.py:284
  103.5 53.7 %reduce-scatter.2.cloned.1.call-start = ((), (), s32[]{:S(2)}) async-start(), calls=%async_computation.8 | async-start | bytes 2949120 | tf_op jit(solution)/shard_map/reduce_scatter | solution.py:386
  126.9 1.2 copy-start.3
  128.1 31.6 %all-to-all-start.4 = ((bf16[32,8,3200]{2,1,0:T(8,128)(2,1)}), bf16[32,8,3200]{2,1,0:T(8,128)(2,1)S(1)}, u32[]{:S(2)}, u32[]{:S(2)}) async-start(bf16[32,8,3200]{2,1,0:T(8,128)(2,1)} %bitcast.12), calls=%async_computation.4 | async-start | bytes 3276800 | tf_op jit(solution)/shard_map/all_to_all | solution.py:284
  159.6 11.2 %copy-start.4 = (bf16[32,8,3200]{2,1,0:T(8,128)(2,1)}, bf16[32,8,3200]{2,1,0:T(8,128)(2,1)S(1)}, u32[]{:S(2)}) copy-start(bf16[32,8,3200]{2,1,0:T(8,128)(2,1)S(1)} %all-to-all-done.4) | copy-start | bytes 4915204
  159.6 24.1 %all-to-all-start.5 = ((bf16[32,8,1280]{2,1,0:T(8,128)(2,1)}), bf16[32,8,1280]{2,1,0:T(8,128)(2,1)S(1)}, u32[]{:S(2)}, u32[]{:S(2)}) async-start(bf16[32,8,1280]{2,1,0:T(8,128)(2,1)} %bitcast.27), calls=%async_computation.6 | async-start | bytes 1310720 | tf_op jit(solution)/shard_map/all_to_all | solution.py:284
  183.7 0.9 copy-start.2
Sparse Core Ops, SparseCore 0:
  35.5 38.3 all-gather.1
  118.4 38.7 reduce-scatter.1
where the time goes:
time: 195 us; the launch traced here: 194 us
  Pallas kernels  55.8 us (29%)
  waiting for transfers between devices  52.7 us (27%)
  starting transfers between devices  38.5 us (20%)
  blocking collectives  27.8 us (14%)
  between operations  14.1 us (7%)
  local copies, waits for them, and re-layouts  4.17 us (2%)
    all_to_all x5, starting transfers between devices, exchange(): lax.all_to_all(block.reshape(ranks, MAIN, block.shape[1]), 'dp', split_ax...  38.5 us
    all_to_all x1, blocking collectives, exchange(): lax.all_to_all(block.reshape(ranks, MAIN, block.shape[1]), 'dp', split_ax...  27.8 us
    all_to_all x5, waiting for transfers between devices, exchange(): lax.all_to_all(block.reshape(ranks, MAIN, block.shape[1]), 'dp', split_ax...  24.9 us
    reduce_scatter x1, waiting for transfers between devices, body(): kv_grad = lax.psum_scatter(kv_part, 'pack', scatter_dimension=0, tiled=True)  21.7 us
    pallas_call x1, Pallas kernels, body(): pl.pallas_call(forward_kernel, grid=(KV_HEADS,), in_specs=[smem, main_spe...  18 us
    pallas_call x1, Pallas kernels, body(): pl.pallas_call(backward_kernel, grid=(KV_HEADS,), in_specs=[smem, smem, m...  14.7 us
    pallas_call x3, Pallas kernels, pack(): pl.pallas_call(pack_kernel, out_shape=shape((slots, width // KV_HEADS * (...  9.53 us
    pallas_call x2, Pallas kernels, unpack(): pl.pallas_call(unpack_kernel, out_shape=shape((rows, QUERY_WIDTH)), compi...  6.19 us
  transfers between devices with their start and end apart: 7, of which 5 were waited for; matrix products, arithmetic and copies ran while one was open for 0% of the time, Pallas kernels for 25%

commit v1 on v0

v1 whole, which is shorter than its diff:
```python
import functools
import math

import jax
import jax.numpy as jnp
from jax import lax
from jax.experimental import pallas as pl
from jax.experimental.pallas import tpu as pltpu
from jax.sharding import PartitionSpec as P

HEAD_DIM = 128
HEADS = 20
KV_HEADS = 4
GROUP = 5
CAP = 10
MAIN = 8
SPARE = CAP - MAIN

QUERY_WIDTH = HEADS * HEAD_DIM
KV_WIDTH = KV_HEADS * HEAD_DIM
GROUP_WIDTH = GROUP * HEAD_DIM
PAIR_WIDTH = 2 * HEAD_DIM
SCALING = HEAD_DIM ** (-0.5)
EXPONENT = SCALING * math.log2(math.e)
MASKED = -1e30
VMEM_LIMIT = 60 * 1024 * 1024
SMALL_VMEM = 16 * 1024 * 1024
BOTH_WIDTH = 2 * GROUP_WIDTH
LONG = 10**11


def dot(left, right, contract=((1,), (0,))):
    return lax.dot_general(left, right, (contract, ((), ())), preferred_element_type=jnp.float32)


def low(x):
    return x.astype(jnp.bfloat16)


def iota(shape, dim):
    return lax.broadcasted_iota(jnp.int32, shape, dim)


def one_hot(condition):
    return jnp.where(condition, 1.0, 0.0).astype(jnp.bfloat16)


def compiler_params(limit=VMEM_LIMIT, **extra):
    return pltpu.CompilerParams(vmem_limit_bytes=limit, **extra)


def ranks_of(dest_row):
    rows = dest_row.shape[1]
    down = iota((rows, rows), 0)
    across = iota((rows, rows), 1)
    dest_col = jnp.sum(
        jnp.where(down == across, dest_row.astype(jnp.float32), 0.0), axis=1, keepdims=True
    ).astype(jnp.int32)
    return dest_col, dest_col == dest_row, down, across


def places_of(dest, rank):
    rank = rank.astype(jnp.int32)
    first = dest * MAIN + rank
    return jnp.where(rank < MAIN, first, -MAIN), jnp.where(rank < MAIN, -MAIN, first - MAIN)


def send_kernel(dest_ref, slot_ref, keys_ref, values_ref, send_ref, p1_ref, p2_ref):
    rows = keys_ref.shape[0]
    slots = send_ref.shape[0]
    dest_row = dest_ref[...]
    _, same, down, across = ranks_of(dest_row)
    rank_row = jnp.sum(jnp.where(same & (down < across), 1.0, 0.0), axis=0, keepdims=True)
    main_row, spare_row = places_of(dest_row, rank_row)
    slot_down = iota((slots, rows), 0)
    p1 = slot_down == main_row
    p1_low = one_hot(p1)
    p1_ref[...] = p1_low
    place = (slot_ref[...] + 1).astype(jnp.float32)
    place_main = jnp.sum(jnp.where(p1, place, 0.0), axis=1, keepdims=True)
    taken = jnp.zeros((slots, rows), jnp.float32)
    spare = jnp.zeros((slots, PAIR_WIDTH), jnp.float32)
    for g in range(KV_HEADS):
        p2 = slot_down == spare_row + SPARE * g
        p2_low = one_hot(p2)
        p2_ref[g] = p2_low
        taken += jnp.where(p2, place, 0.0)
        source = keys_ref if g < 2 else values_ref
        columns = source[:, (g % 2) * PAIR_WIDTH : (g % 2 + 1) * PAIR_WIDTH]
        send_ref[:, g * PAIR_WIDTH : (g + 1) * PAIR_WIDTH] = low(dot(p1_low, columns))
        spare += dot(p2_low, columns)
    place_spare = jnp.sum(taken, axis=1, keepdims=True)
    send_ref[:, 4 * PAIR_WIDTH : 5 * PAIR_WIDTH] = low(spare)
    lane = iota((slots, HEAD_DIM), 1)
    send_ref[:, 5 * PAIR_WIDTH :] = low(
        jnp.where(lane == 0, place_main, jnp.where(lane == 1, place_spare, 0.0))
    )


def home_maps_kernel(dest_ref, p1t_ref, p2t_ref):
    rows, slots = p1t_ref.shape
    dest_col, same, down, across = ranks_of(dest_ref[...])
    rank_col = jnp.sum(jnp.where(same & (across < down), 1.0, 0.0), axis=1, keepdims=True)
    main_col, spare_col = places_of(dest_col, rank_col)
    slot_across = iota((rows, slots), 1)
    p1t_ref[...] = one_hot(slot_across == main_col)
    for g in range(KV_HEADS):
        p2t_ref[g] = one_hot(slot_across == spare_col + SPARE * g)


def landing_of(recv_ref):
    slots = recv_ref.shape[0]
    tile = recv_ref[:, 5 * PAIR_WIDTH :].astype(jnp.float32)
    lane = iota((slots, HEAD_DIM), 1)
    main_col = jnp.sum(jnp.where(lane == 0, tile, 0.0), axis=1, keepdims=True)
    spare_col = jnp.sum(jnp.where(lane == 1, tile, 0.0), axis=1, keepdims=True)
    return main_col, spare_col


def landing_rows(main_col, spare_col):
    slots = main_col.shape[0]
    diagonal = iota((slots, slots), 0) == iota((slots, slots), 1)
    return (
        jnp.sum(jnp.where(diagonal, main_col, 0.0), axis=0, keepdims=True).astype(jnp.int32),
        jnp.sum(jnp.where(diagonal, spare_col, 0.0), axis=0, keepdims=True).astype(jnp.int32),
    )


def landing_maps(rows, slots, main_row, spare_row):
    place_down = iota((rows, slots), 0) + 1
    part_across = (iota((rows, slots), 1) & (MAIN - 1)) >> 1
    r1t = one_hot(place_down == main_row)
    return r1t, [one_hot((place_down == spare_row) & (part_across == g)) for g in range(KV_HEADS)]


def receive_kernel(recv_ref, kv_ref):
    rows = kv_ref.shape[0]
    slots = recv_ref.shape[0]
    r1t, r2t = landing_maps(rows, slots, *landing_rows(*landing_of(recv_ref)))
    spare = recv_ref[:, 4 * PAIR_WIDTH : 5 * PAIR_WIDTH]
    for g in range(KV_HEADS):
        columns = slice(g * PAIR_WIDTH, (g + 1) * PAIR_WIDTH)
        kv_ref[:, columns] = low(dot(r1t, recv_ref[:, columns]) + dot(r2t[g], spare))


def landing_maps_kernel(recv_ref, r1_ref, r2_ref, r1t_ref, r2t_ref):
    slots, rows = r1_ref.shape
    main_col, spare_col = landing_of(recv_ref)
    r1t, r2t = landing_maps(rows, slots, *landing_rows(main_col, spare_col))
    r1t_ref[...] = r1t
    main_col = main_col.astype(jnp.int32)
    spare_col = spare_col.astype(jnp.int32)
    place_across = iota((slots, rows), 1) + 1
    part_down = (iota((slots, rows), 0) & (MAIN - 1)) >> 1
    r1_ref[...] = one_hot(place_across == main_col)
    for g in range(KV_HEADS):
        r2_ref[g] = one_hot((place_across == spare_col) & (part_down == g))
        r2t_ref[g] = r2t[g]


def pack_queries_kernel(query_ref, grad_ref, m1_ref, m2_ref, send_ref):
    m1 = m1_ref[...]
    spare = jnp.zeros((send_ref.shape[0], BOTH_WIDTH), jnp.float32)
    for g in range(KV_HEADS):
        columns = slice(g * GROUP_WIDTH, (g + 1) * GROUP_WIDTH)
        part = jnp.concatenate([query_ref[:, columns], grad_ref[:, columns]], axis=1)
        send_ref[:, g * BOTH_WIDTH : (g + 1) * BOTH_WIDTH] = low(dot(m1, part))
        spare += dot(m2_ref[g], part)
    send_ref[:, KV_HEADS * BOTH_WIDTH :] = low(spare)


def pack_kernel(source_ref, m1_ref, m2_ref, send_ref):
    width = source_ref.shape[1] // KV_HEADS
    m1 = m1_ref[...]
    spare = jnp.zeros((send_ref.shape[0], width), jnp.float32)
    for g in range(KV_HEADS):
        columns = slice(g * width, (g + 1) * width)
        part = low(source_ref[:, columns])
        send_ref[:, columns] = low(dot(m1, part))
        spare += dot(m2_ref[g], part)
    send_ref[:, KV_HEADS * width :] = low(spare)


def unpack_queries_kernel(recv_ref, m1_ref, m2_ref, attended_ref, grad_ref):
    m1 = m1_ref[...]
    spare = recv_ref[:, KV_HEADS * BOTH_WIDTH :]
    for g in range(KV_HEADS):
        part = recv_ref[:, g * BOTH_WIDTH : (g + 1) * BOTH_WIDTH]
        both = low(dot(m1, part) + dot(m2_ref[g], spare))
        columns = slice(g * GROUP_WIDTH, (g + 1) * GROUP_WIDTH)
        attended_ref[:, columns] = both[:, :GROUP_WIDTH]
        grad_ref[:, columns] = both[:, GROUP_WIDTH:]


def unpack_kv_kernel(recv_ref, m1_ref, m2_ref, key_ref, value_ref):
    m1 = m1_ref[...]
    spare = recv_ref[:, KV_HEADS * PAIR_WIDTH :]
    for g in range(KV_HEADS):
        both = low(
            dot(m1, recv_ref[:, g * PAIR_WIDTH : (g + 1) * PAIR_WIDTH]) + dot(m2_ref[g], spare)
        )
        key_ref[:, g * HEAD_DIM : (g + 1) * HEAD_DIM] = both[:, :HEAD_DIM]
        value_ref[:, g * HEAD_DIM : (g + 1) * HEAD_DIM] = both[:, HEAD_DIM:]


def ends_of(info_ref):
    ends = [info_ref[0]]
    for k in range(1, 6):
        ends.append(ends[-1] + info_ref[k])
    return ends


def stack_heads(x):
    return jnp.concatenate(
        [x[:, h * HEAD_DIM : (h + 1) * HEAD_DIM] for h in range(GROUP)], axis=0
    )


def unstack_heads(x):
    rows = x.shape[0] // GROUP
    return jnp.concatenate([x[h * rows : (h + 1) * rows] for h in range(GROUP)], axis=1)


def attention_kernel(
    info_ref, weight_ref, main_ref, spare_ref, key_ref, value_ref, r1t_ref, r2t_ref, r1_ref, r2_ref,
    kv_ref, send_ref, bias, spare_sum, value_ones, raised, dscore, score, dprob,
):
    step = pl.program_id(0)
    rows, keys = bias.shape
    count = len(score)
    e0, e1, e2, e3, e4, _ = ends_of(info_ref)
    place = info_ref[6] * rows + iota((rows, 1), 0)
    rejected = (place >= e1) & (place < e2)

    @pl.when(step == 0)
    def _():
        first = jnp.where(place >= e2, e2, 0)
        hidden_from = jnp.where(place >= e4, e3, jnp.where(rejected, e0, 0))
        hidden_to = jnp.where(place >= e4, e4, jnp.where(rejected, e1, 0))
        other = iota((rows, keys), 1)
        seen = (other >= first) & (other <= place) & ((other < hidden_from) | (other >= hidden_to))
        bias[...] = jnp.where(seen, 0.0, MASKED)
        spare_sum[...] = jnp.zeros_like(spare_sum)
        for n in range(count):
            value_ones[n][:, HEAD_DIM:] = jnp.ones((keys, HEAD_DIM), jnp.bfloat16)

    weight = jnp.where(place >= e2, weight_ref[1], weight_ref[0])
    factor = jnp.where(rejected | (place >= e4), -weight, weight)
    query, cotangent, key, inverse, attended, delta = ([None] * count for _ in range(6))
    for n in range(count):
        columns = slice(n * HEAD_DIM, (n + 1) * HEAD_DIM)
        both = dot(r1t_ref[...], main_ref[:, n * BOTH_WIDTH : (n + 1) * BOTH_WIDTH]) + dot(
            r2t_ref[n], spare_ref[...]
        )
        query[n] = stack_heads(low(both[:, :GROUP_WIDTH]))
        cotangent[n] = stack_heads(low(factor * both[:, GROUP_WIDTH:]))
        key[n] = key_ref[:, columns]
        value_ones[n][:, :HEAD_DIM] = value_ref[:, columns]
    for n in range(count):
        score[n][...] = dot(query[n], key[n], ((1,), (1,)))
    for n in range(count):
        for h in range(GROUP):
            part = slice(h * rows, (h + 1) * rows)
            seen = score[n][part, :] + bias[...]
            highest = jnp.max(seen, axis=1, keepdims=True)
            raised[n][part, :] = low(jnp.exp2((seen - highest) * EXPONENT))
    for n in range(count):
        dprob[n][...] = dot(cotangent[n], value_ones[n][:, :HEAD_DIM], ((1,), (1,)))
    for n in range(count):
        summed = dot(raised[n][...], value_ones[n][...])
        inverse[n] = 1.0 / summed[:, HEAD_DIM:]
        attended[n] = low(summed[:, :HEAD_DIM] * inverse[n])
        delta[n] = jnp.sum(
            cotangent[n].astype(jnp.float32) * attended[n].astype(jnp.float32),
            axis=1,
            keepdims=True,
        )
    for n in range(count):
        dscore[n][...] = raised[n][...] * low(dprob[n][...] - delta[n])
    for n in range(count):
        scaled = inverse[n] * SCALING
        query_grad = low(dot(dscore[n][...], key[n]) * scaled)
        query_low = low(query[n].astype(jnp.float32) * scaled)
        cotangent_low = low(cotangent[n].astype(jnp.float32) * inverse[n])
        first = n * PAIR_WIDTH
        kv_ref[:, first : first + HEAD_DIM] = low(dot(query_low.T, dscore[n][...])).T
        kv_ref[:, first + HEAD_DIM : first + PAIR_WIDTH] = low(dot(cotangent_low.T, raised[n][...])).T
        both = jnp.concatenate([unstack_heads(attended[n]), unstack_heads(query_grad)], axis=1)
        start = pl.multiple_of((step * count + n) * BOTH_WIDTH, BOTH_WIDTH)
        send_ref[:, pl.ds(start, BOTH_WIDTH)] = low(dot(r1_ref[...], both))
        spare_sum[...] += dot(r2_ref[n], both)

    @pl.when(step == KV_HEADS // count - 1)
    def _():
        send_ref[:, KV_HEADS * BOTH_WIDTH :] = low(spare_sum[...])


def shape(dims, kind=jnp.bfloat16):
    return jax.ShapeDtypeStruct(dims, kind)


def cost(flops, moved, exps=0):
    return pl.CostEstimate(flops=int(flops), bytes_accessed=int(moved), transcendentals=int(exps))


def body(queries, keys, values, out_grad, pair_weight, lengths, route_dest, route_slot):
    rows = queries.shape[0]
    ranks = lax.axis_size("dp")
    packs = lax.axis_size("pack")
    seq = rows * packs
    slots = ranks * MAIN
    wide = (KV_HEADS + 1) * BOTH_WIDTH
    narrow = (KV_HEADS + 1) * PAIR_WIDTH
    fence = lax.optimization_barrier

    def exchange(block):
        moved = lax.all_to_all(
            block.reshape(ranks, MAIN, block.shape[1]), "dp", split_axis=0, concat_axis=0, tiled=True
        )
        return moved.reshape(block.shape)

    down = (shape((slots, rows)), shape((KV_HEADS, slots, rows)))
    across = (shape((rows, slots)), shape((KV_HEADS, rows, slots)))
    dest = route_dest.reshape(1, rows)

    kv_send, p1, p2 = pl.pallas_call(
        send_kernel,
        out_shape=(shape((slots, narrow + HEAD_DIM)), *down),
        compiler_params=compiler_params(),
        cost_estimate=cost(4 * slots * rows * 2 * KV_WIDTH, 6 * slots * 2 * KV_WIDTH),
    )(dest, route_slot.reshape(1, rows), keys, values)

    kv_recv = exchange(kv_send)
    p1t, p2t = pl.pallas_call(
        home_maps_kernel,
        out_shape=across,
        compiler_params=compiler_params(),
        cost_estimate=cost(LONG, 6 * slots * rows),
    )(dest)
    query_send = pl.pallas_call(
        pack_queries_kernel,
        out_shape=shape((slots, wide)),
        compiler_params=compiler_params(),
        cost_estimate=cost(LONG, 10 * slots * QUERY_WIDTH),
    )(queries, out_grad, p1, p2)
    kv_recv, query_send, p1t, p2t = fence((kv_recv, query_send, p1t, p2t))

    kv_own = pl.pallas_call(
        receive_kernel,
        out_shape=shape((rows, 2 * KV_WIDTH)),
        compiler_params=compiler_params(SMALL_VMEM),
        cost_estimate=cost(4 * slots * rows * 2 * KV_WIDTH, 6 * slots * 2 * KV_WIDTH),
    )(kv_recv)
    kv_all = lax.all_gather(kv_own, "pack", axis=0, tiled=True)
    kv_recv, query_send, kv_own = fence((kv_recv, query_send, kv_own))
    r1, r2, r1t, r2t = pl.pallas_call(
        landing_maps_kernel,
        out_shape=(*down, *across),
        compiler_params=compiler_params(),
        cost_estimate=cost(LONG, 6 * slots * rows),
    )(kv_recv)
    query_recv = exchange(query_send)

    info = jnp.concatenate(
        [lengths.reshape(6), lax.axis_index("pack").astype(jnp.int32).reshape(1)]
    )
    smem = pl.BlockSpec(memory_space=pltpu.SMEM)
    at_once = 2
    steps = KV_HEADS // at_once
    work = HEADS * rows * seq * HEAD_DIM

    def several(dims, kind=jnp.bfloat16):
        return [pltpu.VMEM(dims, kind)] * at_once

    kv_part, back_send = pl.pallas_call(
        attention_kernel,
        grid=(steps,),
        in_specs=[
            smem,
            smem,
            pl.BlockSpec((slots, at_once * BOTH_WIDTH), lambda g: (0, g)),
            pl.BlockSpec((slots, BOTH_WIDTH), lambda g: (0, KV_HEADS)),
            pl.BlockSpec((seq, at_once * HEAD_DIM), lambda g: (0, g)),
            pl.BlockSpec((seq, at_once * HEAD_DIM), lambda g: (0, steps + g)),
            pl.BlockSpec((rows, slots), lambda g: (0, 0)),
            pl.BlockSpec((at_once, rows, slots), lambda g: (g, 0, 0)),
            pl.BlockSpec((slots, rows), lambda g: (0, 0)),
            pl.BlockSpec((at_once, slots, rows), lambda g: (g, 0, 0)),
        ],
        out_specs=(
            pl.BlockSpec((seq, at_once * PAIR_WIDTH), lambda g: (0, g)),
            pl.BlockSpec((slots, wide), lambda g: (0, 0)),
        ),
        out_shape=(shape((seq, 2 * KV_WIDTH)), shape((slots, wide))),
        scratch_shapes=[
            pltpu.VMEM((rows, seq), jnp.float32),
            pltpu.VMEM((slots, BOTH_WIDTH), jnp.float32),
            several((seq, PAIR_WIDTH)),
            several((GROUP * rows, seq)),
            several((GROUP * rows, seq)),
            several((GROUP * rows, seq), jnp.float32),
            several((GROUP * rows, seq), jnp.float32),
        ],
        compiler_params=compiler_params(dimension_semantics=("arbitrary",)),
        cost_estimate=cost(12 * work, 2 * HEADS * rows * seq, HEADS * rows * seq),
    )(
        info, pair_weight.reshape(2), query_recv, query_recv, kv_all, kv_all, r1t, r2t, r1, r2,
    )

    back_recv = exchange(back_send)
    kv_grad = lax.psum_scatter(kv_part, "pack", scatter_dimension=0, tiled=True)
    kv_grad_send = pl.pallas_call(
        pack_kernel,
        out_shape=shape((slots, narrow)),
        compiler_params=compiler_params(),
        cost_estimate=cost(4 * slots * rows * 2 * KV_WIDTH, 10 * slots * KV_WIDTH),
    )(kv_grad, r1, r2)
    back_recv, kv_grad_send = fence((back_recv, kv_grad_send))
    kv_back = exchange(kv_grad_send)
    attended, query_grad = pl.pallas_call(
        unpack_queries_kernel,
        out_shape=(shape((rows, QUERY_WIDTH)), shape((rows, QUERY_WIDTH))),
        compiler_params=compiler_params(),
        cost_estimate=cost(LONG, 10 * slots * QUERY_WIDTH),
    )(back_recv, p1t, p2t)
    key_grad, value_grad = pl.pallas_call(
        unpack_kv_kernel,
        out_shape=(shape((rows, KV_WIDTH)), shape((rows, KV_WIDTH))),
        compiler_params=compiler_params(SMALL_VMEM),
        cost_estimate=cost(4 * slots * rows * 2 * KV_WIDTH, 4 * slots * 2 * KV_WIDTH),
    )(kv_back, p1t, p2t)
    return attended, query_grad, key_grad, value_grad


def solution(mesh):
    rows = P(("dp", "pack"), None)
    flat = P(("dp", "pack"))
    return jax.shard_map(
        body,
        mesh=mesh,
        in_specs=(rows, rows, rows, rows, P("dp", None), P("dp", None, None), flat, flat),
        out_specs=(rows, rows, rows, rows),
        check_vma=False,
    )
```

time: 195 us -> 180 us (0.923)
  waiting for transfers between devices: 52.7 us -> 92.2 us
  blocking collectives: 27.8 us -> 0 us
  Pallas kernels: 55.8 us -> 42.5 us
  starting transfers between devices: 38.5 us -> 26.8 us
    all_to_all x5 -> x4, waiting for transfers between devices: 24.9 us -> 56.7 us  [exchange(): lax.all_to_all(block.reshape(ranks, MAIN, block.shape[1]), 'dp', split_ax...]
    all_to_all x1 -> x0, blocking collectives: 27.8 us -> none  [exchange(): lax.all_to_all(block.reshape(ranks, MAIN, block.shape[1]), 'dp', split_ax...]
    reduce_scatter x1, waiting for transfers between devices: 21.7 us -> 35.4 us  [body(): kv_grad = lax.psum_scatter(kv_part, 'pack', scatter_dimension=0, tiled=True)]
    pallas_call x8 -> x7, Pallas kernels: 50.8 us -> 38.8 us  [the longest x1 21.1 us: body(): pl.pallas_call(attention_kernel, grid=(steps,), in_specs=[smem, smem, pl....]
    all_to_all x5 -> x4, starting transfers between devices: 38.5 us -> 26.6 us  [exchange(): lax.all_to_all(block.reshape(ranks, MAIN, block.shape[1]), 'dp', split_ax...]
    all_gather x1, waiting for transfers between devices: 6.09 us -> 0.01 us  [body(): kv_all = lax.all_gather(kv_own, 'pack', axis=0, tiled=True)]
    unnamed x12 -> x10, local copies, waits for them, and re-layouts: 4.09 us -> 3.4 us
  transfers between devices with their start and end apart: 7 -> 6, of which waited for: 5 -> 5; matrix products, arithmetic and copies ran while one was open for 0% -> 0% of each run, Pallas kernels for 25% -> 9%
where the time goes in v1:
time: 180 us
  waiting for transfers between devices  92.2 us (51%)
  Pallas kernels  42.5 us (24%)
  starting transfers between devices  26.8 us (15%)
  between operations  14.1 us (8%)
  local copies, waits for them, and re-layouts  3.48 us (2%)
    all_to_all x4, waiting for transfers between devices, exchange(): lax.all_to_all(block.reshape(ranks, MAIN, block.shape[1]), 'dp', split_ax...  56.7 us
    reduce_scatter x1, waiting for transfers between devices, body(): kv_grad = lax.psum_scatter(kv_part, 'pack', scatter_dimension=0, tiled=True)  35.4 us
    all_to_all x4, starting transfers between devices, exchange(): lax.all_to_all(block.reshape(ranks, MAIN, block.shape[1]), 'dp', split_ax...  26.6 us
    pallas_call x1, Pallas kernels, body(): pl.pallas_call(attention_kernel, grid=(steps,), in_specs=[smem, smem, pl....  21.1 us
    pallas_call x1, Pallas kernels, body(): pl.pallas_call(pack_queries_kernel, out_shape=shape((slots, wide)), compi...  4.77 us
    pallas_call x1, Pallas kernels, body(): pl.pallas_call(unpack_queries_kernel, out_shape=(shape((rows, QUERY_WIDTH...  4.19 us
  transfers between devices with their start and end apart: 6, of which 5 were waited for; matrix products, arithmetic and copies ran while one was open for 0% of the time, Pallas kernels for 9%

profile of v1, /device:TPU:1, one launch (start us, length us, event | category | flops | bytes accessed | tf_op | source)
XLA Modules:
  0.0 179.8 jit_solution(14924713275741655483)
XLA Ops:
  7.2 2.6 %shard_map.111 = (bf16[256,1408]{1,0:T(8,128)(2,1)}, bf16[256,160]{1,0:T(8,128)(2,1)}, bf16[4,256,160]{2,1,0:T(8,128)(2,1)}) custom-call(s32[1,160]{1,0:T(1,128)} %bitcast.21, s32[1,160]{1,0:T(1,128)} %bitcast.20, bf16[160,512]{1,0:T(8,128)(2,1)} %keys_ref.1, bf16[160,512]{1,0:T(8,128)(2,1)} %values_ref.1), custom_call_target="tpu_custom_call" | custom-call | flops 167772160 | bytes 1572864 | tf_op jit(solution)/shard_map/pallas_call | solution.py:326
  9.8 8.6 %all-to-all-start = ((bf16[32,8,1408]{2,1,0:T(8,128)(2,1)}), bf16[32,8,1408]{2,1,0:T(8,128)(2,1)}, u32[]{:S(2)}, u32[]{:S(2)}) async-start(bf16[32,8,1408]{2,1,0:T(8,128)(2,1)} %bitcast.19), calls=%async_computation | async-start | bytes 1441792 | tf_op jit(solution)/shard_map/all_to_all | solution.py:317
  18.5 0.0 all-gather.2.cloned.1.call-start
  18.5 1.7 shard_map.113
  20.2 0.0 copy-start.4
  20.2 4.8 %shard_map.112 = bf16[256,6400]{1,0:T(8,128)(2,1)} custom-call(bf16[160,2560]{1,0:T(8,128)(2,1)} %query_ref.1, bf16[160,2560]{1,0:T(8,128)(2,1)} %grad_ref.1, bf16[256,160]{1,0:T(8,128)(2,1)} %get-tuple-element.28.m1_ref, bf16[4,256,160]{2,1,0:T(8,128)(2,1)} %get-tuple-element.29.m2_ref), custom_call_target="tpu_custom_call" | custom-call | flops 99999997952 | bytes 6553600 | tf_op jit(solution)/shard_map/pallas_call | solution.py:340
  25.0 0.0 copy-done.4
  25.0 0.1 reshape.47
  25.0 0.7 pad_add_fusion.info_ref
  25.7 6.4 %all-to-all-done = bf16[32,8,1408]{2,1,0:T(8,128)(2,1)} async-done(((bf16[32,8,1408]{2,1,0:T(8,128)(2,1)}), bf16[32,8,1408]{2,1,0:T(8,128)(2,1)}, u32[]{:S(2)}, u32[]{:S(2)}) %all-to-all-start) | async-done | bytes 720928 | tf_op jit(solution)/shard_map/all_to_all | solution.py:317
  32.1 2.3 %shard_map.114 = bf16[160,1024]{1,0:T(8,128)(2,1)} custom-call(bf16[256,1408]{1,0:T(8,128)(2,1)} %bitcast.5.recv_ref), custom_call_target="tpu_custom_call" | custom-call | flops 167772160 | bytes 1572864 | tf_op jit(solution)/shard_map/pallas_call | solution.py:348
  34.4 0.0 all-gather.2.cloned.1.call-update
  34.4 3.9 %all-to-all-start.1 = ((bf16[32,8,6400]{2,1,0:T(8,128)(2,1)}), bf16[32,8,6400]{2,1,0:T(8,128)(2,1)S(1)}, u32[]{:S(2)}, u32[]{:S(2)}) async-start(bf16[32,8,6400]{2,1,0:T(8,128)(2,1)} %bitcast.13), calls=%async_computation.1 | async-start | bytes 6553600 | tf_op jit(solution)/shard_map/all_to_all | solution.py:317
  38.3 0.2 reduce-scatter.2.cloned.1.call-start
  38.5 2.3 %shard_map.115 = (bf16[256,160]{1,0:T(8,128)(2,1)}, bf16[4,256,160]{2,1,0:T(8,128)(2,1)}, bf16[160,256]{1,0:T(8,128)(2,1)}, bf16[4,160,256]{2,1,0:T(8,128)(2,1)}) custom-call(bf16[256,1408]{1,0:T(8,128)(2,1)} %bitcast.5.recv_ref), custom_call_target="tpu_custom_call" | custom-call | flops 99999997952 | bytes 245760 | tf_op jit(solution)/shard_map/pallas_call | solution.py:356
  40.8 38.5 %all-to-all-done.1 = bf16[32,8,6400]{2,1,0:T(8,128)(2,1)S(1)} async-done(((bf16[32,8,6400]{2,1,0:T(8,128)(2,1)}), bf16[32,8,6400]{2,1,0:T(8,128)(2,1)S(1)}, u32[]{:S(2)}, u32[]{:S(2)}) %all-to-all-start.1) | async-done | bytes 3276832 | tf_op jit(solution)/shard_map/all_to_all | solution.py:317
  79.3 0.0 copy-start.2
  79.3 0.0 all-gather.2.cloned.1.call-done.key_ref.value_ref
  79.3 1.7 copy-done.2
  81.0 21.1 %shard_map.116 = (bf16[1280,1024]{1,0:T(8,128)(2,1)}, bf16[256,6400]{1,0:T(8,128)(2,1)}) custom-call(s32[7]{0:T(128)} %pad_add_fusion.info_ref, f32[2]{0:T(128)} %bitcast.23, bf16[256,6400]{1,0:T(8,128)(2,1)} %bitcast.14, bf16[256,6400]{1,0:T(8,128)(2,1)} %bitcast.15, bf16[1280,1024]{1,0:T(8,128)(2,1)} %all-gather.2.cloned.1.call-done.key_ref.value_ref, ...), custom_call_target="tpu_custom_call" | custom-call | flops 6291456000 | bytes 8192000 | tf_op jit(solution)/shard_map/pallas_call | solution.py:375
  102.1 0.0 reduce-scatter.2.cloned.1.call-update
  102.1 5.7 %all-to-all-start.2 = ((bf16[32,8,6400]{2,1,0:T(8,128)(2,1)}), bf16[32,8,6400]{2,1,0:T(8,128)(2,1)S(1)}, u32[]{:S(2)}, u32[]{:S(2)}) async-start(bf16[32,8,6400]{2,1,0:T(8,128)(2,1)} %bitcast.16), calls=%async_computation.2 | async-start | bytes 6553600 | tf_op jit(solution)/shard_map/all_to_all | solution.py:317
  107.8 35.4 %reduce-scatter.2.cloned.1.call-done.source_ref = bf16[160,1024]{1,0:T(8,128)(2,1)} async-done(((bf16[1280,1024]{1,0:T(8,128)(2,1)}), bf16[160,1024]{1,0:T(8,128)(2,1)}) %reduce-scatter.2.cloned.1.call-update) | async-done | bytes 327696 | tf_op jit(solution)/shard_map/reduce_scatter | solution.py:411
  143.2 2.5 %shard_map.117 = bf16[256,1280]{1,0:T(8,128)(2,1)} custom-call(bf16[160,1024]{1,0:T(8,128)(2,1)} %reduce-scatter.2.cloned.1.call-done.source_ref, bf16[256,160]{1,0:T(8,128)(2,1)} %get-tuple-element.38.r1_ref.m1_ref, bf16[4,256,160]{2,1,0:T(8,128)(2,1)} %get-tuple-element.39.r2_ref.m2_ref), custom_call_target="tpu_custom_call" | custom-call | flops 167772160 | bytes 1310720 | tf_op jit(solution)/shard_map/pallas_call | solution.py:412
  145.7 3.2 %all-to-all-done.2 = bf16[32,8,6400]{2,1,0:T(8,128)(2,1)S(1)} async-done(((bf16[32,8,6400]{2,1,0:T(8,128)(2,1)}), bf16[32,8,6400]{2,1,0:T(8,128)(2,1)S(1)}, u32[]{:S(2)}, u32[]{:S(2)}) %all-to-all-start.2) | async-done | bytes 3276832 | tf_op jit(solution)/shard_map/all_to_all | solution.py:317
  148.9 0.0 copy-start.3
  148.9 1.7 copy-done.3
  150.5 8.4 %all-to-all-start.3 = ((bf16[32,8,1280]{2,1,0:T(8,128)(2,1)}), bf16[32,8,1280]{2,1,0:T(8,128)(2,1)S(1)}, u32[]{:S(2)}, u32[]{:S(2)}) async-start(bf16[32,8,1280]{2,1,0:T(8,128)(2,1)} %bitcast.18), calls=%async_computation.4 | async-start | bytes 1310720 | tf_op jit(solution)/shard_map/all_to_all | solution.py:317
  158.9 0.0 copy-start
  158.9 0.0 copy-start.1
  159.0 4.2 %shard_map.118 = (bf16[160,2560]{1,0:T(8,128)(2,1)}, bf16[160,2560]{1,0:T(8,128)(2,1)}) custom-call(bf16[256,6400]{1,0:T(8,128)(2,1)} %bitcast.17, bf16[160,256]{1,0:T(8,128)(2,1)} %get-tuple-element.43.m1_ref, bf16[4,160,256]{2,1,0:T(8,128)(2,1)} %get-tuple-element.44.m2_ref), custom_call_target="tpu_custom_call" | custom-call | flops 99999997952 | bytes 6553600 | tf_op jit(solution)/shard_map/pallas_call | solution.py:420
  163.1 8.7 %all-to-all-done.3 = bf16[32,8,1280]{2,1,0:T(8,128)(2,1)S(1)} async-done(((bf16[32,8,1280]{2,1,0:T(8,128)(2,1)}), bf16[32,8,1280]{2,1,0:T(8,128)(2,1)S(1)}, u32[]{:S(2)}, u32[]{:S(2)}) %all-to-all-start.3) | async-done | bytes 655392 | tf_op jit(solution)/shard_map/all_to_all | solution.py:317
  171.9 0.0 copy-done
  171.9 0.0 copy-done.1
  171.9 1.1 shard_map.119
Async XLA Ops:
  9.8 22.3 %all-to-all-start = ((bf16[32,8,1408]{2,1,0:T(8,128)(2,1)}), bf16[32,8,1408]{2,1,0:T(8,128)(2,1)}, u32[]{:S(2)}, u32[]{:S(2)}) async-start(bf16[32,8,1408]{2,1,0:T(8,128)(2,1)} %bitcast.19), calls=%async_computation | async-start | bytes 1441792 | tf_op jit(solution)/shard_map/all_to_all | solution.py:317
  18.5 60.8 %all-gather.2.cloned.1.call-start = ((), (), s32[]{:S(2)}) async-start(), calls=%async_computation.5 | async-start | bytes 2949120 | tf_op jit(solution)/shard_map/all_gather | solution.py:354
  20.2 4.8 %copy-start.4 = (s32[1,2,3]{2,1,0:T(2,128)S(1)}, s32[1,2,3]{2,1,0:T(2,128)}, u32[]{:S(2)}) copy-start(s32[1,2,3]{2,1,0:T(2,128)} %param.13) | copy-start | bytes 76
  34.4 44.9 %all-to-all-start.1 = ((bf16[32,8,6400]{2,1,0:T(8,128)(2,1)}), bf16[32,8,6400]{2,1,0:T(8,128)(2,1)S(1)}, u32[]{:S(2)}, u32[]{:S(2)}) async-start(bf16[32,8,6400]{2,1,0:T(8,128)(2,1)} %bitcast.13), calls=%async_computation.1 | async-start | bytes 6553600 | tf_op jit(solution)/shard_map/all_to_all | solution.py:317
  38.3 105.0 %reduce-scatter.2.cloned.1.call-start = ((), (), s32[]{:S(2)}) async-start(), calls=%async_computation.6 | async-start | bytes 2949120 | tf_op jit(solution)/shard_map/reduce_scatter | solution.py:411
  79.3 1.7 copy-start.2
  102.1 46.8 %all-to-all-start.2 = ((bf16[32,8,6400]{2,1,0:T(8,128)(2,1)}), bf16[32,8,6400]{2,1,0:T(8,128)(2,1)S(1)}, u32[]{:S(2)}, u32[]{:S(2)}) async-start(bf16[32,8,6400]{2,1,0:T(8,128)(2,1)} %bitcast.16), calls=%async_computation.2 | async-start | bytes 6553600 | tf_op jit(solution)/shard_map/all_to_all | solution.py:317
  148.9 1.7 copy-start.3
  150.5 21.3 %all-to-all-start.3 = ((bf16[32,8,1280]{2,1,0:T(8,128)(2,1)}), bf16[32,8,1280]{2,1,0:T(8,128)(2,1)S(1)}, u32[]{:S(2)}, u32[]{:S(2)}) async-start(bf16[32,8,1280]{2,1,0:T(8,128)(2,1)} %bitcast.18), calls=%async_computation.4 | async-start | bytes 1310720 | tf_op jit(solution)/shard_map/all_to_all | solution.py:317
  158.9 12.9 %copy-start = (bf16[4,160,256]{2,1,0:T(8,128)(2,1)S(1)}, bf16[4,160,256]{2,1,0:T(8,128)(2,1)}, u32[]{:S(2)}) copy-start(bf16[4,160,256]{2,1,0:T(8,128)(2,1)} %get-tuple-element.44.m2_ref) | copy-start | bytes 983044
  158.9 12.9 %copy-start.1 = (bf16[160,256]{1,0:T(8,128)(2,1)S(1)}, bf16[160,256]{1,0:T(8,128)(2,1)}, u32[]{:S(2)}) copy-start(bf16[160,256]{1,0:T(8,128)(2,1)} %get-tuple-element.43.m1_ref) | copy-start | bytes 245764
Sparse Core Ops, SparseCore 0:
  34.5 38.3 all-gather.1
  102.2 40.9 reduce-scatter.1

commit v2 on v1

--- a/solution.py
+++ b/solution.py
@@ -26,6 +26,7 @@
 VMEM_LIMIT = 60 * 1024 * 1024
 SMALL_VMEM = 16 * 1024 * 1024
 BOTH_WIDTH = 2 * GROUP_WIDTH
+PIECES = ((0, 1, 2), (3,))
 LONG = 10**11
 
 
@@ -65,17 +66,20 @@
     return jnp.where(rank < MAIN, first, -MAIN), jnp.where(rank < MAIN, -MAIN, first - MAIN)
 
 
-def send_kernel(dest_ref, slot_ref, keys_ref, values_ref, send_ref, p1_ref, p2_ref):
-    rows = keys_ref.shape[0]
-    slots = send_ref.shape[0]
+def home_places(dest_ref):
     dest_row = dest_ref[...]
     _, same, down, across = ranks_of(dest_row)
     rank_row = jnp.sum(jnp.where(same & (down < across), 1.0, 0.0), axis=0, keepdims=True)
-    main_row, spare_row = places_of(dest_row, rank_row)
+    return places_of(dest_row, rank_row)
+
+
+def send_kernel(dest_ref, slot_ref, keys_ref, values_ref, send_ref):
+    rows = keys_ref.shape[0]
+    slots = send_ref.shape[0]
+    main_row, spare_row = home_places(dest_ref)
     slot_down = iota((slots, rows), 0)
     p1 = slot_down == main_row
     p1_low = one_hot(p1)
-    p1_ref[...] = p1_low
     place = (slot_ref[...] + 1).astype(jnp.float32)
     place_main = jnp.sum(jnp.where(p1, place, 0.0), axis=1, keepdims=True)
     taken = jnp.zeros((slots, rows), jnp.float32)
@@ -83,7 +87,6 @@
     for g in range(KV_HEADS):
         p2 = slot_down == spare_row + SPARE * g
         p2_low = one_hot(p2)
-        p2_ref[g] = p2_low
         taken += jnp.where(p2, place, 0.0)
         source = keys_ref if g < 2 else values_ref
         columns = source[:, (g % 2) * PAIR_WIDTH : (g % 2 + 1) * PAIR_WIDTH]
@@ -158,15 +161,39 @@
         r2t_ref[g] = r2t[g]
 
 
-def pack_queries_kernel(query_ref, grad_ref, m1_ref, m2_ref, send_ref):
-    m1 = m1_ref[...]
-    spare = jnp.zeros((send_ref.shape[0], BOTH_WIDTH), jnp.float32)
-    for g in range(KV_HEADS):
-        columns = slice(g * GROUP_WIDTH, (g + 1) * GROUP_WIDTH)
-        part = jnp.concatenate([query_ref[:, columns], grad_ref[:, columns]], axis=1)
-        send_ref[:, g * BOTH_WIDTH : (g + 1) * BOTH_WIDTH] = low(dot(m1, part))
-        spare += dot(m2_ref[g], part)
-    send_ref[:, KV_HEADS * BOTH_WIDTH :] = low(spare)
+def spread(tiles):
+    part = -(-tiles // KV_HEADS)
+    return part, [(c * part, min((c + 1) * part, tiles)) for c in range(KV_HEADS)]
+
+
+def pack_queries_kernel(dest_ref, query_ref, grad_ref, *send_refs):
+    rows = query_ref.shape[0]
+    slots = send_refs[0].shape[0]
+    main_row, spare_row = home_places(dest_ref)
+    slot_down = iota((slots, rows), 0)
+    m1 = one_hot(slot_down == main_row)
+    m2 = [one_hot(slot_down == spare_row + SPARE * c) for c in range(KV_HEADS)]
+    for send_ref, heads in zip(send_refs, PIECES):
+        parts = []
+        for n, g in enumerate(heads):
+            columns = slice(g * GROUP_WIDTH, (g + 1) * GROUP_WIDTH)
+            parts.append(jnp.concatenate([query_ref[:, columns], grad_ref[:, columns]], axis=1))
+            send_ref[:, n * BOTH_WIDTH : (n + 1) * BOTH_WIDTH] = low(dot(m1, parts[-1]))
+        whole = jnp.concatenate(parts, axis=1)
+        main = whole.shape[1]
+        part, ranges = spread(main // HEAD_DIM)
+        shortest = ranges[-1][1] - ranges[-1][0]
+        total = sum(
+            dot(m2[c], whole[:, lo * HEAD_DIM : (lo + shortest) * HEAD_DIM])
+            for c, (lo, _) in enumerate(ranges)
+        )
+        send_ref[:, main : main + shortest * HEAD_DIM] = low(total)
+        if shortest < part:
+            total = sum(
+                dot(m2[c], whole[:, (lo + shortest) * HEAD_DIM : hi * HEAD_DIM])
+                for c, (lo, hi) in enumerate(ranges[:-1])
+            )
+            send_ref[:, main + shortest * HEAD_DIM :] = low(total)
 
 
 def pack_kernel(source_ref, m1_ref, m2_ref, send_ref):
@@ -221,51 +248,53 @@
     return jnp.concatenate([x[h * rows : (h + 1) * rows] for h in range(GROUP)], axis=1)
 
 
-def attention_kernel(
-    info_ref, weight_ref, main_ref, spare_ref, key_ref, value_ref, r1t_ref, r2t_ref, r1_ref, r2_ref,
-    kv_ref, send_ref, bias, spare_sum, value_ones, raised, dscore, score, dprob,
+def attend(
+    info_ref, weight_ref, recv_ref, keys, values, r1t_ref, r2t_ref, r1_ref,
+    bias, value_ones, raised, dscore, score, put_kv, put_back,
 ):
-    step = pl.program_id(0)
-    rows, keys = bias.shape
+    rows, length = bias.shape
     count = len(score)
     e0, e1, e2, e3, e4, _ = ends_of(info_ref)
     place = info_ref[6] * rows + iota((rows, 1), 0)
     rejected = (place >= e1) & (place < e2)
-
-    @pl.when(step == 0)
-    def _():
-        first = jnp.where(place >= e2, e2, 0)
-        hidden_from = jnp.where(place >= e4, e3, jnp.where(rejected, e0, 0))
-        hidden_to = jnp.where(place >= e4, e4, jnp.where(rejected, e1, 0))
-        other = iota((rows, keys), 1)
-        seen = (other >= first) & (other <= place) & ((other < hidden_from) | (other >= hidden_to))
-        bias[...] = jnp.where(seen, 0.0, MASKED)
-        spare_sum[...] = jnp.zeros_like(spare_sum)
-        for n in range(count):
-            value_ones[n][:, HEAD_DIM:] = jnp.ones((keys, HEAD_DIM), jnp.bfloat16)
-
+    first = jnp.where(place >= e2, e2, 0)
+    hidden_from = jnp.where(place >= e4, e3, jnp.where(rejected, e0, 0))
+    hidden_to = jnp.where(place >= e4, e4, jnp.where(rejected, e1, 0))
+    other = iota((rows, length), 1)
+    seen = (other >= first) & (other <= place) & ((other < hidden_from) | (other >= hidden_to))
+    bias[...] = jnp.where(seen, 0.0, MASKED)
     weight = jnp.where(place >= e2, weight_ref[1], weight_ref[0])
     factor = jnp.where(rejected | (place >= e4), -weight, weight)
-    query, cotangent, key, inverse, attended, delta = ([None] * count for _ in range(6))
-    for n in range(count):
-        columns = slice(n * HEAD_DIM, (n + 1) * HEAD_DIM)
-        both = dot(r1t_ref[...], main_ref[:, n * BOTH_WIDTH : (n + 1) * BOTH_WIDTH]) + dot(
-            r2t_ref[n], spare_ref[...]
+
+    main = count * BOTH_WIDTH
+    _, ranges = spread(main // HEAD_DIM)
+    r1t = r1t_ref[...]
+    query, cotangent, inverse, attended, delta = ([None] * count for _ in range(5))
+    for n in range(count):
+        value_ones[n][:, HEAD_DIM:] = jnp.ones((length, HEAD_DIM), jnp.bfloat16)
+        value_ones[n][:, :HEAD_DIM] = values[n]()
+        tiles = BOTH_WIDTH // HEAD_DIM
+        spare = []
+        for c, (lo, hi) in enumerate(ranges):
+            start, stop = max(lo, n * tiles), min(hi, (n + 1) * tiles)
+            if start < stop:
+                columns = slice(main + (start - lo) * HEAD_DIM, main + (stop - lo) * HEAD_DIM)
+                spare.append(dot(r2t_ref[c], recv_ref[:, columns]))
+        both = dot(r1t, recv_ref[:, n * BOTH_WIDTH : (n + 1) * BOTH_WIDTH]) + jnp.concatenate(
+            spare, axis=1
         )
         query[n] = stack_heads(low(both[:, :GROUP_WIDTH]))
         cotangent[n] = stack_heads(low(factor * both[:, GROUP_WIDTH:]))
-        key[n] = key_ref[:, columns]
-        value_ones[n][:, :HEAD_DIM] = value_ref[:, columns]
-    for n in range(count):
-        score[n][...] = dot(query[n], key[n], ((1,), (1,)))
+    for n in range(count):
+        score[n][...] = dot(query[n], keys[n](), ((1,), (1,)))
     for n in range(count):
         for h in range(GROUP):
             part = slice(h * rows, (h + 1) * rows)
-            seen = score[n][part, :] + bias[...]
-            highest = jnp.max(seen, axis=1, keepdims=True)
-            raised[n][part, :] = low(jnp.exp2((seen - highest) * EXPONENT))
-    for n in range(count):
-        dprob[n][...] = dot(cotangent[n], value_ones[n][:, :HEAD_DIM], ((1,), (1,)))
+            masked = score[n][part, :] + bias[...]
+            highest = jnp.max(masked, axis=1, keepdims=True)
+            raised[n][part, :] = low(jnp.exp2((masked - highest) * EXPONENT))
+    for n in range(count):
+        score[n][...] = dot(cotangent[n], value_ones[n][:, :HEAD_DIM], ((1,), (1,)))
     for n in range(count):
         summed = dot(raised[n][...], value_ones[n][...])
         inverse[n] = 1.0 / summed[:, HEAD_DIM:]
@@ -276,23 +305,89 @@
             keepdims=True,
         )
     for n in range(count):
-        dscore[n][...] = raised[n][...] * low(dprob[n][...] - delta[n])
+        dscore[n][...] = raised[n][...] * low(score[n][...] - delta[n])
     for n in range(count):
         scaled = inverse[n] * SCALING
-        query_grad = low(dot(dscore[n][...], key[n]) * scaled)
         query_low = low(query[n].astype(jnp.float32) * scaled)
         cotangent_low = low(cotangent[n].astype(jnp.float32) * inverse[n])
-        first = n * PAIR_WIDTH
-        kv_ref[:, first : first + HEAD_DIM] = low(dot(query_low.T, dscore[n][...])).T
-        kv_ref[:, first + HEAD_DIM : first + PAIR_WIDTH] = low(dot(cotangent_low.T, raised[n][...])).T
+        put_kv(
+            n,
+            low(dot(query_low.T, dscore[n][...])).T,
+            low(dot(cotangent_low.T, raised[n][...])).T,
+        )
+        query_grad = low(dot(dscore[n][...], keys[n]()) * scaled)
         both = jnp.concatenate([unstack_heads(attended[n]), unstack_heads(query_grad)], axis=1)
-        start = pl.multiple_of((step * count + n) * BOTH_WIDTH, BOTH_WIDTH)
-        send_ref[:, pl.ds(start, BOTH_WIDTH)] = low(dot(r1_ref[...], both))
-        spare_sum[...] += dot(r2_ref[n], both)
-
-    @pl.when(step == KV_HEADS // count - 1)
-    def _():
-        send_ref[:, KV_HEADS * BOTH_WIDTH :] = low(spare_sum[...])
+        put_back(n, low(dot(r1_ref[...], both)), both)
+
+
+def first_kernel(
+    info_ref, weight_ref, recv_ref, kv_all_ref, r1t_ref, r2t_ref, r1_ref, r2_ref,
+    kv_ref, send_ref, spare_ref,
+    bias, value_ones, raised, dscore, score, kv_own, send_own, copied,
+):
+    count = len(score)
+    spare = []
+    copies = []
+
+    def copy(source, target):
+        copies.append(pltpu.make_async_copy(source, target, copied.at[len(copies)]))
+        copies[-1].start()
+
+    def key(n):
+        return lambda: kv_all_ref[:, n * HEAD_DIM : (n + 1) * HEAD_DIM]
+
+    def value(n):
+        return lambda: kv_all_ref[:, KV_WIDTH + n * HEAD_DIM : KV_WIDTH + (n + 1) * HEAD_DIM]
+
+    def put_kv(n, key_part, value_part):
+        kv_own[n][:, :HEAD_DIM] = key_part
+        kv_own[n][:, HEAD_DIM:] = value_part
+        copy(kv_own[n], kv_ref.at[:, n * PAIR_WIDTH : (n + 1) * PAIR_WIDTH])
+
+    def put_back(n, main, both):
+        send_own[n][...] = main
+        copy(send_own[n], send_ref.at[:, n * BOTH_WIDTH : (n + 1) * BOTH_WIDTH])
+        spare.append(dot(r2_ref[n], both))
+
+    attend(
+        info_ref, weight_ref, recv_ref, [key(n) for n in range(count)],
+        [value(n) for n in range(count)], r1t_ref, r2t_ref, r1_ref,
+        bias, value_ones, raised, dscore, score, put_kv, put_back,
+    )
+    spare_ref[...] = low(sum(spare))
+    for started in copies:
+        started.wait()
+
+
+def last_kernel(
+    info_ref, weight_ref, recv_ref, key_ref, value_ref, r1t_ref, r2t_ref, r1_ref, r2_ref,
+    spare_ref, _kv, _send, kv_ref, send_ref,
+    bias, value_ones, raised, dscore, score, kv_own, send_own, copied,
+):
+    group = KV_HEADS - 1
+    copies = []
+
+    def copy(source, target):
+        copies.append(pltpu.make_async_copy(source, target, copied.at[len(copies)]))
+        copies[-1].start()
+
+    def put_kv(n, key_part, value_part):
+        kv_own[:, :HEAD_DIM] = key_part
+        kv_own[:, HEAD_DIM:] = value_part
+        copy(kv_own, kv_ref.at[:, group * PAIR_WIDTH : (group + 1) * PAIR_WIDTH])
+
+    def put_back(n, main, both):
+        send_own[:, :BOTH_WIDTH] = main
+        send_own[:, BOTH_WIDTH:] = low(dot(r2_ref[0], both)) + spare_ref[...]
+        copy(send_own, send_ref.at[:, group * BOTH_WIDTH :])
+
+    attend(
+        info_ref, weight_ref, recv_ref, [lambda: key_ref[...]], [lambda: value_ref[...]],
+        r1t_ref, r2t_ref, r1_ref,
+        bias, value_ones, raised, dscore, score, put_kv, put_back,
+    )
+    for started in copies:
+        started.wait()
 
 
 def shape(dims, kind=jnp.bfloat16):
@@ -323,9 +418,9 @@
     across = (shape((rows, slots)), shape((KV_HEADS, rows, slots)))
     dest = route_dest.reshape(1, rows)
 
-    kv_send, p1, p2 = pl.pallas_call(
+    kv_send = pl.pallas_call(
         send_kernel,
-        out_shape=(shape((slots, narrow + HEAD_DIM)), *down),
+        out_shape=shape((slots, narrow + HEAD_DIM)),
         compiler_params=compiler_params(),
         cost_estimate=cost(4 * slots * rows * 2 * KV_WIDTH, 6 * slots * 2 * KV_WIDTH),
     )(dest, route_slot.reshape(1, rows), keys, values)
@@ -337,13 +432,18 @@
         compiler_params=compiler_params(),
         cost_estimate=cost(LONG, 6 * slots * rows),
     )(dest)
-    query_send = pl.pallas_call(
+
+    def block_width(heads):
+        tiles = len(heads) * BOTH_WIDTH // HEAD_DIM
+        return (tiles + spread(tiles)[0]) * HEAD_DIM
+
+    first_send, last_send = pl.pallas_call(
         pack_queries_kernel,
-        out_shape=shape((slots, wide)),
+        out_shape=tuple(shape((slots, block_width(heads))) for heads in PIECES),
         compiler_params=compiler_params(),
         cost_estimate=cost(LONG, 10 * slots * QUERY_WIDTH),
-    )(queries, out_grad, p1, p2)
-    kv_recv, query_send, p1t, p2t = fence((kv_recv, query_send, p1t, p2t))
+    )(dest, queries, out_grad)
+    kv_recv, first_send, last_send, p1t, p2t = fence((kv_recv, first_send, last_send, p1t, p2t))
 
     kv_own = pl.pallas_call(
         receive_kernel,
@@ -352,59 +452,90 @@
         cost_estimate=cost(4 * slots * rows * 2 * KV_WIDTH, 6 * slots * 2 * KV_WIDTH),
     )(kv_recv)
     kv_all = lax.all_gather(kv_own, "pack", axis=0, tiled=True)
-    kv_recv, query_send, kv_own = fence((kv_recv, query_send, kv_own))
+    kv_recv, first_send, last_send, kv_own = fence((kv_recv, first_send, last_send, kv_own))
     r1, r2, r1t, r2t = pl.pallas_call(
         landing_maps_kernel,
         out_shape=(*down, *across),
         compiler_params=compiler_params(),
         cost_estimate=cost(LONG, 6 * slots * rows),
     )(kv_recv)
-    query_recv = exchange(query_send)
+    first_recv = exchange(first_send)
+    first_recv, last_send, r1, r2, r1t, r2t = fence((first_recv, last_send, r1, r2, r1t, r2t))
+    last_recv = exchange(last_send)
 
     info = jnp.concatenate(
         [lengths.reshape(6), lax.axis_index("pack").astype(jnp.int32).reshape(1)]
     )
+    weight = pair_weight.reshape(2)
     smem = pl.BlockSpec(memory_space=pltpu.SMEM)
-    at_once = 2
-    steps = KV_HEADS // at_once
-    work = HEADS * rows * seq * HEAD_DIM
-
-    def several(dims, kind=jnp.bfloat16):
-        return [pltpu.VMEM(dims, kind)] * at_once
-
+    vmem = pl.BlockSpec(memory_space=pltpu.VMEM)
+    anywhere = pl.BlockSpec(memory_space=pl.ANY)
+    work = GROUP * rows * seq * HEAD_DIM
+    group_rows = GROUP * rows
+
+    def scratch(count):
+        return [
+            pltpu.VMEM((rows, seq), jnp.float32),
+            [pltpu.VMEM((seq, PAIR_WIDTH), jnp.bfloat16)] * count,
+            [pltpu.VMEM((group_rows, seq), jnp.bfloat16)] * count,
+            [pltpu.VMEM((group_rows, seq), jnp.bfloat16)] * count,
+            [pltpu.VMEM((group_rows, seq), jnp.float32)] * count,
+        ]
+
+    count = len(PIECES[0])
+    kv_first, back_first, back_spare = pl.pallas_call(
+        first_kernel,
+        in_specs=[smem, smem, vmem, vmem, vmem, vmem, vmem, vmem],
+        out_specs=(anywhere, anywhere, vmem),
+        out_shape=(
+            shape((seq, 2 * KV_WIDTH)),
+            shape((slots, wide)),
+            shape((slots, BOTH_WIDTH)),
+        ),
+        scratch_shapes=[
+            *scratch(count),
+            [pltpu.VMEM((seq, PAIR_WIDTH), jnp.bfloat16)] * count,
+            [pltpu.VMEM((slots, BOTH_WIDTH), jnp.bfloat16)] * count,
+            pltpu.SemaphoreType.DMA((2 * count,)),
+        ],
+        compiler_params=compiler_params(),
+        cost_estimate=cost(LONG, 2 * HEADS * rows * seq, HEADS * rows * seq),
+    )(info, weight, first_recv, kv_all, r1t, r2t, r1, r2)
+
+    def whole(dims):
+        return pl.BlockSpec(dims, lambda i: (0,) * len(dims))
+
+    group = KV_HEADS - 1
     kv_part, back_send = pl.pallas_call(
-        attention_kernel,
-        grid=(steps,),
+        last_kernel,
+        grid=(1,),
         in_specs=[
             smem,
             smem,
-            pl.BlockSpec((slots, at_once * BOTH_WIDTH), lambda g: (0, g)),
-            pl.BlockSpec((slots, BOTH_WIDTH), lambda g: (0, KV_HEADS)),
-            pl.BlockSpec((seq, at_once * HEAD_DIM), lambda g: (0, g)),
-            pl.BlockSpec((seq, at_once * HEAD_DIM), lambda g: (0, steps + g)),
-            pl.BlockSpec((rows, slots), lambda g: (0, 0)),
-            pl.BlockSpec((at_once, rows, slots), lambda g: (g, 0, 0)),
-            pl.BlockSpec((slots, rows), lambda g: (0, 0)),
-            pl.BlockSpec((at_once, slots, rows), lambda g: (g, 0, 0)),
+            whole(last_recv.shape),
+            pl.BlockSpec((seq, HEAD_DIM), lambda i: (0, group)),
+            pl.BlockSpec((seq, HEAD_DIM), lambda i: (0, KV_HEADS + group)),
+            whole(r1t.shape),
+            whole(r2t.shape),
+            whole(r1.shape),
+            pl.BlockSpec((1, slots, rows), lambda i: (group, 0, 0)),
+            whole(back_spare.shape),
+            anywhere,
+            anywhere,
         ],
-        out_specs=(
-            pl.BlockSpec((seq, at_once * PAIR_WIDTH), lambda g: (0, g)),
-            pl.BlockSpec((slots, wide), lambda g: (0, 0)),
-        ),
+        out_specs=(anywhere, anywhere),
         out_shape=(shape((seq, 2 * KV_WIDTH)), shape((slots, wide))),
+        input_output_aliases={10: 0, 11: 1},
         scratch_shapes=[
-            pltpu.VMEM((rows, seq), jnp.float32),
-            pltpu.VMEM((slots, BOTH_WIDTH), jnp.float32),
-            several((seq, PAIR_WIDTH)),
-            several((GROUP * rows, seq)),
-            several((GROUP * rows, seq)),
-            several((GROUP * rows, seq), jnp.float32),
-            several((GROUP * rows, seq), jnp.float32),
+            *scratch(1),
+            pltpu.VMEM((seq, PAIR_WIDTH), jnp.bfloat16),
+            pltpu.VMEM((slots, 2 * BOTH_WIDTH), jnp.bfloat16),
+            pltpu.SemaphoreType.DMA((2,)),
         ],
         compiler_params=compiler_params(dimension_semantics=("arbitrary",)),
-        cost_estimate=cost(12 * work, 2 * HEADS * rows * seq, HEADS * rows * seq),
+        cost_estimate=cost(12 * work, 2 * GROUP * rows * seq, GROUP * rows * seq),
     )(
-        info, pair_weight.reshape(2), query_recv, query_recv, kv_all, kv_all, r1t, r2t, r1, r2,
+        info, weight, last_recv, kv_all, kv_all, r1t, r2t, r1, r2, back_spare, kv_first, back_first,
     )
 
     back_recv = exchange(back_send)
@@ -420,7 +551,7 @@
     attended, query_grad = pl.pallas_call(
         unpack_queries_kernel,
         out_shape=(shape((rows, QUERY_WIDTH)), shape((rows, QUERY_WIDTH))),
-        compiler_params=compiler_params(),
+        compiler_params=compiler_params(SMALL_VMEM),
         cost_estimate=cost(LONG, 10 * slots * QUERY_WIDTH),
     )(back_recv, p1t, p2t)
     key_grad, value_grad = pl.pallas_call(

time: 180 us -> 184 us (1.022)
  waiting for transfers between devices: 92.2 us -> 85.4 us
  starting transfers between devices: 26.8 us -> 33 us
  Pallas kernels: 42.5 us -> 47.4 us
    all_to_all x4 -> x5, waiting for transfers between devices: 56.7 us -> 50.1 us  [exchange(): lax.all_to_all(block.reshape(ranks, MAIN, block.shape[1]), 'dp', split_ax...]
    all_to_all x4 -> x5, starting transfers between devices: 26.6 us -> 32.7 us  [exchange(): lax.all_to_all(block.reshape(ranks, MAIN, block.shape[1]), 'dp', split_ax...]
    pallas_call x3 -> x4, Pallas kernels: 28.5 us -> 34.4 us  [the longest x1 19.1 us: body(): pl.pallas_call(first_kernel, in_specs=[smem, smem, vmem, vmem, vmem, vmem...]
    pallas_call x1, Pallas kernels: 4.19 us -> 2.14 us  [body(): pl.pallas_call(unpack_queries_kernel, out_shape=(shape((rows, QUERY_WIDTH...]
  transfers between devices with their start and end apart: 6 -> 7, of which waited for: 5 -> 5; matrix products, arithmetic and copies ran while one was open for 0% -> 0% of each run, Pallas kernels for 9% -> 18%
where the time goes in v2:
time: 184 us
  waiting for transfers between devices  85.4 us (46%)
  Pallas kernels  47.4 us (26%)
  starting transfers between devices  33 us (18%)
  between operations  14.2 us (8%)
  local copies, waits for them, and re-layouts  2.98 us (2%)
    all_to_all x5, waiting for transfers between devices, exchange(): lax.all_to_all(block.reshape(ranks, MAIN, block.shape[1]), 'dp', split_ax...  50.1 us
    reduce_scatter x1, waiting for transfers between devices, body(): kv_grad = lax.psum_scatter(kv_part, 'pack', scatter_dimension=0, tiled=True)  35.2 us
    all_to_all x5, starting transfers between devices, exchange(): lax.all_to_all(block.reshape(ranks, MAIN, block.shape[1]), 'dp', split_ax...  32.7 us
    pallas_call x1, Pallas kernels, body(): pl.pallas_call(first_kernel, in_specs=[smem, smem, vmem, vmem, vmem, vmem...  19.1 us
    pallas_call x1, Pallas kernels, body(): pl.pallas_call(last_kernel, grid=(1,), in_specs=[smem, smem, whole(last_r...  8.14 us
    pallas_call x1, Pallas kernels, body(): pl.pallas_call(pack_queries_kernel, out_shape=tuple((shape((slots, block_...  4.46 us
  transfers between devices with their start and end apart: 7, of which 5 were waited for; matrix products, arithmetic and copies ran while one was open for 0% of the time, Pallas kernels for 18%

profile of v2, /device:TPU:1, one launch (start us, length us, event | category | flops | bytes accessed | tf_op | source)
XLA Modules:
  0.0 183.5 jit_solution(13842254478387088264)
XLA Ops:
  7.2 2.6 %shard_map.111 = bf16[256,1408]{1,0:T(8,128)(2,1)} custom-call(s32[1,160]{1,0:T(1,128)} %bitcast.23, s32[1,160]{1,0:T(1,128)} %bitcast.22, bf16[160,512]{1,0:T(8,128)(2,1)} %keys_ref.1, bf16[160,512]{1,0:T(8,128)(2,1)} %values_ref.1), custom_call_target="tpu_custom_call" | custom-call | flops 167772160 | bytes 1572864 | tf_op jit(solution)/shard_map/pallas_call | solution.py:421
  9.8 8.6 %all-to-all-start = ((bf16[32,8,1408]{2,1,0:T(8,128)(2,1)}), bf16[32,8,1408]{2,1,0:T(8,128)(2,1)}, u32[]{:S(2)}, u32[]{:S(2)}) async-start(bf16[32,8,1408]{2,1,0:T(8,128)(2,1)} %bitcast.17), calls=%async_computation | async-start | bytes 1441792 | tf_op jit(solution)/shard_map/all_to_all | solution.py:412
  18.4 0.0 all-gather.2.cloned.1.call-start
  18.5 1.7 shard_map.113
  20.2 0.0 copy-start.5
  20.2 4.5 %shard_map.112 = (bf16[256,4864]{1,0:T(8,128)(2,1)}, bf16[256,1664]{1,0:T(8,128)(2,1)}) custom-call(s32[1,160]{1,0:T(1,128)} %bitcast.25, bf16[160,2560]{1,0:T(8,128)(2,1)} %query_ref.1, bf16[160,2560]{1,0:T(8,128)(2,1)} %grad_ref.1), custom_call_target="tpu_custom_call" | custom-call | flops 99999997952 | bytes 6553600 | tf_op jit(solution)/shard_map/pallas_call | solution.py:440
  24.7 0.0 copy-done.5
  24.7 0.1 reshape.53
  24.8 0.6 pad_add_fusion.info_ref
  25.3 6.7 %all-to-all-done = bf16[32,8,1408]{2,1,0:T(8,128)(2,1)} async-done(((bf16[32,8,1408]{2,1,0:T(8,128)(2,1)}), bf16[32,8,1408]{2,1,0:T(8,128)(2,1)}, u32[]{:S(2)}, u32[]{:S(2)}) %all-to-all-start) | async-done | bytes 720928 | tf_op jit(solution)/shard_map/all_to_all | solution.py:412
  32.1 2.3 %shard_map.114 = bf16[160,1024]{1,0:T(8,128)(2,1)} custom-call(bf16[256,1408]{1,0:T(8,128)(2,1)} %bitcast.5.recv_ref), custom_call_target="tpu_custom_call" | custom-call | flops 167772160 | bytes 1572864 | tf_op jit(solution)/shard_map/pallas_call | solution.py:448
  34.3 0.0 all-gather.2.cloned.1.call-update
  34.4 3.9 %all-to-all-start.1 = ((bf16[32,8,4864]{2,1,0:T(8,128)(2,1)}), bf16[32,8,4864]{2,1,0:T(8,128)(2,1)S(1)}, u32[]{:S(2)}, u32[]{:S(2)}) async-start(bf16[32,8,4864]{2,1,0:T(8,128)(2,1)} %bitcast.19), calls=%async_computation.1 | async-start | bytes 4980736 | tf_op jit(solution)/shard_map/all_to_all | solution.py:412
  38.2 2.3 %shard_map.115 = (bf16[256,160]{1,0:T(8,128)(2,1)}, bf16[4,256,160]{2,1,0:T(8,128)(2,1)}, bf16[160,256]{1,0:T(8,128)(2,1)}, bf16[4,160,256]{2,1,0:T(8,128)(2,1)}) custom-call(bf16[256,1408]{1,0:T(8,128)(2,1)} %bitcast.5.recv_ref), custom_call_target="tpu_custom_call" | custom-call | flops 99999997952 | bytes 245760 | tf_op jit(solution)/shard_map/pallas_call | solution.py:456
  40.6 30.1 %all-to-all-done.1 = bf16[32,8,4864]{2,1,0:T(8,128)(2,1)S(1)} async-done(((bf16[32,8,4864]{2,1,0:T(8,128)(2,1)}), bf16[32,8,4864]{2,1,0:T(8,128)(2,1)S(1)}, u32[]{:S(2)}, u32[]{:S(2)}) %all-to-all-start.1) | async-done | bytes 2490400 | tf_op jit(solution)/shard_map/all_to_all | solution.py:412
  70.7 0.0 copy-start.4
  70.7 4.5 %all-to-all-start.2 = ((bf16[32,8,1664]{2,1,0:T(8,128)(2,1)}), bf16[32,8,1664]{2,1,0:T(8,128)(2,1)S(1)}, u32[]{:S(2)}, u32[]{:S(2)}) async-start(bf16[32,8,1664]{2,1,0:T(8,128)(2,1)} %bitcast.21), calls=%async_computation.2 | async-start | bytes 1703936 | tf_op jit(solution)/shard_map/all_to_all | solution.py:412
  75.2 0.2 reduce-scatter.2.cloned.1.call-start
  75.4 0.0 all-gather.2.cloned.1.call-done.kv_all_ref.key_ref.value_ref
  75.4 0.0 copy-done.4
  75.4 19.1 %shard_map.116 = (bf16[1280,1024]{1,0:T(8,128)(2,1)}, bf16[256,6400]{1,0:T(8,128)(2,1)}, bf16[256,1280]{1,0:T(8,128)(2,1)}) custom-call(s32[7]{0:T(128)} %pad_add_fusion.info_ref, f32[2]{0:T(128)} %bitcast.26, bf16[256,4864]{1,0:T(8,128)(2,1)} %bitcast.20, bf16[1280,1024]{1,0:T(8,128)(2,1)} %all-gather.2.cloned.1.call-done.kv_all_ref.key_ref.value_ref, ...), custom_call_target="tpu_custom_call" | custom-call | flops 99999997952 | bytes 8192000 | tf_op jit(solution)/shard_map/pallas_call | solution.py:486
  94.6 0.0 all-to-all-done.2
  94.6 0.0 copy-start.3
  94.6 0.9 copy-done.3
  95.6 8.1 %shard_map.117 = (bf16[1280,1024]{1,0:T(8,128)(2,1)}, bf16[256,6400]{1,0:T(8,128)(2,1)}) custom-call(s32[7]{0:T(128)} %pad_add_fusion.info_ref, f32[2]{0:T(128)} %bitcast.27, bf16[256,1664]{1,0:T(8,128)(2,1)} %bitcast.16, ...), custom_call_target="tpu_custom_call", output_to_operand_aliasing={{0}: (10, {}), {1}: (11, {})} | custom-call | flops 1572864000 | bytes 2048000 | tf_op jit(solution)/shard_map/pallas_call | solution.py:509
  103.7 0.0 reduce-scatter.2.cloned.1.call-update
  103.7 7.9 %all-to-all-start.3 = ((bf16[32,8,6400]{2,1,0:T(8,128)(2,1)}), bf16[32,8,6400]{2,1,0:T(8,128)(2,1)S(1)}, u32[]{:S(2)}, u32[]{:S(2)}) async-start(bf16[32,8,6400]{2,1,0:T(8,128)(2,1)} %bitcast.15), calls=%async_computation.3 | async-start | bytes 6553600 | tf_op jit(solution)/shard_map/all_to_all | solution.py:412
  111.6 0.0 copy-start.2
  111.7 35.2 %reduce-scatter.2.cloned.1.call-done.source_ref = bf16[160,1024]{1,0:T(8,128)(2,1)} async-done(((bf16[1280,1024]{1,0:T(8,128)(2,1)}), bf16[160,1024]{1,0:T(8,128)(2,1)}) %reduce-scatter.2.cloned.1.call-update) | async-done | bytes 327696 | tf_op jit(solution)/shard_map/reduce_scatter | solution.py:542
  146.9 2.5 %shard_map.118 = bf16[256,1280]{1,0:T(8,128)(2,1)} custom-call(bf16[160,1024]{1,0:T(8,128)(2,1)} %reduce-scatter.2.cloned.1.call-done.source_ref, bf16[256,160]{1,0:T(8,128)(2,1)} %get-tuple-element.54.r1_ref.m1_ref, bf16[4,256,160]{2,1,0:T(8,128)(2,1)} %get-tuple-element.55.r2_ref.m2_ref), custom_call_target="tpu_custom_call" | custom-call | flops 167772160 | bytes 1310720 | tf_op jit(solution)/shard_map/pallas_call | solution.py:543
  149.4 3.4 %all-to-all-done.3 = bf16[32,8,6400]{2,1,0:T(8,128)(2,1)S(1)} async-done(((bf16[32,8,6400]{2,1,0:T(8,128)(2,1)}), bf16[32,8,6400]{2,1,0:T(8,128)(2,1)S(1)}, u32[]{:S(2)}, u32[]{:S(2)}) %all-to-all-start.3) | async-done | bytes 3276832 | tf_op jit(solution)/shard_map/all_to_all | solution.py:412
  152.7 7.8 %all-to-all-start.4 = ((bf16[32,8,1280]{2,1,0:T(8,128)(2,1)}), bf16[32,8,1280]{2,1,0:T(8,128)(2,1)}, u32[]{:S(2)}, u32[]{:S(2)}) async-start(bf16[32,8,1280]{2,1,0:T(8,128)(2,1)} %bitcast.18), calls=%async_computation.5 | async-start | bytes 1310720 | tf_op jit(solution)/shard_map/all_to_all | solution.py:412
  160.6 0.0 copy-done.2
  160.6 0.0 copy-start
  160.6 1.0 copy-done
  161.5 2.1 %shard_map.119 = (bf16[160,2560]{1,0:T(8,128)(2,1)}, bf16[160,2560]{1,0:T(8,128)(2,1)}) custom-call(bf16[256,6400]{1,0:T(8,128)(2,1)S(1)} %bitcast.14, bf16[160,256]{1,0:T(8,128)(2,1)S(1)} %copy-done.2, bf16[4,160,256]{2,1,0:T(8,128)(2,1)S(1)} %copy-done), custom_call_target="tpu_custom_call" | custom-call | flops 99999997952 | bytes 6553600 | tf_op jit(solution)/shard_map/pallas_call | solution.py:551
  163.7 9.9 %all-to-all-done.4 = bf16[32,8,1280]{2,1,0:T(8,128)(2,1)} async-done(((bf16[32,8,1280]{2,1,0:T(8,128)(2,1)}), bf16[32,8,1280]{2,1,0:T(8,128)(2,1)}, u32[]{:S(2)}, u32[]{:S(2)}) %all-to-all-start.4) | async-done | bytes 655392 | tf_op jit(solution)/shard_map/all_to_all | solution.py:412
  173.6 0.0 copy-start.1
  173.6 1.0 copy-done.1
  174.5 2.2 %shard_map.120 = (bf16[160,512]{1,0:T(8,128)(2,1)}, bf16[160,512]{1,0:T(8,128)(2,1)}) custom-call(bf16[256,1280]{1,0:T(8,128)(2,1)} %bitcast.13.recv_ref, bf16[160,256]{1,0:T(8,128)(2,1)S(1)} %copy-done.2, bf16[4,160,256]{2,1,0:T(8,128)(2,1)S(1)} %copy-done.1), custom_call_target="tpu_custom_call" | custom-call | flops 167772160 | bytes 1048576 | tf_op jit(solution)/shard_map/pallas_call | solution.py:557
Async XLA Ops:
  9.8 22.3 %all-to-all-start = ((bf16[32,8,1408]{2,1,0:T(8,128)(2,1)}), bf16[32,8,1408]{2,1,0:T(8,128)(2,1)}, u32[]{:S(2)}, u32[]{:S(2)}) async-start(bf16[32,8,1408]{2,1,0:T(8,128)(2,1)} %bitcast.17), calls=%async_computation | async-start | bytes 1441792 | tf_op jit(solution)/shard_map/all_to_all | solution.py:412
  18.4 57.0 %all-gather.2.cloned.1.call-start = ((), (), s32[]{:S(2)}) async-start(), calls=%async_computation.6 | async-start | bytes 2949120 | tf_op jit(solution)/shard_map/all_gather | solution.py:454
  20.2 4.5 %copy-start.5 = (s32[1,2,3]{2,1,0:T(2,128)S(1)}, s32[1,2,3]{2,1,0:T(2,128)}, u32[]{:S(2)}) copy-start(s32[1,2,3]{2,1,0:T(2,128)} %param.13) | copy-start | bytes 76
  34.4 36.3 %all-to-all-start.1 = ((bf16[32,8,4864]{2,1,0:T(8,128)(2,1)}), bf16[32,8,4864]{2,1,0:T(8,128)(2,1)S(1)}, u32[]{:S(2)}, u32[]{:S(2)}) async-start(bf16[32,8,4864]{2,1,0:T(8,128)(2,1)} %bitcast.19), calls=%async_computation.1 | async-start | bytes 4980736 | tf_op jit(solution)/shard_map/all_to_all | solution.py:412
  70.7 4.8 %copy-start.4 = (bf16[32,8,4864]{2,1,0:T(8,128)(2,1)}, bf16[32,8,4864]{2,1,0:T(8,128)(2,1)S(1)}, u32[]{:S(2)}) copy-start(bf16[32,8,4864]{2,1,0:T(8,128)(2,1)S(1)} %all-to-all-done.1) | copy-start | bytes 7471108
  70.7 23.9 %all-to-all-start.2 = ((bf16[32,8,1664]{2,1,0:T(8,128)(2,1)}), bf16[32,8,1664]{2,1,0:T(8,128)(2,1)S(1)}, u32[]{:S(2)}, u32[]{:S(2)}) async-start(bf16[32,8,1664]{2,1,0:T(8,128)(2,1)} %bitcast.21), calls=%async_computation.2 | async-start | bytes 1703936 | tf_op jit(solution)/shard_map/all_to_all | solution.py:412
  75.2 71.7 %reduce-scatter.2.cloned.1.call-start = ((), (), s32[]{:S(2)}) async-start(), calls=%async_computation.7 | async-start | bytes 2949120 | tf_op jit(solution)/shard_map/reduce_scatter | solution.py:542
  94.6 1.0 copy-start.3
  103.7 49.0 %all-to-all-start.3 = ((bf16[32,8,6400]{2,1,0:T(8,128)(2,1)}), bf16[32,8,6400]{2,1,0:T(8,128)(2,1)S(1)}, u32[]{:S(2)}, u32[]{:S(2)}) async-start(bf16[32,8,6400]{2,1,0:T(8,128)(2,1)} %bitcast.15), calls=%async_computation.3 | async-start | bytes 6553600 | tf_op jit(solution)/shard_map/all_to_all | solution.py:412
  111.6 48.9 %copy-start.2 = (bf16[160,256]{1,0:T(8,128)(2,1)S(1)}, bf16[160,256]{1,0:T(8,128)(2,1)}, u32[]{:S(2)}) copy-start(bf16[160,256]{1,0:T(8,128)(2,1)} %get-tuple-element.63.m1_ref) | copy-start | bytes 245764
  152.7 20.8 %all-to-all-start.4 = ((bf16[32,8,1280]{2,1,0:T(8,128)(2,1)}), bf16[32,8,1280]{2,1,0:T(8,128)(2,1)}, u32[]{:S(2)}, u32[]{:S(2)}) async-start(bf16[32,8,1280]{2,1,0:T(8,128)(2,1)} %bitcast.18), calls=%async_computation.5 | async-start | bytes 1310720 | tf_op jit(solution)/shard_map/all_to_all | solution.py:412
  160.6 1.0 copy-start
  173.6 1.0 copy-start.1
Sparse Core Ops, SparseCore 0:
  34.5 38.3 all-gather.1
  103.9 42.9 reduce-scatter.1

commit v3 on v1

--- a/solution.py
+++ b/solution.py
@@ -97,15 +97,21 @@
     )
 
 
-def home_maps_kernel(dest_ref, p1t_ref, p2t_ref):
-    rows, slots = p1t_ref.shape
+def home_kernel(dest_ref, home_ref):
     dest_col, same, down, across = ranks_of(dest_ref[...])
     rank_col = jnp.sum(jnp.where(same & (across < down), 1.0, 0.0), axis=1, keepdims=True)
     main_col, spare_col = places_of(dest_col, rank_col)
+    lane = iota(home_ref.shape, 1)
+    home_ref[...] = jnp.where(lane == 0, main_col, spare_col)
+
+
+def home_maps(home_ref, slots):
+    rows = home_ref.shape[0]
     slot_across = iota((rows, slots), 1)
-    p1t_ref[...] = one_hot(slot_across == main_col)
-    for g in range(KV_HEADS):
-        p2t_ref[g] = one_hot(slot_across == spare_col + SPARE * g)
+    spare_col = home_ref[:, 1:2]
+    return one_hot(slot_across == home_ref[:, :1]), [
+        one_hot(slot_across == spare_col + SPARE * g) for g in range(KV_HEADS)
+    ]
 
 
 def landing_of(recv_ref):
@@ -181,23 +187,23 @@
     send_ref[:, KV_HEADS * width :] = low(spare)
 
 
-def unpack_queries_kernel(recv_ref, m1_ref, m2_ref, attended_ref, grad_ref):
-    m1 = m1_ref[...]
+def unpack_queries_kernel(recv_ref, home_ref, attended_ref, grad_ref):
+    m1, m2 = home_maps(home_ref, recv_ref.shape[0])
     spare = recv_ref[:, KV_HEADS * BOTH_WIDTH :]
     for g in range(KV_HEADS):
         part = recv_ref[:, g * BOTH_WIDTH : (g + 1) * BOTH_WIDTH]
-        both = low(dot(m1, part) + dot(m2_ref[g], spare))
+        both = low(dot(m1, part) + dot(m2[g], spare))
         columns = slice(g * GROUP_WIDTH, (g + 1) * GROUP_WIDTH)
         attended_ref[:, columns] = both[:, :GROUP_WIDTH]
         grad_ref[:, columns] = both[:, GROUP_WIDTH:]
 
 
-def unpack_kv_kernel(recv_ref, m1_ref, m2_ref, key_ref, value_ref):
-    m1 = m1_ref[...]
+def unpack_kv_kernel(recv_ref, home_ref, key_ref, value_ref):
+    m1, m2 = home_maps(home_ref, recv_ref.shape[0])
     spare = recv_ref[:, KV_HEADS * PAIR_WIDTH :]
     for g in range(KV_HEADS):
         both = low(
-            dot(m1, recv_ref[:, g * PAIR_WIDTH : (g + 1) * PAIR_WIDTH]) + dot(m2_ref[g], spare)
+            dot(m1, recv_ref[:, g * PAIR_WIDTH : (g + 1) * PAIR_WIDTH]) + dot(m2[g], spare)
         )
         key_ref[:, g * HEAD_DIM : (g + 1) * HEAD_DIM] = both[:, :HEAD_DIM]
         value_ref[:, g * HEAD_DIM : (g + 1) * HEAD_DIM] = both[:, HEAD_DIM:]
@@ -223,11 +229,18 @@
 
 def attention_kernel(
     info_ref, weight_ref, main_ref, spare_ref, key_ref, value_ref, r1t_ref, r2t_ref, r1_ref, r2_ref,
-    kv_ref, send_ref, bias, spare_sum, value_ones, raised, dscore, score, dprob,
+    kv_ref, send_ref, bias, spare_sum, value_ones, raised, dscore, score, dprob, ready, left,
 ):
     step = pl.program_id(0)
     rows, keys = bias.shape
     count = len(score)
+    steps = KV_HEADS // count
+
+    def leave(k):
+        first = k * count * BOTH_WIDTH
+        columns = pl.ds(first, BOTH_WIDTH if k == steps else count * BOTH_WIDTH)
+        return pltpu.make_async_copy(ready.at[:, columns], send_ref.at[:, columns], left.at[k])
+
     e0, e1, e2, e3, e4, _ = ends_of(info_ref)
     place = info_ref[6] * rows + iota((rows, 1), 0)
     rejected = (place >= e1) & (place < e2)
@@ -287,12 +300,21 @@
         kv_ref[:, first + HEAD_DIM : first + PAIR_WIDTH] = low(dot(cotangent_low.T, raised[n][...])).T
         both = jnp.concatenate([unstack_heads(attended[n]), unstack_heads(query_grad)], axis=1)
         start = pl.multiple_of((step * count + n) * BOTH_WIDTH, BOTH_WIDTH)
-        send_ref[:, pl.ds(start, BOTH_WIDTH)] = low(dot(r1_ref[...], both))
+        ready[:, pl.ds(start, BOTH_WIDTH)] = low(dot(r1_ref[...], both))
         spare_sum[...] += dot(r2_ref[n], both)
 
-    @pl.when(step == KV_HEADS // count - 1)
+    for k in range(steps):
+
+        @pl.when(step == k)
+        def _():
+            leave(k).start()
+
+    @pl.when(step == steps - 1)
     def _():
-        send_ref[:, KV_HEADS * BOTH_WIDTH :] = low(spare_sum[...])
+        ready[:, KV_HEADS * BOTH_WIDTH :] = low(spare_sum[...])
+        leave(steps).start()
+        for k in range(steps + 1):
+            leave(k).wait()
 
 
 def shape(dims, kind=jnp.bfloat16):
@@ -331,9 +353,9 @@
     )(dest, route_slot.reshape(1, rows), keys, values)
 
     kv_recv = exchange(kv_send)
-    p1t, p2t = pl.pallas_call(
-        home_maps_kernel,
-        out_shape=across,
+    home = pl.pallas_call(
+        home_kernel,
+        out_shape=shape((rows, HEAD_DIM), jnp.int32),
         compiler_params=compiler_params(),
         cost_estimate=cost(LONG, 6 * slots * rows),
     )(dest)
@@ -343,7 +365,7 @@
         compiler_params=compiler_params(),
         cost_estimate=cost(LONG, 10 * slots * QUERY_WIDTH),
     )(queries, out_grad, p1, p2)
-    kv_recv, query_send, p1t, p2t = fence((kv_recv, query_send, p1t, p2t))
+    kv_recv, query_send, home = fence((kv_recv, query_send, home))
 
     kv_own = pl.pallas_call(
         receive_kernel,
@@ -389,7 +411,7 @@
         ],
         out_specs=(
             pl.BlockSpec((seq, at_once * PAIR_WIDTH), lambda g: (0, g)),
-            pl.BlockSpec((slots, wide), lambda g: (0, 0)),
+            pl.BlockSpec(memory_space=pl.ANY),
         ),
         out_shape=(shape((seq, 2 * KV_WIDTH)), shape((slots, wide))),
         scratch_shapes=[
@@ -400,6 +422,8 @@
             several((GROUP * rows, seq)),
             several((GROUP * rows, seq), jnp.float32),
             several((GROUP * rows, seq), jnp.float32),
+            pltpu.VMEM((slots, wide), jnp.bfloat16),
+            pltpu.SemaphoreType.DMA((steps + 1,)),
         ],
         compiler_params=compiler_params(dimension_semantics=("arbitrary",)),
         cost_estimate=cost(12 * work, 2 * HEADS * rows * seq, HEADS * rows * seq),
@@ -420,15 +444,15 @@
     attended, query_grad = pl.pallas_call(
         unpack_queries_kernel,
         out_shape=(shape((rows, QUERY_WIDTH)), shape((rows, QUERY_WIDTH))),
-        compiler_params=compiler_params(),
+        compiler_params=compiler_params(SMALL_VMEM),
         cost_estimate=cost(LONG, 10 * slots * QUERY_WIDTH),
-    )(back_recv, p1t, p2t)
+    )(back_recv, home)
     key_grad, value_grad = pl.pallas_call(
         unpack_kv_kernel,
         out_shape=(shape((rows, KV_WIDTH)), shape((rows, KV_WIDTH))),
         compiler_params=compiler_params(SMALL_VMEM),
         cost_estimate=cost(4 * slots * rows * 2 * KV_WIDTH, 4 * slots * 2 * KV_WIDTH),
-    )(kv_back, p1t, p2t)
+    )(kv_back, home)
     return attended, query_grad, key_grad, value_grad
 
 

time: 180 us -> 180 us (level)
  waiting for transfers between devices: 92.2 us -> 94.6 us
    all_to_all x4, waiting for transfers between devices: 56.7 us -> 59.4 us  [exchange(): lax.all_to_all(block.reshape(ranks, MAIN, block.shape[1]), 'dp', split_ax...]
    pallas_call x1, Pallas kernels: 4.19 us -> 2.18 us  [body(): pl.pallas_call(unpack_queries_kernel, out_shape=(shape((rows, QUERY_WIDTH...]
  transfers between devices with their start and end apart: 6 -> 6, of which waited for: 5 -> 5; matrix products, arithmetic and copies ran while one was open for 0% -> 0% of each run, Pallas kernels for 9% -> 7%
where the time goes in v3:
time: 180 us; the launch traced here: 179 us
  waiting for transfers between devices  94.6 us (53%)
  Pallas kernels  41.6 us (23%)
  starting transfers between devices  26.8 us (15%)
  between operations  14.1 us (8%)
  local copies, waits for them, and re-layouts  1.81 us (1%)
    all_to_all x4, waiting for transfers between devices, exchange(): lax.all_to_all(block.reshape(ranks, MAIN, block.shape[1]), 'dp', split_ax...  59.4 us
    reduce_scatter x1, waiting for transfers between devices, body(): kv_grad = lax.psum_scatter(kv_part, 'pack', scatter_dimension=0, tiled=True)  35.2 us
    all_to_all x4, starting transfers between devices, exchange(): lax.all_to_all(block.reshape(ranks, MAIN, block.shape[1]), 'dp', split_ax...  26.6 us
    pallas_call x1, Pallas kernels, body(): pl.pallas_call(attention_kernel, grid=(steps,), in_specs=[smem, smem, pl....  21.3 us
    pallas_call x1, Pallas kernels, body(): pl.pallas_call(pack_queries_kernel, out_shape=shape((slots, wide)), compi...  4.77 us
  transfers between devices with their start and end apart: 6, of which 5 were waited for; matrix products, arithmetic and copies ran while one was open for 0% of the time, Pallas kernels for 7%

profile of v3, /device:TPU:1, one launch (start us, length us, event | category | flops | bytes accessed | tf_op | source)
XLA Modules:
  0.0 179.5 jit_solution(10994345868394276714)
XLA Ops:
  7.2 2.6 %shard_map.111 = (bf16[256,1408]{1,0:T(8,128)(2,1)}, bf16[256,160]{1,0:T(8,128)(2,1)}, bf16[4,256,160]{2,1,0:T(8,128)(2,1)}) custom-call(s32[1,160]{1,0:T(1,128)} %bitcast.20, s32[1,160]{1,0:T(1,128)} %bitcast.19, bf16[160,512]{1,0:T(8,128)(2,1)} %keys_ref.1, bf16[160,512]{1,0:T(8,128)(2,1)} %values_ref.1), custom_call_target="tpu_custom_call" | custom-call | flops 167772160 | bytes 1572864 | tf_op jit(solution)/shard_map/pallas_call | solution.py:348
  9.8 8.6 %all-to-all-start = ((bf16[32,8,1408]{2,1,0:T(8,128)(2,1)}), bf16[32,8,1408]{2,1,0:T(8,128)(2,1)}, u32[]{:S(2)}, u32[]{:S(2)}) async-start(bf16[32,8,1408]{2,1,0:T(8,128)(2,1)} %bitcast.18), calls=%async_computation | async-start | bytes 1441792 | tf_op jit(solution)/shard_map/all_to_all | solution.py:339
  18.5 0.0 all-gather.2.cloned.1.call-start
  18.5 1.5 shard_map.113.home_ref
  20.0 0.0 copy-start.2
  20.0 4.8 %shard_map.112 = bf16[256,6400]{1,0:T(8,128)(2,1)} custom-call(bf16[160,2560]{1,0:T(8,128)(2,1)} %query_ref.1, bf16[160,2560]{1,0:T(8,128)(2,1)} %grad_ref.1, bf16[256,160]{1,0:T(8,128)(2,1)} %get-tuple-element.25.m1_ref, bf16[4,256,160]{2,1,0:T(8,128)(2,1)} %get-tuple-element.26.m2_ref), custom_call_target="tpu_custom_call" | custom-call | flops 99999997952 | bytes 6553600 | tf_op jit(solution)/shard_map/pallas_call | solution.py:362
  24.8 0.0 copy-done.2
  24.8 0.1 reshape.47
  24.9 0.6 pad_add_fusion.info_ref
  25.4 6.7 %all-to-all-done = bf16[32,8,1408]{2,1,0:T(8,128)(2,1)} async-done(((bf16[32,8,1408]{2,1,0:T(8,128)(2,1)}), bf16[32,8,1408]{2,1,0:T(8,128)(2,1)}, u32[]{:S(2)}, u32[]{:S(2)}) %all-to-all-start) | async-done | bytes 720928 | tf_op jit(solution)/shard_map/all_to_all | solution.py:339
  32.1 2.3 %shard_map.114 = bf16[160,1024]{1,0:T(8,128)(2,1)} custom-call(bf16[256,1408]{1,0:T(8,128)(2,1)} %bitcast.5.recv_ref), custom_call_target="tpu_custom_call" | custom-call | flops 167772160 | bytes 1572864 | tf_op jit(solution)/shard_map/pallas_call | solution.py:370
  34.4 0.0 all-gather.2.cloned.1.call-update
  34.4 3.9 %all-to-all-start.1 = ((bf16[32,8,6400]{2,1,0:T(8,128)(2,1)}), bf16[32,8,6400]{2,1,0:T(8,128)(2,1)S(1)}, u32[]{:S(2)}, u32[]{:S(2)}) async-start(bf16[32,8,6400]{2,1,0:T(8,128)(2,1)} %bitcast.13), calls=%async_computation.1 | async-start | bytes 6553600 | tf_op jit(solution)/shard_map/all_to_all | solution.py:339
  38.3 0.2 reduce-scatter.2.cloned.1.call-start
  38.5 2.3 %shard_map.115 = (bf16[256,160]{1,0:T(8,128)(2,1)}, bf16[4,256,160]{2,1,0:T(8,128)(2,1)}, bf16[160,256]{1,0:T(8,128)(2,1)}, bf16[4,160,256]{2,1,0:T(8,128)(2,1)}) custom-call(bf16[256,1408]{1,0:T(8,128)(2,1)} %bitcast.5.recv_ref), custom_call_target="tpu_custom_call" | custom-call | flops 99999997952 | bytes 245760 | tf_op jit(solution)/shard_map/pallas_call | solution.py:378
  40.8 38.5 %all-to-all-done.1 = bf16[32,8,6400]{2,1,0:T(8,128)(2,1)S(1)} async-done(((bf16[32,8,6400]{2,1,0:T(8,128)(2,1)}), bf16[32,8,6400]{2,1,0:T(8,128)(2,1)S(1)}, u32[]{:S(2)}, u32[]{:S(2)}) %all-to-all-start.1) | async-done | bytes 3276832 | tf_op jit(solution)/shard_map/all_to_all | solution.py:339
  79.3 0.0 copy-start.1
  79.3 0.0 all-gather.2.cloned.1.call-done.key_ref.value_ref
  79.3 1.7 copy-done.1
  81.0 21.3 %shard_map.116 = (bf16[1280,1024]{1,0:T(8,128)(2,1)}, bf16[256,6400]{1,0:T(8,128)(2,1)}) custom-call(s32[7]{0:T(128)} %pad_add_fusion.info_ref, f32[2]{0:T(128)} %bitcast.22, bf16[256,6400]{1,0:T(8,128)(2,1)} %bitcast.14, bf16[256,6400]{1,0:T(8,128)(2,1)} %bitcast.15, bf16[1280,1024]{1,0:T(8,128)(2,1)} %all-gather.2.cloned.1.call-done.key_ref.value_ref, ...), custom_call_target="tpu_custom_call" | custom-call | flops 6291456000 | bytes 8192000 | tf_op jit(solution)/shard_map/pallas_call | solution.py:397
  102.3 0.0 reduce-scatter.2.cloned.1.call-update
  102.3 0.0 copy-start
  102.3 5.8 %all-to-all-start.2 = ((bf16[32,8,6400]{2,1,0:T(8,128)(2,1)}), bf16[32,8,6400]{2,1,0:T(8,128)(2,1)S(1)}, u32[]{:S(2)}, u32[]{:S(2)}) async-start(bf16[32,8,6400]{2,1,0:T(8,128)(2,1)} %bitcast.16), calls=%async_computation.2 | async-start | bytes 6553600 | tf_op jit(solution)/shard_map/all_to_all | solution.py:339
  108.1 35.2 %reduce-scatter.2.cloned.1.call-done.source_ref = bf16[160,1024]{1,0:T(8,128)(2,1)} async-done(((bf16[1280,1024]{1,0:T(8,128)(2,1)}), bf16[160,1024]{1,0:T(8,128)(2,1)}) %reduce-scatter.2.cloned.1.call-update) | async-done | bytes 327696 | tf_op jit(solution)/shard_map/reduce_scatter | solution.py:435
  143.3 2.5 %shard_map.117 = bf16[256,1280]{1,0:T(8,128)(2,1)} custom-call(bf16[160,1024]{1,0:T(8,128)(2,1)} %reduce-scatter.2.cloned.1.call-done.source_ref, bf16[256,160]{1,0:T(8,128)(2,1)} %get-tuple-element.33.r1_ref.m1_ref, bf16[4,256,160]{2,1,0:T(8,128)(2,1)} %get-tuple-element.34.r2_ref.m2_ref), custom_call_target="tpu_custom_call" | custom-call | flops 167772160 | bytes 1310720 | tf_op jit(solution)/shard_map/pallas_call | solution.py:436
  145.8 3.4 %all-to-all-done.2 = bf16[32,8,6400]{2,1,0:T(8,128)(2,1)S(1)} async-done(((bf16[32,8,6400]{2,1,0:T(8,128)(2,1)}), bf16[32,8,6400]{2,1,0:T(8,128)(2,1)S(1)}, u32[]{:S(2)}, u32[]{:S(2)}) %all-to-all-start.2) | async-done | bytes 3276832 | tf_op jit(solution)/shard_map/all_to_all | solution.py:339
  149.2 8.2 %all-to-all-start.3 = ((bf16[32,8,1280]{2,1,0:T(8,128)(2,1)}), bf16[32,8,1280]{2,1,0:T(8,128)(2,1)}, u32[]{:S(2)}, u32[]{:S(2)}) async-start(bf16[32,8,1280]{2,1,0:T(8,128)(2,1)} %bitcast.17), calls=%async_computation.4 | async-start | bytes 1310720 | tf_op jit(solution)/shard_map/all_to_all | solution.py:339
  157.5 0.0 copy-done
  157.5 2.2 %shard_map.118 = (bf16[160,2560]{1,0:T(8,128)(2,1)}, bf16[160,2560]{1,0:T(8,128)(2,1)}) custom-call(bf16[256,6400]{1,0:T(8,128)(2,1)S(1)} %bitcast.12, s32[160,128]{1,0:T(8,128)S(1)} %copy-done), custom_call_target="tpu_custom_call" | custom-call | flops 99999997952 | bytes 6553600 | tf_op jit(solution)/shard_map/pallas_call | solution.py:444
  159.7 10.8 %all-to-all-done.3 = bf16[32,8,1280]{2,1,0:T(8,128)(2,1)} async-done(((bf16[32,8,1280]{2,1,0:T(8,128)(2,1)}), bf16[32,8,1280]{2,1,0:T(8,128)(2,1)}, u32[]{:S(2)}, u32[]{:S(2)}) %all-to-all-start.3) | async-done | bytes 655392 | tf_op jit(solution)/shard_map/all_to_all | solution.py:339
  170.5 2.2 %shard_map.119 = (bf16[160,512]{1,0:T(8,128)(2,1)}, bf16[160,512]{1,0:T(8,128)(2,1)}) custom-call(bf16[256,1280]{1,0:T(8,128)(2,1)} %bitcast.11.recv_ref, s32[160,128]{1,0:T(8,128)S(1)} %copy-done), custom_call_target="tpu_custom_call" | custom-call | flops 167772160 | bytes 1048576 | tf_op jit(solution)/shard_map/pallas_call | solution.py:450
Async XLA Ops:
  9.8 22.3 %all-to-all-start = ((bf16[32,8,1408]{2,1,0:T(8,128)(2,1)}), bf16[32,8,1408]{2,1,0:T(8,128)(2,1)}, u32[]{:S(2)}, u32[]{:S(2)}) async-start(bf16[32,8,1408]{2,1,0:T(8,128)(2,1)} %bitcast.18), calls=%async_computation | async-start | bytes 1441792 | tf_op jit(solution)/shard_map/all_to_all | solution.py:339
  18.5 60.8 %all-gather.2.cloned.1.call-start = ((), (), s32[]{:S(2)}) async-start(), calls=%async_computation.5 | async-start | bytes 2949120 | tf_op jit(solution)/shard_map/all_gather | solution.py:376
  20.0 4.8 %copy-start.2 = (s32[1,2,3]{2,1,0:T(2,128)S(1)}, s32[1,2,3]{2,1,0:T(2,128)}, u32[]{:S(2)}) copy-start(s32[1,2,3]{2,1,0:T(2,128)} %param.13) | copy-start | bytes 76
  34.4 44.9 %all-to-all-start.1 = ((bf16[32,8,6400]{2,1,0:T(8,128)(2,1)}), bf16[32,8,6400]{2,1,0:T(8,128)(2,1)S(1)}, u32[]{:S(2)}, u32[]{:S(2)}) async-start(bf16[32,8,6400]{2,1,0:T(8,128)(2,1)} %bitcast.13), calls=%async_computation.1 | async-start | bytes 6553600 | tf_op jit(solution)/shard_map/all_to_all | solution.py:339
  38.3 105.0 %reduce-scatter.2.cloned.1.call-start = ((), (), s32[]{:S(2)}) async-start(), calls=%async_computation.6 | async-start | bytes 2949120 | tf_op jit(solution)/shard_map/reduce_scatter | solution.py:435
  79.3 1.7 copy-start.1
  102.3 55.2 %copy-start = (s32[160,128]{1,0:T(8,128)S(1)}, s32[160,128]{1,0:T(8,128)}, u32[]{:S(2)}) copy-start(s32[160,128]{1,0:T(8,128)} %shard_map.113.home_ref) | copy-start | bytes 245764
  102.3 46.9 %all-to-all-start.2 = ((bf16[32,8,6400]{2,1,0:T(8,128)(2,1)}), bf16[32,8,6400]{2,1,0:T(8,128)(2,1)S(1)}, u32[]{:S(2)}, u32[]{:S(2)}) async-start(bf16[32,8,6400]{2,1,0:T(8,128)(2,1)} %bitcast.16), calls=%async_computation.2 | async-start | bytes 6553600 | tf_op jit(solution)/shard_map/all_to_all | solution.py:339
  149.2 21.2 %all-to-all-start.3 = ((bf16[32,8,1280]{2,1,0:T(8,128)(2,1)}), bf16[32,8,1280]{2,1,0:T(8,128)(2,1)}, u32[]{:S(2)}, u32[]{:S(2)}) async-start(bf16[32,8,1280]{2,1,0:T(8,128)(2,1)} %bitcast.17), calls=%async_computation.4 | async-start | bytes 1310720 | tf_op jit(solution)/shard_map/all_to_all | solution.py:339
Sparse Core Ops, SparseCore 0:
  34.5 38.3 all-gather.1
  102.4 40.8 reduce-scatter.1

commit v4 on v3

--- a/solution.py
+++ b/solution.py
@@ -114,9 +114,9 @@
     ]
 
 
-def landing_of(recv_ref):
-    slots = recv_ref.shape[0]
-    tile = recv_ref[:, 5 * PAIR_WIDTH :].astype(jnp.float32)
+def landing_of(tile):
+    slots = tile.shape[0]
+    tile = tile.astype(jnp.float32)
     lane = iota((slots, HEAD_DIM), 1)
     main_col = jnp.sum(jnp.where(lane == 0, tile, 0.0), axis=1, keepdims=True)
     spare_col = jnp.sum(jnp.where(lane == 1, tile, 0.0), axis=1, keepdims=True)
@@ -132,36 +132,32 @@
     )
 
 
-def landing_maps(rows, slots, main_row, spare_row):
+def across_maps(rows, main_row, spare_row):
+    slots = main_row.shape[1]
     place_down = iota((rows, slots), 0) + 1
     part_across = (iota((rows, slots), 1) & (MAIN - 1)) >> 1
-    r1t = one_hot(place_down == main_row)
-    return r1t, [one_hot((place_down == spare_row) & (part_across == g)) for g in range(KV_HEADS)]
-
-
-def receive_kernel(recv_ref, kv_ref):
-    rows = kv_ref.shape[0]
-    slots = recv_ref.shape[0]
-    r1t, r2t = landing_maps(rows, slots, *landing_rows(*landing_of(recv_ref)))
-    spare = recv_ref[:, 4 * PAIR_WIDTH : 5 * PAIR_WIDTH]
-    for g in range(KV_HEADS):
-        columns = slice(g * PAIR_WIDTH, (g + 1) * PAIR_WIDTH)
-        kv_ref[:, columns] = low(dot(r1t, recv_ref[:, columns]) + dot(r2t[g], spare))
-
-
-def landing_maps_kernel(recv_ref, r1_ref, r2_ref, r1t_ref, r2t_ref):
-    slots, rows = r1_ref.shape
-    main_col, spare_col = landing_of(recv_ref)
-    r1t, r2t = landing_maps(rows, slots, *landing_rows(main_col, spare_col))
-    r1t_ref[...] = r1t
+    return one_hot(place_down == main_row), [
+        one_hot((place_down == spare_row) & (part_across == g)) for g in range(KV_HEADS)
+    ]
+
+
+def down_maps(rows, main_col, spare_col):
+    slots = main_col.shape[0]
     main_col = main_col.astype(jnp.int32)
     spare_col = spare_col.astype(jnp.int32)
     place_across = iota((slots, rows), 1) + 1
     part_down = (iota((slots, rows), 0) & (MAIN - 1)) >> 1
-    r1_ref[...] = one_hot(place_across == main_col)
-    for g in range(KV_HEADS):
-        r2_ref[g] = one_hot((place_across == spare_col) & (part_down == g))
-        r2t_ref[g] = r2t[g]
+    return one_hot(place_across == main_col), [
+        one_hot((place_across == spare_col) & (part_down == g)) for g in range(KV_HEADS)
+    ]
+
+
+def receive_kernel(recv_ref, kv_ref):
+    r1t, r2t = across_maps(kv_ref.shape[0], *landing_rows(*landing_of(recv_ref[:, 5 * PAIR_WIDTH :])))
+    spare = recv_ref[:, 4 * PAIR_WIDTH : 5 * PAIR_WIDTH]
+    for g in range(KV_HEADS):
+        columns = slice(g * PAIR_WIDTH, (g + 1) * PAIR_WIDTH)
+        kv_ref[:, columns] = low(dot(r1t, recv_ref[:, columns]) + dot(r2t[g], spare))
 
 
 def pack_queries_kernel(query_ref, grad_ref, m1_ref, m2_ref, send_ref):
@@ -175,15 +171,15 @@
     send_ref[:, KV_HEADS * BOTH_WIDTH :] = low(spare)
 
 
-def pack_kernel(source_ref, m1_ref, m2_ref, send_ref):
+def pack_kernel(source_ref, landing_ref, send_ref):
     width = source_ref.shape[1] // KV_HEADS
-    m1 = m1_ref[...]
+    m1, m2 = down_maps(source_ref.shape[0], *landing_of(landing_ref[...]))
     spare = jnp.zeros((send_ref.shape[0], width), jnp.float32)
     for g in range(KV_HEADS):
         columns = slice(g * width, (g + 1) * width)
         part = low(source_ref[:, columns])
         send_ref[:, columns] = low(dot(m1, part))
-        spare += dot(m2_ref[g], part)
+        spare += dot(m2[g], part)
     send_ref[:, KV_HEADS * width :] = low(spare)
 
 
@@ -228,8 +224,9 @@
 
 
 def attention_kernel(
-    info_ref, weight_ref, main_ref, spare_ref, key_ref, value_ref, r1t_ref, r2t_ref, r1_ref, r2_ref,
+    info_ref, weight_ref, main_ref, spare_ref, key_ref, value_ref, landing_ref,
     kv_ref, send_ref, bias, spare_sum, value_ones, raised, dscore, score, dprob, ready, left,
+    r1, r2, r1t, r2t,
 ):
     step = pl.program_id(0)
     rows, keys = bias.shape
@@ -254,6 +251,12 @@
         seen = (other >= first) & (other <= place) & ((other < hidden_from) | (other >= hidden_to))
         bias[...] = jnp.where(seen, 0.0, MASKED)
         spare_sum[...] = jnp.zeros_like(spare_sum)
+        landing = landing_of(landing_ref[...])
+        r1[...], down = down_maps(rows, *landing)
+        r1t[...], across = across_maps(rows, *landing_rows(*landing))
+        for g in range(KV_HEADS):
+            r2[g] = down[g]
+            r2t[g] = across[g]
         for n in range(count):
             value_ones[n][:, HEAD_DIM:] = jnp.ones((keys, HEAD_DIM), jnp.bfloat16)
 
@@ -262,8 +265,8 @@
     query, cotangent, key, inverse, attended, delta = ([None] * count for _ in range(6))
     for n in range(count):
         columns = slice(n * HEAD_DIM, (n + 1) * HEAD_DIM)
-        both = dot(r1t_ref[...], main_ref[:, n * BOTH_WIDTH : (n + 1) * BOTH_WIDTH]) + dot(
-            r2t_ref[n], spare_ref[...]
+        both = dot(r1t[...], main_ref[:, n * BOTH_WIDTH : (n + 1) * BOTH_WIDTH]) + dot(
+            r2t[step * count + n], spare_ref[...]
         )
         query[n] = stack_heads(low(both[:, :GROUP_WIDTH]))
         cotangent[n] = stack_heads(low(factor * both[:, GROUP_WIDTH:]))
@@ -300,8 +303,8 @@
         kv_ref[:, first + HEAD_DIM : first + PAIR_WIDTH] = low(dot(cotangent_low.T, raised[n][...])).T
         both = jnp.concatenate([unstack_heads(attended[n]), unstack_heads(query_grad)], axis=1)
         start = pl.multiple_of((step * count + n) * BOTH_WIDTH, BOTH_WIDTH)
-        ready[:, pl.ds(start, BOTH_WIDTH)] = low(dot(r1_ref[...], both))
-        spare_sum[...] += dot(r2_ref[n], both)
+        ready[:, pl.ds(start, BOTH_WIDTH)] = low(dot(r1[...], both))
+        spare_sum[...] += dot(r2[step * count + n], both)
 
     for k in range(steps):
 
@@ -342,7 +345,6 @@
         return moved.reshape(block.shape)
 
     down = (shape((slots, rows)), shape((KV_HEADS, slots, rows)))
-    across = (shape((rows, slots)), shape((KV_HEADS, rows, slots)))
     dest = route_dest.reshape(1, rows)
 
     kv_send, p1, p2 = pl.pallas_call(
@@ -365,7 +367,10 @@
         compiler_params=compiler_params(),
         cost_estimate=cost(LONG, 10 * slots * QUERY_WIDTH),
     )(queries, out_grad, p1, p2)
-    kv_recv, query_send, home = fence((kv_recv, query_send, home))
+    info = jnp.concatenate(
+        [lengths.reshape(6), lax.axis_index("pack").astype(jnp.int32).reshape(1)]
+    )
+    kv_recv, query_send, home, info = fence((kv_recv, query_send, home, info))
 
     kv_own = pl.pallas_call(
         receive_kernel,
@@ -374,20 +379,12 @@
         cost_estimate=cost(4 * slots * rows * 2 * KV_WIDTH, 6 * slots * 2 * KV_WIDTH),
     )(kv_recv)
     kv_all = lax.all_gather(kv_own, "pack", axis=0, tiled=True)
-    kv_recv, query_send, kv_own = fence((kv_recv, query_send, kv_own))
-    r1, r2, r1t, r2t = pl.pallas_call(
-        landing_maps_kernel,
-        out_shape=(*down, *across),
-        compiler_params=compiler_params(),
-        cost_estimate=cost(LONG, 6 * slots * rows),
-    )(kv_recv)
+    query_send, kv_own = fence((query_send, kv_own))
     query_recv = exchange(query_send)
 
-    info = jnp.concatenate(
-        [lengths.reshape(6), lax.axis_index("pack").astype(jnp.int32).reshape(1)]
-    )
     smem = pl.BlockSpec(memory_space=pltpu.SMEM)
     at_once = 2
+    landing_spec = pl.BlockSpec((slots, HEAD_DIM), lambda g: (0, narrow // HEAD_DIM))
     steps = KV_HEADS // at_once
     work = HEADS * rows * seq * HEAD_DIM
 
@@ -404,10 +401,7 @@
             pl.BlockSpec((slots, BOTH_WIDTH), lambda g: (0, KV_HEADS)),
             pl.BlockSpec((seq, at_once * HEAD_DIM), lambda g: (0, g)),
             pl.BlockSpec((seq, at_once * HEAD_DIM), lambda g: (0, steps + g)),
-            pl.BlockSpec((rows, slots), lambda g: (0, 0)),
-            pl.BlockSpec((at_once, rows, slots), lambda g: (g, 0, 0)),
-            pl.BlockSpec((slots, rows), lambda g: (0, 0)),
-            pl.BlockSpec((at_once, slots, rows), lambda g: (g, 0, 0)),
+            landing_spec,
         ],
         out_specs=(
             pl.BlockSpec((seq, at_once * PAIR_WIDTH), lambda g: (0, g)),
@@ -424,21 +418,28 @@
             several((GROUP * rows, seq), jnp.float32),
             pltpu.VMEM((slots, wide), jnp.bfloat16),
             pltpu.SemaphoreType.DMA((steps + 1,)),
+            pltpu.VMEM((slots, rows), jnp.bfloat16),
+            pltpu.VMEM((KV_HEADS, slots, rows), jnp.bfloat16),
+            pltpu.VMEM((rows, slots), jnp.bfloat16),
+            pltpu.VMEM((KV_HEADS, rows, slots), jnp.bfloat16),
         ],
         compiler_params=compiler_params(dimension_semantics=("arbitrary",)),
         cost_estimate=cost(12 * work, 2 * HEADS * rows * seq, HEADS * rows * seq),
     )(
-        info, pair_weight.reshape(2), query_recv, query_recv, kv_all, kv_all, r1t, r2t, r1, r2,
+        info, pair_weight.reshape(2), query_recv, query_recv, kv_all, kv_all, kv_recv,
     )
 
     back_recv = exchange(back_send)
     kv_grad = lax.psum_scatter(kv_part, "pack", scatter_dimension=0, tiled=True)
     kv_grad_send = pl.pallas_call(
         pack_kernel,
+        grid=(1,),
+        in_specs=[pl.BlockSpec((rows, 2 * KV_WIDTH), lambda i: (0, 0)), landing_spec],
+        out_specs=pl.BlockSpec((slots, narrow), lambda i: (0, 0)),
         out_shape=shape((slots, narrow)),
         compiler_params=compiler_params(),
         cost_estimate=cost(4 * slots * rows * 2 * KV_WIDTH, 10 * slots * KV_WIDTH),
-    )(kv_grad, r1, r2)
+    )(kv_grad, kv_recv)
     back_recv, kv_grad_send = fence((back_recv, kv_grad_send))
     kv_back = exchange(kv_grad_send)
     attended, query_grad = pl.pallas_call(

time: 180 us -> 178 us (0.989)
  blocking collectives: 0 us -> 45.8 us
  waiting for transfers between devices: 94.6 us -> 56.4 us
  starting transfers between devices: 26.8 us -> 20.7 us
  Pallas kernels: 41.6 us -> 39.5 us
    all_to_all x0 -> x1, blocking collectives: none -> 45.8 us  [exchange(): lax.all_to_all(block.reshape(ranks, MAIN, block.shape[1]), 'dp', split_ax...]
    all_to_all x4 -> x3, waiting for transfers between devices: 59.4 us -> 21.5 us  [exchange(): lax.all_to_all(block.reshape(ranks, MAIN, block.shape[1]), 'dp', split_ax...]
    all_to_all x4 -> x3, starting transfers between devices: 26.6 us -> 20.6 us  [exchange(): lax.all_to_all(block.reshape(ranks, MAIN, block.shape[1]), 'dp', split_ax...]
    pallas_call x2 -> x1, Pallas kernels: 4.77 us -> 2.33 us  [body(): pl.pallas_call(pack_kernel, grid=(1,), in_specs=[pl.BlockSpec((rows, 2 *...]
  transfers between devices with their start and end apart: 6 -> 5, of which waited for: 5 -> 4; matrix products, arithmetic and copies ran while one was open for 0% -> 0% of each run, Pallas kernels for 7% -> 6%
where the time goes in v4:
time: 178 us; the launch traced here: 177 us
  waiting for transfers between devices  56.4 us (32%)
  blocking collectives  45.8 us (26%)
  Pallas kernels  39.5 us (22%)
  starting transfers between devices  20.7 us (12%)
  between operations  14.1 us (8%)
    all_to_all x1, blocking collectives, exchange(): lax.all_to_all(block.reshape(ranks, MAIN, block.shape[1]), 'dp', split_ax...  45.8 us
    reduce_scatter x1, waiting for transfers between devices, body(): kv_grad = lax.psum_scatter(kv_part, 'pack', scatter_dimension=0, tiled=True)  34.8 us
    pallas_call x1, Pallas kernels, body(): pl.pallas_call(attention_kernel, grid=(steps,), in_specs=[smem, smem, pl....  21.6 us
    all_to_all x3, waiting for transfers between devices, exchange(): lax.all_to_all(block.reshape(ranks, MAIN, block.shape[1]), 'dp', split_ax...  21.5 us
    all_to_all x3, starting transfers between devices, exchange(): lax.all_to_all(block.reshape(ranks, MAIN, block.shape[1]), 'dp', split_ax...  20.6 us
    pallas_call x1, Pallas kernels, body(): pl.pallas_call(pack_queries_kernel, out_shape=shape((slots, wide)), compi...  4.78 us
  transfers between devices with their start and end apart: 5, of which 4 were waited for; matrix products, arithmetic and copies ran while one was open for 0% of the time, Pallas kernels for 6%

profile of v4, /device:TPU:1, one launch (start us, length us, event | category | flops | bytes accessed | tf_op | source)
XLA Modules:
  0.0 177.1 jit_solution(14473722906106812682)
XLA Ops:
  7.2 2.6 %shard_map.111 = (bf16[256,1408]{1,0:T(8,128)(2,1)}, bf16[256,160]{1,0:T(8,128)(2,1)}, bf16[4,256,160]{2,1,0:T(8,128)(2,1)}) custom-call(s32[1,160]{1,0:T(1,128)} %bitcast.20, s32[1,160]{1,0:T(1,128)} %bitcast.19, bf16[160,512]{1,0:T(8,128)(2,1)} %keys_ref.1, bf16[160,512]{1,0:T(8,128)(2,1)} %values_ref.1), custom_call_target="tpu_custom_call" | custom-call | flops 167772160 | bytes 1572864 | tf_op jit(solution)/shard_map/pallas_call | solution.py:350
  9.8 8.6 %all-to-all-start = ((bf16[32,8,1408]{2,1,0:T(8,128)(2,1)}), bf16[32,8,1408]{2,1,0:T(8,128)(2,1)}, u32[]{:S(2)}, u32[]{:S(2)}) async-start(bf16[32,8,1408]{2,1,0:T(8,128)(2,1)} %bitcast.18), calls=%async_computation | async-start | bytes 1441792 | tf_op jit(solution)/shard_map/all_to_all | solution.py:342
  18.5 0.0 all-gather.2.cloned.1.call-start
  18.5 1.5 shard_map.113.home_ref
  20.0 0.0 copy-start.1
  20.0 4.8 %shard_map.112 = bf16[256,6400]{1,0:T(8,128)(2,1)} custom-call(bf16[160,2560]{1,0:T(8,128)(2,1)} %query_ref.1, bf16[160,2560]{1,0:T(8,128)(2,1)} %grad_ref.1, bf16[256,160]{1,0:T(8,128)(2,1)} %get-tuple-element.21.m1_ref, bf16[4,256,160]{2,1,0:T(8,128)(2,1)} %get-tuple-element.22.m2_ref), custom_call_target="tpu_custom_call" | custom-call | flops 99999997952 | bytes 6553600 | tf_op jit(solution)/shard_map/pallas_call | solution.py:364
  24.8 0.0 copy-done.1
  24.8 0.1 reshape.51
  24.9 0.6 pad_add_fusion.info_ref
  25.5 6.6 %all-to-all-done = bf16[32,8,1408]{2,1,0:T(8,128)(2,1)} async-done(((bf16[32,8,1408]{2,1,0:T(8,128)(2,1)}), bf16[32,8,1408]{2,1,0:T(8,128)(2,1)}, u32[]{:S(2)}, u32[]{:S(2)}) %all-to-all-start) | async-done | bytes 720928 | tf_op jit(solution)/shard_map/all_to_all | solution.py:342
  32.1 2.3 %shard_map.114 = bf16[160,1024]{1,0:T(8,128)(2,1)} custom-call(bf16[256,1408]{1,0:T(8,128)(2,1)} %bitcast.3.recv_ref.landing_ref), custom_call_target="tpu_custom_call" | custom-call | flops 167772160 | bytes 1572864 | tf_op jit(solution)/shard_map/pallas_call | solution.py:375
  34.4 0.0 all-gather.2.cloned.1.call-update
  34.4 0.0 reduce-scatter.2.cloned.1.call-start
  34.4 45.8 %all_to_all.20 = bf16[32,8,6400]{2,1,0:T(8,128)(2,1)} all-to-all(bf16[32,8,6400]{2,1,0:T(8,128)(2,1)} %bitcast.13), channel_id=1, replica_groups=mesh['dp'=32,'pack'=8] {'dp'}, dimensions={0} | all-to-all | bytes 6553600 | tf_op jit(solution)/shard_map/all_to_all | solution.py:342
  80.3 0.0 all-gather.2.cloned.1.call-done.key_ref.value_ref
  80.3 21.6 %shard_map.115 = (bf16[1280,1024]{1,0:T(8,128)(2,1)}, bf16[256,6400]{1,0:T(8,128)(2,1)}) custom-call(s32[7]{0:T(128)} %pad_add_fusion.info_ref, f32[2]{0:T(128)} %bitcast.22, bf16[256,6400]{1,0:T(8,128)(2,1)} %bitcast.15, bf16[256,6400]{1,0:T(8,128)(2,1)} %bitcast.16, bf16[1280,1024]{1,0:T(8,128)(2,1)} %all-gather.2.cloned.1.call-done.key_ref.value_ref, ...), custom_call_target="tpu_custom_call" | custom-call | flops 6291456000 | bytes 8192000 | tf_op jit(solution)/shard_map/pallas_call | solution.py:394
  101.9 0.0 reduce-scatter.2.cloned.1.call-update
  101.9 0.0 copy-start
  101.9 4.3 %all-to-all-start.2 = ((bf16[32,8,6400]{2,1,0:T(8,128)(2,1)}), bf16[32,8,6400]{2,1,0:T(8,128)(2,1)S(1)}, u32[]{:S(2)}, u32[]{:S(2)}) async-start(bf16[32,8,6400]{2,1,0:T(8,128)(2,1)} %bitcast.14), calls=%async_computation.2 | async-start | bytes 6553600 | tf_op jit(solution)/shard_map/all_to_all | solution.py:342
  106.2 34.8 %reduce-scatter.2.cloned.1.call-done.source_ref = bf16[160,1024]{1,0:T(8,128)(2,1)} async-done(((bf16[1280,1024]{1,0:T(8,128)(2,1)}), bf16[160,1024]{1,0:T(8,128)(2,1)}) %reduce-scatter.2.cloned.1.call-update) | async-done | bytes 327696 | tf_op jit(solution)/shard_map/reduce_scatter | solution.py:433
  141.1 2.3 %shard_map.116 = bf16[256,1280]{1,0:T(8,128)(2,1)} custom-call(bf16[160,1024]{1,0:T(8,128)(2,1)} %reduce-scatter.2.cloned.1.call-done.source_ref, bf16[256,1408]{1,0:T(8,128)(2,1)} %bitcast.3.recv_ref.landing_ref), custom_call_target="tpu_custom_call" | custom-call | flops 167772160 | bytes 1310720 | tf_op jit(solution)/shard_map/pallas_call | solution.py:434
  143.4 4.0 %all-to-all-done.2 = bf16[32,8,6400]{2,1,0:T(8,128)(2,1)S(1)} async-done(((bf16[32,8,6400]{2,1,0:T(8,128)(2,1)}), bf16[32,8,6400]{2,1,0:T(8,128)(2,1)S(1)}, u32[]{:S(2)}, u32[]{:S(2)}) %all-to-all-start.2) | async-done | bytes 3276832 | tf_op jit(solution)/shard_map/all_to_all | solution.py:342
  147.4 7.7 %all-to-all-start.3 = ((bf16[32,8,1280]{2,1,0:T(8,128)(2,1)}), bf16[32,8,1280]{2,1,0:T(8,128)(2,1)}, u32[]{:S(2)}, u32[]{:S(2)}) async-start(bf16[32,8,1280]{2,1,0:T(8,128)(2,1)} %bitcast.17), calls=%async_computation.4 | async-start | bytes 1310720 | tf_op jit(solution)/shard_map/all_to_all | solution.py:342
  155.1 0.0 copy-done
  155.1 2.2 %shard_map.117 = (bf16[160,2560]{1,0:T(8,128)(2,1)}, bf16[160,2560]{1,0:T(8,128)(2,1)}) custom-call(bf16[256,6400]{1,0:T(8,128)(2,1)S(1)} %bitcast.12, s32[160,128]{1,0:T(8,128)S(1)} %copy-done), custom_call_target="tpu_custom_call" | custom-call | flops 99999997952 | bytes 6553600 | tf_op jit(solution)/shard_map/pallas_call | solution.py:445
  157.3 10.8 %all-to-all-done.3 = bf16[32,8,1280]{2,1,0:T(8,128)(2,1)} async-done(((bf16[32,8,1280]{2,1,0:T(8,128)(2,1)}), bf16[32,8,1280]{2,1,0:T(8,128)(2,1)}, u32[]{:S(2)}, u32[]{:S(2)}) %all-to-all-start.3) | async-done | bytes 655392 | tf_op jit(solution)/shard_map/all_to_all | solution.py:342
  168.1 2.2 %shard_map.118 = (bf16[160,512]{1,0:T(8,128)(2,1)}, bf16[160,512]{1,0:T(8,128)(2,1)}) custom-call(bf16[256,1280]{1,0:T(8,128)(2,1)} %bitcast.11.recv_ref, s32[160,128]{1,0:T(8,128)S(1)} %copy-done), custom_call_target="tpu_custom_call" | custom-call | flops 167772160 | bytes 1048576 | tf_op jit(solution)/shard_map/pallas_call | solution.py:451
Async XLA Ops:
  9.8 22.3 %all-to-all-start = ((bf16[32,8,1408]{2,1,0:T(8,128)(2,1)}), bf16[32,8,1408]{2,1,0:T(8,128)(2,1)}, u32[]{:S(2)}, u32[]{:S(2)}) async-start(bf16[32,8,1408]{2,1,0:T(8,128)(2,1)} %bitcast.18), calls=%async_computation | async-start | bytes 1441792 | tf_op jit(solution)/shard_map/all_to_all | solution.py:342
  18.5 61.8 %all-gather.2.cloned.1.call-start = ((), (), s32[]{:S(2)}) async-start(), calls=%async_computation.5 | async-start | bytes 2949120 | tf_op jit(solution)/shard_map/all_gather | solution.py:381
  20.0 4.8 %copy-start.1 = (s32[1,2,3]{2,1,0:T(2,128)S(1)}, s32[1,2,3]{2,1,0:T(2,128)}, u32[]{:S(2)}) copy-start(s32[1,2,3]{2,1,0:T(2,128)} %param.13) | copy-start | bytes 76
  34.4 106.7 %reduce-scatter.2.cloned.1.call-start = ((), (), s32[]{:S(2)}) async-start(), calls=%async_computation.6 | async-start | bytes 2949120 | tf_op jit(solution)/shard_map/reduce_scatter | solution.py:433
  101.9 53.2 %copy-start = (s32[160,128]{1,0:T(8,128)S(1)}, s32[160,128]{1,0:T(8,128)}, u32[]{:S(2)}) copy-start(s32[160,128]{1,0:T(8,128)} %shard_map.113.home_ref) | copy-start | bytes 245764
  101.9 45.5 %all-to-all-start.2 = ((bf16[32,8,6400]{2,1,0:T(8,128)(2,1)}), bf16[32,8,6400]{2,1,0:T(8,128)(2,1)S(1)}, u32[]{:S(2)}, u32[]{:S(2)}) async-start(bf16[32,8,6400]{2,1,0:T(8,128)(2,1)} %bitcast.14), calls=%async_computation.2 | async-start | bytes 6553600 | tf_op jit(solution)/shard_map/all_to_all | solution.py:342
  147.4 20.7 %all-to-all-start.3 = ((bf16[32,8,1280]{2,1,0:T(8,128)(2,1)}), bf16[32,8,1280]{2,1,0:T(8,128)(2,1)}, u32[]{:S(2)}, u32[]{:S(2)}) async-start(bf16[32,8,1280]{2,1,0:T(8,128)(2,1)} %bitcast.17), calls=%async_computation.4 | async-start | bytes 1310720 | tf_op jit(solution)/shard_map/all_to_all | solution.py:342
Sparse Core Ops, SparseCore 0:
  34.5 38.3 all-gather.1
  102.1 38.9 reduce-scatter.1

commit v5 on v4

--- a/solution.py
+++ b/solution.py
@@ -224,19 +224,34 @@
 
 
 def attention_kernel(
-    info_ref, weight_ref, main_ref, spare_ref, key_ref, value_ref, landing_ref,
-    kv_ref, send_ref, bias, spare_sum, value_ones, raised, dscore, score, dprob, ready, left,
-    r1, r2, r1t, r2t,
+    info_ref, weight_ref, recv_ref, key_ref, value_ref, landing_ref,
+    kv_ref, send_ref, bias, spare_sum, value_ones, raised, dscore, score, dprob,
+    held, ready, kv_own, r12, r1t, r2t, arrived, left, kv_left,
 ):
     step = pl.program_id(0)
     rows, keys = bias.shape
     count = len(score)
     steps = KV_HEADS // count
 
-    def leave(k):
-        first = k * count * BOTH_WIDTH
-        columns = pl.ds(first, BOTH_WIDTH if k == steps else count * BOTH_WIDTH)
-        return pltpu.make_async_copy(ready.at[:, columns], send_ref.at[:, columns], left.at[k])
+    main = KV_HEADS * BOTH_WIDTH
+    slots = held.shape[0]
+
+    def arrive(part):
+        columns = pl.ds(main, BOTH_WIDTH)
+        if part < steps:
+            columns = pl.ds(part * count * BOTH_WIDTH, count * BOTH_WIDTH)
+        return pltpu.make_async_copy(recv_ref.at[:, columns], held.at[:, columns], arrived.at[part])
+
+    def leave(block):
+        start = block * BOTH_WIDTH if isinstance(block, int) else pl.multiple_of(block * BOTH_WIDTH, BOTH_WIDTH)
+        columns = pl.ds(start, BOTH_WIDTH)
+        return pltpu.make_async_copy(ready.at[:, columns], send_ref.at[:, columns], left.at[block])
+
+    def leave_kv(g):
+        start = g * PAIR_WIDTH if isinstance(g, int) else pl.multiple_of(g * PAIR_WIDTH, PAIR_WIDTH)
+        return pltpu.make_async_copy(
+            kv_own.at[g], kv_ref.at[:, pl.ds(start, PAIR_WIDTH)], kv_left.at[g]
+        )
 
     e0, e1, e2, e3, e4, _ = ends_of(info_ref)
     place = info_ref[6] * rows + iota((rows, 1), 0)
@@ -244,6 +259,8 @@
 
     @pl.when(step == 0)
     def _():
+        for part in (steps, *range(steps)):
+            arrive(part).start()
         first = jnp.where(place >= e2, e2, 0)
         hidden_from = jnp.where(place >= e4, e3, jnp.where(rejected, e0, 0))
         hidden_to = jnp.where(place >= e4, e4, jnp.where(rejected, e1, 0))
@@ -252,22 +269,30 @@
         bias[...] = jnp.where(seen, 0.0, MASKED)
         spare_sum[...] = jnp.zeros_like(spare_sum)
         landing = landing_of(landing_ref[...])
-        r1[...], down = down_maps(rows, *landing)
+        r1, down = down_maps(rows, *landing)
         r1t[...], across = across_maps(rows, *landing_rows(*landing))
         for g in range(KV_HEADS):
-            r2[g] = down[g]
+            r12[g, :slots] = r1
+            r12[g, slots:] = down[g]
             r2t[g] = across[g]
         for n in range(count):
             value_ones[n][:, HEAD_DIM:] = jnp.ones((keys, HEAD_DIM), jnp.bfloat16)
+        arrive(steps).wait()
+
+    for part in range(steps):
+
+        @pl.when(step == part)
+        def _():
+            arrive(part).wait()
 
     weight = jnp.where(place >= e2, weight_ref[1], weight_ref[0])
     factor = jnp.where(rejected | (place >= e4), -weight, weight)
     query, cotangent, key, inverse, attended, delta = ([None] * count for _ in range(6))
     for n in range(count):
         columns = slice(n * HEAD_DIM, (n + 1) * HEAD_DIM)
-        both = dot(r1t[...], main_ref[:, n * BOTH_WIDTH : (n + 1) * BOTH_WIDTH]) + dot(
-            r2t[step * count + n], spare_ref[...]
-        )
+        g = step * count + n
+        start = pl.multiple_of(g * BOTH_WIDTH, BOTH_WIDTH)
+        both = dot(r1t[...], held[:, pl.ds(start, BOTH_WIDTH)]) + dot(r2t[g], held[:, main:])
         query[n] = stack_heads(low(both[:, :GROUP_WIDTH]))
         cotangent[n] = stack_heads(low(factor * both[:, GROUP_WIDTH:]))
         key[n] = key_ref[:, columns]
@@ -294,30 +319,28 @@
     for n in range(count):
         dscore[n][...] = raised[n][...] * low(dprob[n][...] - delta[n])
     for n in range(count):
+        g = step * count + n
         scaled = inverse[n] * SCALING
-        query_grad = low(dot(dscore[n][...], key[n]) * scaled)
         query_low = low(query[n].astype(jnp.float32) * scaled)
         cotangent_low = low(cotangent[n].astype(jnp.float32) * inverse[n])
-        first = n * PAIR_WIDTH
-        kv_ref[:, first : first + HEAD_DIM] = low(dot(query_low.T, dscore[n][...])).T
-        kv_ref[:, first + HEAD_DIM : first + PAIR_WIDTH] = low(dot(cotangent_low.T, raised[n][...])).T
+        kv_own[g, :, :HEAD_DIM] = low(dot(query_low.T, dscore[n][...])).T
+        kv_own[g, :, HEAD_DIM:] = low(dot(cotangent_low.T, raised[n][...])).T
+        leave_kv(g).start()
+        query_grad = low(dot(dscore[n][...], key[n]) * scaled)
         both = jnp.concatenate([unstack_heads(attended[n]), unstack_heads(query_grad)], axis=1)
-        start = pl.multiple_of((step * count + n) * BOTH_WIDTH, BOTH_WIDTH)
-        ready[:, pl.ds(start, BOTH_WIDTH)] = low(dot(r1[...], both))
-        spare_sum[...] += dot(r2[step * count + n], both)
-
-    for k in range(steps):
-
-        @pl.when(step == k)
-        def _():
-            leave(k).start()
+        placed = dot(r12[g], both)
+        ready[:, pl.ds(pl.multiple_of(g * BOTH_WIDTH, BOTH_WIDTH), BOTH_WIDTH)] = low(placed[:slots])
+        leave(g).start()
+        spare_sum[...] += placed[slots:]
 
     @pl.when(step == steps - 1)
     def _():
-        ready[:, KV_HEADS * BOTH_WIDTH :] = low(spare_sum[...])
-        leave(steps).start()
-        for k in range(steps + 1):
-            leave(k).wait()
+        ready[:, main:] = low(spare_sum[...])
+        leave(KV_HEADS).start()
+        for block in range(KV_HEADS):
+            leave(block).wait()
+            leave_kv(block).wait()
+        leave(KV_HEADS).wait()
 
 
 def shape(dims, kind=jnp.bfloat16):
@@ -383,6 +406,7 @@
     query_recv = exchange(query_send)
 
     smem = pl.BlockSpec(memory_space=pltpu.SMEM)
+    anywhere = pl.BlockSpec(memory_space=pl.ANY)
     at_once = 2
     landing_spec = pl.BlockSpec((slots, HEAD_DIM), lambda g: (0, narrow // HEAD_DIM))
     steps = KV_HEADS // at_once
@@ -397,15 +421,14 @@
         in_specs=[
             smem,
             smem,
-            pl.BlockSpec((slots, at_once * BOTH_WIDTH), lambda g: (0, g)),
-            pl.BlockSpec((slots, BOTH_WIDTH), lambda g: (0, KV_HEADS)),
+            anywhere,
             pl.BlockSpec((seq, at_once * HEAD_DIM), lambda g: (0, g)),
             pl.BlockSpec((seq, at_once * HEAD_DIM), lambda g: (0, steps + g)),
             landing_spec,
         ],
         out_specs=(
-            pl.BlockSpec((seq, at_once * PAIR_WIDTH), lambda g: (0, g)),
-            pl.BlockSpec(memory_space=pl.ANY),
+            anywhere,
+            anywhere,
         ),
         out_shape=(shape((seq, 2 * KV_WIDTH)), shape((slots, wide))),
         scratch_shapes=[
@@ -417,16 +440,19 @@
             several((GROUP * rows, seq), jnp.float32),
             several((GROUP * rows, seq), jnp.float32),
             pltpu.VMEM((slots, wide), jnp.bfloat16),
-            pltpu.SemaphoreType.DMA((steps + 1,)),
-            pltpu.VMEM((slots, rows), jnp.bfloat16),
-            pltpu.VMEM((KV_HEADS, slots, rows), jnp.bfloat16),
+            pltpu.VMEM((slots, wide), jnp.bfloat16),
+            pltpu.VMEM((KV_HEADS, seq, PAIR_WIDTH), jnp.bfloat16),
+            pltpu.VMEM((KV_HEADS, 2 * slots, rows), jnp.bfloat16),
             pltpu.VMEM((rows, slots), jnp.bfloat16),
             pltpu.VMEM((KV_HEADS, rows, slots), jnp.bfloat16),
+            pltpu.SemaphoreType.DMA((steps + 1,)),
+            pltpu.SemaphoreType.DMA((KV_HEADS + 1,)),
+            pltpu.SemaphoreType.DMA((KV_HEADS,)),
         ],
         compiler_params=compiler_params(dimension_semantics=("arbitrary",)),
         cost_estimate=cost(12 * work, 2 * HEADS * rows * seq, HEADS * rows * seq),
     )(
-        info, pair_weight.reshape(2), query_recv, query_recv, kv_all, kv_all, kv_recv,
+        info, pair_weight.reshape(2), query_recv, kv_all, kv_all, kv_recv,
     )
 
     back_recv = exchange(back_send)

time: 178 us -> 182 us (1.022)
  Pallas kernels: 39.5 us -> 43.5 us
    pallas_call x1, Pallas kernels: 21.6 us -> 25.6 us  [body(): pl.pallas_call(attention_kernel, grid=(steps,), in_specs=[smem, smem, any...]
where the time goes in v5:
time: 182 us; the launch traced here: 181 us
  waiting for transfers between devices  56.4 us (31%)
  blocking collectives  45.8 us (25%)
  Pallas kernels  43.5 us (24%)
  starting transfers between devices  20.7 us (11%)
  between operations  14.1 us (8%)
    all_to_all x1, blocking collectives, exchange(): lax.all_to_all(block.reshape(ranks, MAIN, block.shape[1]), 'dp', split_ax...  45.8 us
    reduce_scatter x1, waiting for transfers between devices, body(): kv_grad = lax.psum_scatter(kv_part, 'pack', scatter_dimension=0, tiled=True)  34.8 us
    pallas_call x1, Pallas kernels, body(): pl.pallas_call(attention_kernel, grid=(steps,), in_specs=[smem, smem, any...  25.6 us
    all_to_all x3, waiting for transfers between devices, exchange(): lax.all_to_all(block.reshape(ranks, MAIN, block.shape[1]), 'dp', split_ax...  21.5 us
    all_to_all x3, starting transfers between devices, exchange(): lax.all_to_all(block.reshape(ranks, MAIN, block.shape[1]), 'dp', split_ax...  20.6 us
    pallas_call x1, Pallas kernels, body(): pl.pallas_call(pack_queries_kernel, out_shape=shape((slots, wide)), compi...  4.78 us
  transfers between devices with their start and end apart: 5, of which 4 were waited for; matrix products, arithmetic and copies ran while one was open for 0% of the time, Pallas kernels for 6%

profile of v5, /device:TPU:1, one launch (start us, length us, event | category | flops | bytes accessed | tf_op | source)
XLA Modules:
  0.0 181.1 jit_solution(12710198065567767263)
XLA Ops:
  7.2 2.6 %shard_map.111 = (bf16[256,1408]{1,0:T(8,128)(2,1)}, bf16[256,160]{1,0:T(8,128)(2,1)}, bf16[4,256,160]{2,1,0:T(8,128)(2,1)}) custom-call(s32[1,160]{1,0:T(1,128)} %bitcast.19, s32[1,160]{1,0:T(1,128)} %bitcast.18, bf16[160,512]{1,0:T(8,128)(2,1)} %keys_ref.1, bf16[160,512]{1,0:T(8,128)(2,1)} %values_ref.1), custom_call_target="tpu_custom_call" | custom-call | flops 167772160 | bytes 1572864 | tf_op jit(solution)/shard_map/pallas_call | solution.py:373
  9.8 8.6 %all-to-all-start = ((bf16[32,8,1408]{2,1,0:T(8,128)(2,1)}), bf16[32,8,1408]{2,1,0:T(8,128)(2,1)}, u32[]{:S(2)}, u32[]{:S(2)}) async-start(bf16[32,8,1408]{2,1,0:T(8,128)(2,1)} %bitcast.17), calls=%async_computation | async-start | bytes 1441792 | tf_op jit(solution)/shard_map/all_to_all | solution.py:365
  18.5 0.0 all-gather.2.cloned.1.call-start
  18.5 1.5 shard_map.113.home_ref
  20.0 0.0 copy-start.1
  20.0 4.8 %shard_map.112 = bf16[256,6400]{1,0:T(8,128)(2,1)} custom-call(bf16[160,2560]{1,0:T(8,128)(2,1)} %query_ref.1, bf16[160,2560]{1,0:T(8,128)(2,1)} %grad_ref.1, bf16[256,160]{1,0:T(8,128)(2,1)} %get-tuple-element.21.m1_ref, bf16[4,256,160]{2,1,0:T(8,128)(2,1)} %get-tuple-element.22.m2_ref), custom_call_target="tpu_custom_call" | custom-call | flops 99999997952 | bytes 6553600 | tf_op jit(solution)/shard_map/pallas_call | solution.py:387
  24.8 0.0 copy-done.1
  24.8 0.1 reshape.51
  24.9 0.6 pad_add_fusion.info_ref
  25.5 6.6 %all-to-all-done = bf16[32,8,1408]{2,1,0:T(8,128)(2,1)} async-done(((bf16[32,8,1408]{2,1,0:T(8,128)(2,1)}), bf16[32,8,1408]{2,1,0:T(8,128)(2,1)}, u32[]{:S(2)}, u32[]{:S(2)}) %all-to-all-start) | async-done | bytes 720928 | tf_op jit(solution)/shard_map/all_to_all | solution.py:365
  32.1 2.3 %shard_map.114 = bf16[160,1024]{1,0:T(8,128)(2,1)} custom-call(bf16[256,1408]{1,0:T(8,128)(2,1)} %bitcast.3.recv_ref.landing_ref), custom_call_target="tpu_custom_call" | custom-call | flops 167772160 | bytes 1572864 | tf_op jit(solution)/shard_map/pallas_call | solution.py:398
  34.4 0.0 all-gather.2.cloned.1.call-update
  34.4 0.0 reduce-scatter.2.cloned.1.call-start
  34.4 45.8 %all_to_all.20 = bf16[32,8,6400]{2,1,0:T(8,128)(2,1)} all-to-all(bf16[32,8,6400]{2,1,0:T(8,128)(2,1)} %bitcast.13), channel_id=1, replica_groups=mesh['dp'=32,'pack'=8] {'dp'}, dimensions={0} | all-to-all | bytes 6553600 | tf_op jit(solution)/shard_map/all_to_all | solution.py:365
  80.3 0.0 all-gather.2.cloned.1.call-done.key_ref.value_ref
  80.3 25.6 %shard_map.115 = (bf16[1280,1024]{1,0:T(8,128)(2,1)}, bf16[256,6400]{1,0:T(8,128)(2,1)}) custom-call(s32[7]{0:T(128)} %pad_add_fusion.info_ref, f32[2]{0:T(128)} %bitcast.21, bf16[256,6400]{1,0:T(8,128)(2,1)} %bitcast.15, bf16[1280,1024]{1,0:T(8,128)(2,1)} %all-gather.2.cloned.1.call-done.key_ref.value_ref, ...), custom_call_target="tpu_custom_call" | custom-call | flops 6291456000 | bytes 8192000 | tf_op jit(solution)/shard_map/pallas_call | solution.py:418
  105.9 0.0 reduce-scatter.2.cloned.1.call-update
  105.9 0.0 copy-start
  105.9 4.3 %all-to-all-start.2 = ((bf16[32,8,6400]{2,1,0:T(8,128)(2,1)}), bf16[32,8,6400]{2,1,0:T(8,128)(2,1)S(1)}, u32[]{:S(2)}, u32[]{:S(2)}) async-start(bf16[32,8,6400]{2,1,0:T(8,128)(2,1)} %bitcast.14), calls=%async_computation.2 | async-start | bytes 6553600 | tf_op jit(solution)/shard_map/all_to_all | solution.py:365
  110.2 34.8 %reduce-scatter.2.cloned.1.call-done.source_ref = bf16[160,1024]{1,0:T(8,128)(2,1)} async-done(((bf16[1280,1024]{1,0:T(8,128)(2,1)}), bf16[160,1024]{1,0:T(8,128)(2,1)}) %reduce-scatter.2.cloned.1.call-update) | async-done | bytes 327696 | tf_op jit(solution)/shard_map/reduce_scatter | solution.py:459
  145.0 2.3 %shard_map.116 = bf16[256,1280]{1,0:T(8,128)(2,1)} custom-call(bf16[160,1024]{1,0:T(8,128)(2,1)} %reduce-scatter.2.cloned.1.call-done.source_ref, bf16[256,1408]{1,0:T(8,128)(2,1)} %bitcast.3.recv_ref.landing_ref), custom_call_target="tpu_custom_call" | custom-call | flops 167772160 | bytes 1310720 | tf_op jit(solution)/shard_map/pallas_call | solution.py:460
  147.3 4.1 %all-to-all-done.2 = bf16[32,8,6400]{2,1,0:T(8,128)(2,1)S(1)} async-done(((bf16[32,8,6400]{2,1,0:T(8,128)(2,1)}), bf16[32,8,6400]{2,1,0:T(8,128)(2,1)S(1)}, u32[]{:S(2)}, u32[]{:S(2)}) %all-to-all-start.2) | async-done | bytes 3276832 | tf_op jit(solution)/shard_map/all_to_all | solution.py:365
  151.4 7.7 %all-to-all-start.3 = ((bf16[32,8,1280]{2,1,0:T(8,128)(2,1)}), bf16[32,8,1280]{2,1,0:T(8,128)(2,1)}, u32[]{:S(2)}, u32[]{:S(2)}) async-start(bf16[32,8,1280]{2,1,0:T(8,128)(2,1)} %bitcast.16), calls=%async_computation.4 | async-start | bytes 1310720 | tf_op jit(solution)/shard_map/all_to_all | solution.py:365
  159.1 0.0 copy-done
  159.1 2.2 %shard_map.117 = (bf16[160,2560]{1,0:T(8,128)(2,1)}, bf16[160,2560]{1,0:T(8,128)(2,1)}) custom-call(bf16[256,6400]{1,0:T(8,128)(2,1)S(1)} %bitcast.12, s32[160,128]{1,0:T(8,128)S(1)} %copy-done), custom_call_target="tpu_custom_call" | custom-call | flops 99999997952 | bytes 6553600 | tf_op jit(solution)/shard_map/pallas_call | solution.py:471
  161.3 10.8 %all-to-all-done.3 = bf16[32,8,1280]{2,1,0:T(8,128)(2,1)} async-done(((bf16[32,8,1280]{2,1,0:T(8,128)(2,1)}), bf16[32,8,1280]{2,1,0:T(8,128)(2,1)}, u32[]{:S(2)}, u32[]{:S(2)}) %all-to-all-start.3) | async-done | bytes 655392 | tf_op jit(solution)/shard_map/all_to_all | solution.py:365
  172.1 2.2 %shard_map.118 = (bf16[160,512]{1,0:T(8,128)(2,1)}, bf16[160,512]{1,0:T(8,128)(2,1)}) custom-call(bf16[256,1280]{1,0:T(8,128)(2,1)} %bitcast.11.recv_ref, s32[160,128]{1,0:T(8,128)S(1)} %copy-done), custom_call_target="tpu_custom_call" | custom-call | flops 167772160 | bytes 1048576 | tf_op jit(solution)/shard_map/pallas_call | solution.py:477
Async XLA Ops:
  9.8 22.3 %all-to-all-start = ((bf16[32,8,1408]{2,1,0:T(8,128)(2,1)}), bf16[32,8,1408]{2,1,0:T(8,128)(2,1)}, u32[]{:S(2)}, u32[]{:S(2)}) async-start(bf16[32,8,1408]{2,1,0:T(8,128)(2,1)} %bitcast.17), calls=%async_computation | async-start | bytes 1441792 | tf_op jit(solution)/shard_map/all_to_all | solution.py:365
  18.5 61.8 %all-gather.2.cloned.1.call-start = ((), (), s32[]{:S(2)}) async-start(), calls=%async_computation.5 | async-start | bytes 2949120 | tf_op jit(solution)/shard_map/all_gather | solution.py:404
  20.0 4.8 %copy-start.1 = (s32[1,2,3]{2,1,0:T(2,128)S(1)}, s32[1,2,3]{2,1,0:T(2,128)}, u32[]{:S(2)}) copy-start(s32[1,2,3]{2,1,0:T(2,128)} %param.13) | copy-start | bytes 76
  34.4 110.6 %reduce-scatter.2.cloned.1.call-start = ((), (), s32[]{:S(2)}) async-start(), calls=%async_computation.6 | async-start | bytes 2949120 | tf_op jit(solution)/shard_map/reduce_scatter | solution.py:459
  105.9 53.2 %copy-start = (s32[160,128]{1,0:T(8,128)S(1)}, s32[160,128]{1,0:T(8,128)}, u32[]{:S(2)}) copy-start(s32[160,128]{1,0:T(8,128)} %shard_map.113.home_ref) | copy-start | bytes 245764
  105.9 45.5 %all-to-all-start.2 = ((bf16[32,8,6400]{2,1,0:T(8,128)(2,1)}), bf16[32,8,6400]{2,1,0:T(8,128)(2,1)S(1)}, u32[]{:S(2)}, u32[]{:S(2)}) async-start(bf16[32,8,6400]{2,1,0:T(8,128)(2,1)} %bitcast.14), calls=%async_computation.2 | async-start | bytes 6553600 | tf_op jit(solution)/shard_map/all_to_all | solution.py:365
  151.4 20.7 %all-to-all-start.3 = ((bf16[32,8,1280]{2,1,0:T(8,128)(2,1)}), bf16[32,8,1280]{2,1,0:T(8,128)(2,1)}, u32[]{:S(2)}, u32[]{:S(2)}) async-start(bf16[32,8,1280]{2,1,0:T(8,128)(2,1)} %bitcast.16), calls=%async_computation.4 | async-start | bytes 1310720 | tf_op jit(solution)/shard_map/all_to_all | solution.py:365
Sparse Core Ops, SparseCore 0:
  34.5 38.3 all-gather.1
  106.0 38.9 reduce-scatter.1

commit v6 on v4

--- a/solution.py
+++ b/solution.py
@@ -225,19 +225,12 @@
 
 def attention_kernel(
     info_ref, weight_ref, main_ref, spare_ref, key_ref, value_ref, landing_ref,
-    kv_ref, send_ref, bias, spare_sum, value_ones, raised, dscore, score, dprob, ready, left,
-    r1, r2, r1t, r2t,
+    kv_ref, send_ref, bias, spare_sum, value_ones, raised, dscore, score, dprob, r12, r1t, r2t,
 ):
     step = pl.program_id(0)
     rows, keys = bias.shape
     count = len(score)
-    steps = KV_HEADS // count
-
-    def leave(k):
-        first = k * count * BOTH_WIDTH
-        columns = pl.ds(first, BOTH_WIDTH if k == steps else count * BOTH_WIDTH)
-        return pltpu.make_async_copy(ready.at[:, columns], send_ref.at[:, columns], left.at[k])
-
+    slots = main_ref.shape[0]
     e0, e1, e2, e3, e4, _ = ends_of(info_ref)
     place = info_ref[6] * rows + iota((rows, 1), 0)
     rejected = (place >= e1) & (place < e2)
@@ -252,10 +245,11 @@
         bias[...] = jnp.where(seen, 0.0, MASKED)
         spare_sum[...] = jnp.zeros_like(spare_sum)
         landing = landing_of(landing_ref[...])
-        r1[...], down = down_maps(rows, *landing)
+        r1, down = down_maps(rows, *landing)
         r1t[...], across = across_maps(rows, *landing_rows(*landing))
         for g in range(KV_HEADS):
-            r2[g] = down[g]
+            r12[g, :slots] = r1
+            r12[g, slots:] = down[g]
             r2t[g] = across[g]
         for n in range(count):
             value_ones[n][:, HEAD_DIM:] = jnp.ones((keys, HEAD_DIM), jnp.bfloat16)
@@ -303,21 +297,13 @@
         kv_ref[:, first + HEAD_DIM : first + PAIR_WIDTH] = low(dot(cotangent_low.T, raised[n][...])).T
         both = jnp.concatenate([unstack_heads(attended[n]), unstack_heads(query_grad)], axis=1)
         start = pl.multiple_of((step * count + n) * BOTH_WIDTH, BOTH_WIDTH)
-        ready[:, pl.ds(start, BOTH_WIDTH)] = low(dot(r1[...], both))
-        spare_sum[...] += dot(r2[step * count + n], both)
-
-    for k in range(steps):
-
-        @pl.when(step == k)
-        def _():
-            leave(k).start()
-
-    @pl.when(step == steps - 1)
+        placed = dot(r12[step * count + n], both)
+        send_ref[:, pl.ds(start, BOTH_WIDTH)] = low(placed[:slots])
+        spare_sum[...] += placed[slots:]
+
+    @pl.when(step == KV_HEADS // count - 1)
     def _():
-        ready[:, KV_HEADS * BOTH_WIDTH :] = low(spare_sum[...])
-        leave(steps).start()
-        for k in range(steps + 1):
-            leave(k).wait()
+        send_ref[:, KV_HEADS * BOTH_WIDTH :] = low(spare_sum[...])
 
 
 def shape(dims, kind=jnp.bfloat16):
@@ -405,7 +391,7 @@
         ],
         out_specs=(
             pl.BlockSpec((seq, at_once * PAIR_WIDTH), lambda g: (0, g)),
-            pl.BlockSpec(memory_space=pl.ANY),
+            pl.BlockSpec((slots, wide), lambda g: (0, 0)),
         ),
         out_shape=(shape((seq, 2 * KV_WIDTH)), shape((slots, wide))),
         scratch_shapes=[
@@ -416,10 +402,7 @@
             several((GROUP * rows, seq)),
             several((GROUP * rows, seq), jnp.float32),
             several((GROUP * rows, seq), jnp.float32),
-            pltpu.VMEM((slots, wide), jnp.bfloat16),
-            pltpu.SemaphoreType.DMA((steps + 1,)),
-            pltpu.VMEM((slots, rows), jnp.bfloat16),
-            pltpu.VMEM((KV_HEADS, slots, rows), jnp.bfloat16),
+            pltpu.VMEM((KV_HEADS, 2 * slots, rows), jnp.bfloat16),
             pltpu.VMEM((rows, slots), jnp.bfloat16),
             pltpu.VMEM((KV_HEADS, rows, slots), jnp.bfloat16),
         ],

time: 178 us -> 177 us (level)
  no operation moved by 1% of the time
where the time goes in v6:
time: 177 us; the launch traced here: 176 us
  waiting for transfers between devices  56.4 us (32%)
  blocking collectives  45.8 us (26%)
  Pallas kernels  38.8 us (22%)
  starting transfers between devices  20.6 us (12%)
  between operations  14.1 us (8%)
    all_to_all x1, blocking collectives, exchange(): lax.all_to_all(block.reshape(ranks, MAIN, block.shape[1]), 'dp', split_ax...  45.8 us
    reduce_scatter x1, waiting for transfers between devices, body(): kv_grad = lax.psum_scatter(kv_part, 'pack', scatter_dimension=0, tiled=True)  34.8 us
    all_to_all x3, waiting for transfers between devices, exchange(): lax.all_to_all(block.reshape(ranks, MAIN, block.shape[1]), 'dp', split_ax...  21.5 us
    pallas_call x1, Pallas kernels, body(): pl.pallas_call(attention_kernel, grid=(steps,), in_specs=[smem, smem, pl....  20.9 us
    all_to_all x3, starting transfers between devices, exchange(): lax.all_to_all(block.reshape(ranks, MAIN, block.shape[1]), 'dp', split_ax...  20.6 us
    pallas_call x1, Pallas kernels, body(): pl.pallas_call(pack_queries_kernel, out_shape=shape((slots, wide)), compi...  4.78 us
  transfers between devices with their start and end apart: 5, of which 4 were waited for; matrix products, arithmetic and copies ran while one was open for 0% of the time, Pallas kernels for 6%

profile of v6, /device:TPU:1, one launch (start us, length us, event | category | flops | bytes accessed | tf_op | source)
XLA Modules:
  0.0 176.3 jit_solution(14590815532442316474)
XLA Ops:
  7.2 2.6 %shard_map.111 = (bf16[256,1408]{1,0:T(8,128)(2,1)}, bf16[256,160]{1,0:T(8,128)(2,1)}, bf16[4,256,160]{2,1,0:T(8,128)(2,1)}) custom-call(s32[1,160]{1,0:T(1,128)} %bitcast.20, s32[1,160]{1,0:T(1,128)} %bitcast.19, bf16[160,512]{1,0:T(8,128)(2,1)} %keys_ref.1, bf16[160,512]{1,0:T(8,128)(2,1)} %values_ref.1), custom_call_target="tpu_custom_call" | custom-call | flops 167772160 | bytes 1572864 | tf_op jit(solution)/shard_map/pallas_call | solution.py:336
  9.8 8.6 %all-to-all-start = ((bf16[32,8,1408]{2,1,0:T(8,128)(2,1)}), bf16[32,8,1408]{2,1,0:T(8,128)(2,1)}, u32[]{:S(2)}, u32[]{:S(2)}) async-start(bf16[32,8,1408]{2,1,0:T(8,128)(2,1)} %bitcast.18), calls=%async_computation | async-start | bytes 1441792 | tf_op jit(solution)/shard_map/all_to_all | solution.py:328
  18.5 0.0 all-gather.2.cloned.1.call-start
  18.5 1.5 shard_map.113.home_ref
  20.0 0.0 copy-start.1
  20.0 4.8 %shard_map.112 = bf16[256,6400]{1,0:T(8,128)(2,1)} custom-call(bf16[160,2560]{1,0:T(8,128)(2,1)} %query_ref.1, bf16[160,2560]{1,0:T(8,128)(2,1)} %grad_ref.1, bf16[256,160]{1,0:T(8,128)(2,1)} %get-tuple-element.21.m1_ref, bf16[4,256,160]{2,1,0:T(8,128)(2,1)} %get-tuple-element.22.m2_ref), custom_call_target="tpu_custom_call" | custom-call | flops 99999997952 | bytes 6553600 | tf_op jit(solution)/shard_map/pallas_call | solution.py:350
  24.8 0.0 copy-done.1
  24.8 0.1 reshape.51
  24.9 0.6 pad_add_fusion.info_ref
  25.5 6.6 %all-to-all-done = bf16[32,8,1408]{2,1,0:T(8,128)(2,1)} async-done(((bf16[32,8,1408]{2,1,0:T(8,128)(2,1)}), bf16[32,8,1408]{2,1,0:T(8,128)(2,1)}, u32[]{:S(2)}, u32[]{:S(2)}) %all-to-all-start) | async-done | bytes 720928 | tf_op jit(solution)/shard_map/all_to_all | solution.py:328
  32.1 2.3 %shard_map.114 = bf16[160,1024]{1,0:T(8,128)(2,1)} custom-call(bf16[256,1408]{1,0:T(8,128)(2,1)} %bitcast.3.recv_ref.landing_ref), custom_call_target="tpu_custom_call" | custom-call | flops 167772160 | bytes 1572864 | tf_op jit(solution)/shard_map/pallas_call | solution.py:361
  34.4 0.0 all-gather.2.cloned.1.call-update
  34.4 0.0 reduce-scatter.2.cloned.1.call-start
  34.4 45.8 %all_to_all.20 = bf16[32,8,6400]{2,1,0:T(8,128)(2,1)} all-to-all(bf16[32,8,6400]{2,1,0:T(8,128)(2,1)} %bitcast.13), channel_id=1, replica_groups=mesh['dp'=32,'pack'=8] {'dp'}, dimensions={0} | all-to-all | bytes 6553600 | tf_op jit(solution)/shard_map/all_to_all | solution.py:328
  80.3 0.0 all-gather.2.cloned.1.call-done.key_ref.value_ref
  80.3 20.9 %shard_map.115 = (bf16[1280,1024]{1,0:T(8,128)(2,1)}, bf16[256,6400]{1,0:T(8,128)(2,1)}) custom-call(s32[7]{0:T(128)} %pad_add_fusion.info_ref, f32[2]{0:T(128)} %bitcast.22, bf16[256,6400]{1,0:T(8,128)(2,1)} %bitcast.15, bf16[256,6400]{1,0:T(8,128)(2,1)} %bitcast.16, bf16[1280,1024]{1,0:T(8,128)(2,1)} %all-gather.2.cloned.1.call-done.key_ref.value_ref, ...), custom_call_target="tpu_custom_call" | custom-call | flops 6291456000 | bytes 8192000 | tf_op jit(solution)/shard_map/pallas_call | solution.py:380
  101.1 0.0 reduce-scatter.2.cloned.1.call-update
  101.2 0.0 copy-start
  101.2 4.3 %all-to-all-start.2 = ((bf16[32,8,6400]{2,1,0:T(8,128)(2,1)}), bf16[32,8,6400]{2,1,0:T(8,128)(2,1)S(1)}, u32[]{:S(2)}, u32[]{:S(2)}) async-start(bf16[32,8,6400]{2,1,0:T(8,128)(2,1)} %bitcast.14), calls=%async_computation.2 | async-start | bytes 6553600 | tf_op jit(solution)/shard_map/all_to_all | solution.py:328
  105.4 34.8 %reduce-scatter.2.cloned.1.call-done.source_ref = bf16[160,1024]{1,0:T(8,128)(2,1)} async-done(((bf16[1280,1024]{1,0:T(8,128)(2,1)}), bf16[160,1024]{1,0:T(8,128)(2,1)}) %reduce-scatter.2.cloned.1.call-update) | async-done | bytes 327696 | tf_op jit(solution)/shard_map/reduce_scatter | solution.py:416
  140.3 2.3 %shard_map.116 = bf16[256,1280]{1,0:T(8,128)(2,1)} custom-call(bf16[160,1024]{1,0:T(8,128)(2,1)} %reduce-scatter.2.cloned.1.call-done.source_ref, bf16[256,1408]{1,0:T(8,128)(2,1)} %bitcast.3.recv_ref.landing_ref), custom_call_target="tpu_custom_call" | custom-call | flops 167772160 | bytes 1310720 | tf_op jit(solution)/shard_map/pallas_call | solution.py:417
  142.6 4.0 %all-to-all-done.2 = bf16[32,8,6400]{2,1,0:T(8,128)(2,1)S(1)} async-done(((bf16[32,8,6400]{2,1,0:T(8,128)(2,1)}), bf16[32,8,6400]{2,1,0:T(8,128)(2,1)S(1)}, u32[]{:S(2)}, u32[]{:S(2)}) %all-to-all-start.2) | async-done | bytes 3276832 | tf_op jit(solution)/shard_map/all_to_all | solution.py:328
  146.6 7.7 %all-to-all-start.3 = ((bf16[32,8,1280]{2,1,0:T(8,128)(2,1)}), bf16[32,8,1280]{2,1,0:T(8,128)(2,1)}, u32[]{:S(2)}, u32[]{:S(2)}) async-start(bf16[32,8,1280]{2,1,0:T(8,128)(2,1)} %bitcast.17), calls=%async_computation.4 | async-start | bytes 1310720 | tf_op jit(solution)/shard_map/all_to_all | solution.py:328
  154.3 0.0 copy-done
  154.3 2.2 %shard_map.117 = (bf16[160,2560]{1,0:T(8,128)(2,1)}, bf16[160,2560]{1,0:T(8,128)(2,1)}) custom-call(bf16[256,6400]{1,0:T(8,128)(2,1)S(1)} %bitcast.12, s32[160,128]{1,0:T(8,128)S(1)} %copy-done), custom_call_target="tpu_custom_call" | custom-call | flops 99999997952 | bytes 6553600 | tf_op jit(solution)/shard_map/pallas_call | solution.py:428
  156.5 10.8 %all-to-all-done.3 = bf16[32,8,1280]{2,1,0:T(8,128)(2,1)} async-done(((bf16[32,8,1280]{2,1,0:T(8,128)(2,1)}), bf16[32,8,1280]{2,1,0:T(8,128)(2,1)}, u32[]{:S(2)}, u32[]{:S(2)}) %all-to-all-start.3) | async-done | bytes 655392 | tf_op jit(solution)/shard_map/all_to_all | solution.py:328
  167.3 2.2 %shard_map.118 = (bf16[160,512]{1,0:T(8,128)(2,1)}, bf16[160,512]{1,0:T(8,128)(2,1)}) custom-call(bf16[256,1280]{1,0:T(8,128)(2,1)} %bitcast.11.recv_ref, s32[160,128]{1,0:T(8,128)S(1)} %copy-done), custom_call_target="tpu_custom_call" | custom-call | flops 167772160 | bytes 1048576 | tf_op jit(solution)/shard_map/pallas_call | solution.py:434
Async XLA Ops:
  9.8 22.3 %all-to-all-start = ((bf16[32,8,1408]{2,1,0:T(8,128)(2,1)}), bf16[32,8,1408]{2,1,0:T(8,128)(2,1)}, u32[]{:S(2)}, u32[]{:S(2)}) async-start(bf16[32,8,1408]{2,1,0:T(8,128)(2,1)} %bitcast.18), calls=%async_computation | async-start | bytes 1441792 | tf_op jit(solution)/shard_map/all_to_all | solution.py:328
  18.5 61.8 %all-gather.2.cloned.1.call-start = ((), (), s32[]{:S(2)}) async-start(), calls=%async_computation.5 | async-start | bytes 2949120 | tf_op jit(solution)/shard_map/all_gather | solution.py:367
  20.0 4.8 %copy-start.1 = (s32[1,2,3]{2,1,0:T(2,128)S(1)}, s32[1,2,3]{2,1,0:T(2,128)}, u32[]{:S(2)}) copy-start(s32[1,2,3]{2,1,0:T(2,128)} %param.13) | copy-start | bytes 76
  34.4 105.9 %reduce-scatter.2.cloned.1.call-start = ((), (), s32[]{:S(2)}) async-start(), calls=%async_computation.6 | async-start | bytes 2949120 | tf_op jit(solution)/shard_map/reduce_scatter | solution.py:416
  101.2 53.2 %copy-start = (s32[160,128]{1,0:T(8,128)S(1)}, s32[160,128]{1,0:T(8,128)}, u32[]{:S(2)}) copy-start(s32[160,128]{1,0:T(8,128)} %shard_map.113.home_ref) | copy-start | bytes 245764
  101.2 45.5 %all-to-all-start.2 = ((bf16[32,8,6400]{2,1,0:T(8,128)(2,1)}), bf16[32,8,6400]{2,1,0:T(8,128)(2,1)S(1)}, u32[]{:S(2)}, u32[]{:S(2)}) async-start(bf16[32,8,6400]{2,1,0:T(8,128)(2,1)} %bitcast.14), calls=%async_computation.2 | async-start | bytes 6553600 | tf_op jit(solution)/shard_map/all_to_all | solution.py:328
  146.6 20.7 %all-to-all-start.3 = ((bf16[32,8,1280]{2,1,0:T(8,128)(2,1)}), bf16[32,8,1280]{2,1,0:T(8,128)(2,1)}, u32[]{:S(2)}, u32[]{:S(2)}) async-start(bf16[32,8,1280]{2,1,0:T(8,128)(2,1)} %bitcast.17), calls=%async_computation.4 | async-start | bytes 1310720 | tf_op jit(solution)/shard_map/all_to_all | solution.py:328
Sparse Core Ops, SparseCore 0:
  34.5 38.3 all-gather.1
  101.3 38.9 reduce-scatter.1

commit v7 on v6

--- a/solution.py
+++ b/solution.py
@@ -65,35 +65,35 @@
     return jnp.where(rank < MAIN, first, -MAIN), jnp.where(rank < MAIN, -MAIN, first - MAIN)
 
 
-def send_kernel(dest_ref, slot_ref, keys_ref, values_ref, send_ref, p1_ref, p2_ref):
-    rows = keys_ref.shape[0]
-    slots = send_ref.shape[0]
+def home_places(dest_ref):
     dest_row = dest_ref[...]
     _, same, down, across = ranks_of(dest_row)
     rank_row = jnp.sum(jnp.where(same & (down < across), 1.0, 0.0), axis=0, keepdims=True)
-    main_row, spare_row = places_of(dest_row, rank_row)
+    return places_of(dest_row, rank_row)
+
+
+def send_kernel(dest_ref, slot_ref, keys_ref, values_ref, send_ref):
+    rows = keys_ref.shape[0]
+    slots = send_ref.shape[0]
+    main_row, spare_row = home_places(dest_ref)
     slot_down = iota((slots, rows), 0)
-    p1 = slot_down == main_row
-    p1_low = one_hot(p1)
-    p1_ref[...] = p1_low
-    place = (slot_ref[...] + 1).astype(jnp.float32)
-    place_main = jnp.sum(jnp.where(p1, place, 0.0), axis=1, keepdims=True)
-    taken = jnp.zeros((slots, rows), jnp.float32)
+    p1 = one_hot(slot_down == main_row)
+    taken = jnp.zeros((slots, rows), jnp.bfloat16)
     spare = jnp.zeros((slots, PAIR_WIDTH), jnp.float32)
     for g in range(KV_HEADS):
-        p2 = slot_down == spare_row + SPARE * g
-        p2_low = one_hot(p2)
-        p2_ref[g] = p2_low
-        taken += jnp.where(p2, place, 0.0)
+        p2 = one_hot(slot_down == spare_row + SPARE * g)
+        taken += p2
         source = keys_ref if g < 2 else values_ref
         columns = source[:, (g % 2) * PAIR_WIDTH : (g % 2 + 1) * PAIR_WIDTH]
-        send_ref[:, g * PAIR_WIDTH : (g + 1) * PAIR_WIDTH] = low(dot(p1_low, columns))
-        spare += dot(p2_low, columns)
-    place_spare = jnp.sum(taken, axis=1, keepdims=True)
+        send_ref[:, g * PAIR_WIDTH : (g + 1) * PAIR_WIDTH] = low(dot(p1, columns))
+        spare += dot(p2, columns)
     send_ref[:, 4 * PAIR_WIDTH : 5 * PAIR_WIDTH] = low(spare)
-    lane = iota((slots, HEAD_DIM), 1)
+    place = (slot_ref[...] + 1).astype(jnp.float32)
+    line = iota((HEAD_DIM, rows), 0)
+    in_main = low(jnp.where(line == 0, place, 0.0))
+    in_spare = low(jnp.where(line == 1, place, 0.0))
     send_ref[:, 5 * PAIR_WIDTH :] = low(
-        jnp.where(lane == 0, place_main, jnp.where(lane == 1, place_spare, 0.0))
+        dot(p1, in_main, ((1,), (1,))) + dot(taken, in_spare, ((1,), (1,)))
     )
 
 
@@ -123,13 +123,10 @@
     return main_col, spare_col
 
 
-def landing_rows(main_col, spare_col):
-    slots = main_col.shape[0]
-    diagonal = iota((slots, slots), 0) == iota((slots, slots), 1)
-    return (
-        jnp.sum(jnp.where(diagonal, main_col, 0.0), axis=0, keepdims=True).astype(jnp.int32),
-        jnp.sum(jnp.where(diagonal, spare_col, 0.0), axis=0, keepdims=True).astype(jnp.int32),
-    )
+def landing_rows(tile):
+    pick = one_hot(iota((8, HEAD_DIM), 0) == iota((8, HEAD_DIM), 1))
+    both = dot(pick, tile, ((1,), (1,))).astype(jnp.int32)
+    return both[:1, :], both[1:2, :]
 
 
 def across_maps(rows, main_row, spare_row):
@@ -153,21 +150,23 @@
 
 
 def receive_kernel(recv_ref, kv_ref):
-    r1t, r2t = across_maps(kv_ref.shape[0], *landing_rows(*landing_of(recv_ref[:, 5 * PAIR_WIDTH :])))
+    r1t, r2t = across_maps(kv_ref.shape[0], *landing_rows(recv_ref[:, 5 * PAIR_WIDTH :]))
     spare = recv_ref[:, 4 * PAIR_WIDTH : 5 * PAIR_WIDTH]
     for g in range(KV_HEADS):
         columns = slice(g * PAIR_WIDTH, (g + 1) * PAIR_WIDTH)
         kv_ref[:, columns] = low(dot(r1t, recv_ref[:, columns]) + dot(r2t[g], spare))
 
 
-def pack_queries_kernel(query_ref, grad_ref, m1_ref, m2_ref, send_ref):
-    m1 = m1_ref[...]
+def pack_queries_kernel(dest_ref, query_ref, grad_ref, send_ref):
+    slot_down = iota((send_ref.shape[0], query_ref.shape[0]), 0)
+    main_row, spare_row = home_places(dest_ref)
+    m1 = one_hot(slot_down == main_row)
     spare = jnp.zeros((send_ref.shape[0], BOTH_WIDTH), jnp.float32)
     for g in range(KV_HEADS):
         columns = slice(g * GROUP_WIDTH, (g + 1) * GROUP_WIDTH)
         part = jnp.concatenate([query_ref[:, columns], grad_ref[:, columns]], axis=1)
         send_ref[:, g * BOTH_WIDTH : (g + 1) * BOTH_WIDTH] = low(dot(m1, part))
-        spare += dot(m2_ref[g], part)
+        spare += dot(one_hot(slot_down == spare_row + SPARE * g), part)
     send_ref[:, KV_HEADS * BOTH_WIDTH :] = low(spare)
 
 
@@ -244,9 +243,9 @@
         seen = (other >= first) & (other <= place) & ((other < hidden_from) | (other >= hidden_to))
         bias[...] = jnp.where(seen, 0.0, MASKED)
         spare_sum[...] = jnp.zeros_like(spare_sum)
-        landing = landing_of(landing_ref[...])
-        r1, down = down_maps(rows, *landing)
-        r1t[...], across = across_maps(rows, *landing_rows(*landing))
+        landing = landing_ref[...]
+        r1, down = down_maps(rows, *landing_of(landing))
+        r1t[...], across = across_maps(rows, *landing_rows(landing))
         for g in range(KV_HEADS):
             r12[g, :slots] = r1
             r12[g, slots:] = down[g]
@@ -330,12 +329,11 @@
         )
         return moved.reshape(block.shape)
 
-    down = (shape((slots, rows)), shape((KV_HEADS, slots, rows)))
     dest = route_dest.reshape(1, rows)
 
-    kv_send, p1, p2 = pl.pallas_call(
+    kv_send = pl.pallas_call(
         send_kernel,
-        out_shape=(shape((slots, narrow + HEAD_DIM)), *down),
+        out_shape=shape((slots, narrow + HEAD_DIM)),
         compiler_params=compiler_params(),
         cost_estimate=cost(4 * slots * rows * 2 * KV_WIDTH, 6 * slots * 2 * KV_WIDTH),
     )(dest, route_slot.reshape(1, rows), keys, values)
@@ -352,7 +350,7 @@
         out_shape=shape((slots, wide)),
         compiler_params=compiler_params(),
         cost_estimate=cost(LONG, 10 * slots * QUERY_WIDTH),
-    )(queries, out_grad, p1, p2)
+    )(dest, queries, out_grad)
     info = jnp.concatenate(
         [lengths.reshape(6), lax.axis_index("pack").astype(jnp.int32).reshape(1)]
     )

time: 177 us -> 177 us (level)
  no operation moved by 1% of the time
where the time goes in v7:
time: 177 us; the launch traced here: 176 us
  waiting for transfers between devices  56.4 us (32%)
  blocking collectives  45.8 us (26%)
  Pallas kernels  38.6 us (22%)
  starting transfers between devices  20.6 us (12%)
  between operations  14.1 us (8%)
    all_to_all x1, blocking collectives, exchange(): lax.all_to_all(block.reshape(ranks, MAIN, block.shape[1]), 'dp', split_ax...  45.8 us
    reduce_scatter x1, waiting for transfers between devices, body(): kv_grad = lax.psum_scatter(kv_part, 'pack', scatter_dimension=0, tiled=True)  34.9 us
    all_to_all x3, waiting for transfers between devices, exchange(): lax.all_to_all(block.reshape(ranks, MAIN, block.shape[1]), 'dp', split_ax...  21.5 us
    pallas_call x1, Pallas kernels, body(): pl.pallas_call(attention_kernel, grid=(steps,), in_specs=[smem, smem, pl....  20.9 us
    all_to_all x3, starting transfers between devices, exchange(): lax.all_to_all(block.reshape(ranks, MAIN, block.shape[1]), 'dp', split_ax...  20.6 us
    pallas_call x1, Pallas kernels, body(): pl.pallas_call(pack_queries_kernel, out_shape=shape((slots, wide)), compi...  4.72 us
  transfers between devices with their start and end apart: 5, of which 4 were waited for; matrix products, arithmetic and copies ran while one was open for 0% of the time, Pallas kernels for 6%

profile of v7, /device:TPU:1, one launch (start us, length us, event | category | flops | bytes accessed | tf_op | source)
XLA Modules:
  0.0 176.3 jit_solution(14071638337514489818)
XLA Ops:
  7.2 2.5 %shard_map.111 = bf16[256,1408]{1,0:T(8,128)(2,1)} custom-call(s32[1,160]{1,0:T(1,128)} %bitcast.20, s32[1,160]{1,0:T(1,128)} %bitcast.19, bf16[160,512]{1,0:T(8,128)(2,1)} %keys_ref.1, bf16[160,512]{1,0:T(8,128)(2,1)} %values_ref.1), custom_call_target="tpu_custom_call" | custom-call | flops 167772160 | bytes 1572864 | tf_op jit(solution)/shard_map/pallas_call | solution.py:334
  9.7 8.6 %all-to-all-start = ((bf16[32,8,1408]{2,1,0:T(8,128)(2,1)}), bf16[32,8,1408]{2,1,0:T(8,128)(2,1)}, u32[]{:S(2)}, u32[]{:S(2)}) async-start(bf16[32,8,1408]{2,1,0:T(8,128)(2,1)} %bitcast.17), calls=%async_computation | async-start | bytes 1441792 | tf_op jit(solution)/shard_map/all_to_all | solution.py:327
  18.3 0.0 all-gather.2.cloned.1.call-start
  18.4 1.5 shard_map.113.home_ref
  19.9 0.0 copy-start.1
  19.9 4.7 %shard_map.112 = bf16[256,6400]{1,0:T(8,128)(2,1)} custom-call(s32[1,160]{1,0:T(1,128)} %bitcast.22, bf16[160,2560]{1,0:T(8,128)(2,1)} %query_ref.1, bf16[160,2560]{1,0:T(8,128)(2,1)} %grad_ref.1), custom_call_target="tpu_custom_call" | custom-call | flops 99999997952 | bytes 6553600 | tf_op jit(solution)/shard_map/pallas_call | solution.py:348
  24.6 0.0 copy-done.1
  24.6 0.1 reshape.51
  24.7 0.6 pad_add_fusion.info_ref
  25.3 6.7 %all-to-all-done = bf16[32,8,1408]{2,1,0:T(8,128)(2,1)} async-done(((bf16[32,8,1408]{2,1,0:T(8,128)(2,1)}), bf16[32,8,1408]{2,1,0:T(8,128)(2,1)}, u32[]{:S(2)}, u32[]{:S(2)}) %all-to-all-start) | async-done | bytes 720928 | tf_op jit(solution)/shard_map/all_to_all | solution.py:327
  32.0 2.3 %shard_map.114 = bf16[160,1024]{1,0:T(8,128)(2,1)} custom-call(bf16[256,1408]{1,0:T(8,128)(2,1)} %bitcast.3.recv_ref.landing_ref), custom_call_target="tpu_custom_call" | custom-call | flops 167772160 | bytes 1572864 | tf_op jit(solution)/shard_map/pallas_call | solution.py:359
  34.3 0.0 all-gather.2.cloned.1.call-update
  34.3 0.0 reduce-scatter.2.cloned.1.call-start
  34.3 45.8 %all_to_all.20 = bf16[32,8,6400]{2,1,0:T(8,128)(2,1)} all-to-all(bf16[32,8,6400]{2,1,0:T(8,128)(2,1)} %bitcast.13), channel_id=1, replica_groups=mesh['dp'=32,'pack'=8] {'dp'}, dimensions={0} | all-to-all | bytes 6553600 | tf_op jit(solution)/shard_map/all_to_all | solution.py:327
  80.2 0.0 all-gather.2.cloned.1.call-done.key_ref.value_ref
  80.2 20.9 %shard_map.115 = (bf16[1280,1024]{1,0:T(8,128)(2,1)}, bf16[256,6400]{1,0:T(8,128)(2,1)}) custom-call(s32[7]{0:T(128)} %pad_add_fusion.info_ref, f32[2]{0:T(128)} %bitcast.23, bf16[256,6400]{1,0:T(8,128)(2,1)} %bitcast.15, bf16[256,6400]{1,0:T(8,128)(2,1)} %bitcast.16, bf16[1280,1024]{1,0:T(8,128)(2,1)} %all-gather.2.cloned.1.call-done.key_ref.value_ref, ...), custom_call_target="tpu_custom_call" | custom-call | flops 6291456000 | bytes 8192000 | tf_op jit(solution)/shard_map/pallas_call | solution.py:378
  101.1 0.0 reduce-scatter.2.cloned.1.call-update
  101.1 0.0 copy-start
  101.1 4.3 %all-to-all-start.2 = ((bf16[32,8,6400]{2,1,0:T(8,128)(2,1)}), bf16[32,8,6400]{2,1,0:T(8,128)(2,1)S(1)}, u32[]{:S(2)}, u32[]{:S(2)}) async-start(bf16[32,8,6400]{2,1,0:T(8,128)(2,1)} %bitcast.14), calls=%async_computation.2 | async-start | bytes 6553600 | tf_op jit(solution)/shard_map/all_to_all | solution.py:327
  105.4 34.9 %reduce-scatter.2.cloned.1.call-done.source_ref = bf16[160,1024]{1,0:T(8,128)(2,1)} async-done(((bf16[1280,1024]{1,0:T(8,128)(2,1)}), bf16[160,1024]{1,0:T(8,128)(2,1)}) %reduce-scatter.2.cloned.1.call-update) | async-done | bytes 327696 | tf_op jit(solution)/shard_map/reduce_scatter | solution.py:414
  140.3 2.3 %shard_map.116 = bf16[256,1280]{1,0:T(8,128)(2,1)} custom-call(bf16[160,1024]{1,0:T(8,128)(2,1)} %reduce-scatter.2.cloned.1.call-done.source_ref, bf16[256,1408]{1,0:T(8,128)(2,1)} %bitcast.3.recv_ref.landing_ref), custom_call_target="tpu_custom_call" | custom-call | flops 167772160 | bytes 1310720 | tf_op jit(solution)/shard_map/pallas_call | solution.py:415
  142.6 4.0 %all-to-all-done.2 = bf16[32,8,6400]{2,1,0:T(8,128)(2,1)S(1)} async-done(((bf16[32,8,6400]{2,1,0:T(8,128)(2,1)}), bf16[32,8,6400]{2,1,0:T(8,128)(2,1)S(1)}, u32[]{:S(2)}, u32[]{:S(2)}) %all-to-all-start.2) | async-done | bytes 3276832 | tf_op jit(solution)/shard_map/all_to_all | solution.py:327
  146.6 7.7 %all-to-all-start.3 = ((bf16[32,8,1280]{2,1,0:T(8,128)(2,1)}), bf16[32,8,1280]{2,1,0:T(8,128)(2,1)}, u32[]{:S(2)}, u32[]{:S(2)}) async-start(bf16[32,8,1280]{2,1,0:T(8,128)(2,1)} %bitcast.18), calls=%async_computation.4 | async-start | bytes 1310720 | tf_op jit(solution)/shard_map/all_to_all | solution.py:327
  154.2 0.0 copy-done
  154.3 2.2 %shard_map.117 = (bf16[160,2560]{1,0:T(8,128)(2,1)}, bf16[160,2560]{1,0:T(8,128)(2,1)}) custom-call(bf16[256,6400]{1,0:T(8,128)(2,1)S(1)} %bitcast.12, s32[160,128]{1,0:T(8,128)S(1)} %copy-done), custom_call_target="tpu_custom_call" | custom-call | flops 99999997952 | bytes 6553600 | tf_op jit(solution)/shard_map/pallas_call | solution.py:426
  156.4 10.8 %all-to-all-done.3 = bf16[32,8,1280]{2,1,0:T(8,128)(2,1)} async-done(((bf16[32,8,1280]{2,1,0:T(8,128)(2,1)}), bf16[32,8,1280]{2,1,0:T(8,128)(2,1)}, u32[]{:S(2)}, u32[]{:S(2)}) %all-to-all-start.3) | async-done | bytes 655392 | tf_op jit(solution)/shard_map/all_to_all | solution.py:327
  167.2 2.2 %shard_map.118 = (bf16[160,512]{1,0:T(8,128)(2,1)}, bf16[160,512]{1,0:T(8,128)(2,1)}) custom-call(bf16[256,1280]{1,0:T(8,128)(2,1)} %bitcast.11.recv_ref, s32[160,128]{1,0:T(8,128)S(1)} %copy-done), custom_call_target="tpu_custom_call" | custom-call | flops 167772160 | bytes 1048576 | tf_op jit(solution)/shard_map/pallas_call | solution.py:432
Async XLA Ops:
  9.7 22.3 %all-to-all-start = ((bf16[32,8,1408]{2,1,0:T(8,128)(2,1)}), bf16[32,8,1408]{2,1,0:T(8,128)(2,1)}, u32[]{:S(2)}, u32[]{:S(2)}) async-start(bf16[32,8,1408]{2,1,0:T(8,128)(2,1)} %bitcast.17), calls=%async_computation | async-start | bytes 1441792 | tf_op jit(solution)/shard_map/all_to_all | solution.py:327
  18.3 61.9 %all-gather.2.cloned.1.call-start = ((), (), s32[]{:S(2)}) async-start(), calls=%async_computation.5 | async-start | bytes 2949120 | tf_op jit(solution)/shard_map/all_gather | solution.py:365
  19.9 4.7 %copy-start.1 = (s32[1,2,3]{2,1,0:T(2,128)S(1)}, s32[1,2,3]{2,1,0:T(2,128)}, u32[]{:S(2)}) copy-start(s32[1,2,3]{2,1,0:T(2,128)} %param.13) | copy-start | bytes 76
  34.3 106.0 %reduce-scatter.2.cloned.1.call-start = ((), (), s32[]{:S(2)}) async-start(), calls=%async_computation.6 | async-start | bytes 2949120 | tf_op jit(solution)/shard_map/reduce_scatter | solution.py:414
  101.1 53.2 %copy-start = (s32[160,128]{1,0:T(8,128)S(1)}, s32[160,128]{1,0:T(8,128)}, u32[]{:S(2)}) copy-start(s32[160,128]{1,0:T(8,128)} %shard_map.113.home_ref) | copy-start | bytes 245764
  101.1 45.5 %all-to-all-start.2 = ((bf16[32,8,6400]{2,1,0:T(8,128)(2,1)}), bf16[32,8,6400]{2,1,0:T(8,128)(2,1)S(1)}, u32[]{:S(2)}, u32[]{:S(2)}) async-start(bf16[32,8,6400]{2,1,0:T(8,128)(2,1)} %bitcast.14), calls=%async_computation.2 | async-start | bytes 6553600 | tf_op jit(solution)/shard_map/all_to_all | solution.py:327
  146.6 20.7 %all-to-all-start.3 = ((bf16[32,8,1280]{2,1,0:T(8,128)(2,1)}), bf16[32,8,1280]{2,1,0:T(8,128)(2,1)}, u32[]{:S(2)}, u32[]{:S(2)}) async-start(bf16[32,8,1280]{2,1,0:T(8,128)(2,1)} %bitcast.18), calls=%async_computation.4 | async-start | bytes 1310720 | tf_op jit(solution)/shard_map/all_to_all | solution.py:327
Sparse Core Ops, SparseCore 0:
  34.4 38.3 all-gather.1
  101.2 39.0 reduce-scatter.1

commit v8 on v6

--- a/solution.py
+++ b/solution.py
@@ -157,7 +157,8 @@
     spare = recv_ref[:, 4 * PAIR_WIDTH : 5 * PAIR_WIDTH]
     for g in range(KV_HEADS):
         columns = slice(g * PAIR_WIDTH, (g + 1) * PAIR_WIDTH)
-        kv_ref[:, columns] = low(dot(r1t, recv_ref[:, columns]) + dot(r2t[g], spare))
+        maps = jnp.concatenate([r1t, r2t[g]], axis=1)
+        kv_ref[:, columns] = low(dot(maps, jnp.concatenate([recv_ref[:, columns], spare], axis=0)))
 
 
 def pack_queries_kernel(query_ref, grad_ref, m1_ref, m2_ref, send_ref):

time: 177 us -> 177 us (level)
  no operation moved by 1% of the time
where the time goes in v8:
time: 177 us; the launch traced here: 176 us
  waiting for transfers between devices  56.4 us (32%)
  blocking collectives  45.8 us (26%)
  Pallas kernels  38.8 us (22%)
  starting transfers between devices  20.6 us (12%)
  between operations  14.1 us (8%)
    all_to_all x1, blocking collectives, exchange(): lax.all_to_all(block.reshape(ranks, MAIN, block.shape[1]), 'dp', split_ax...  45.8 us
    reduce_scatter x1, waiting for transfers between devices, body(): kv_grad = lax.psum_scatter(kv_part, 'pack', scatter_dimension=0, tiled=True)  35.4 us
    all_to_all x3, waiting for transfers between devices, exchange(): lax.all_to_all(block.reshape(ranks, MAIN, block.shape[1]), 'dp', split_ax...  20.9 us
    pallas_call x1, Pallas kernels, body(): pl.pallas_call(attention_kernel, grid=(steps,), in_specs=[smem, smem, pl....  20.9 us
    all_to_all x3, starting transfers between devices, exchange(): lax.all_to_all(block.reshape(ranks, MAIN, block.shape[1]), 'dp', split_ax...  20.6 us
    pallas_call x1, Pallas kernels, body(): pl.pallas_call(pack_queries_kernel, out_shape=shape((slots, wide)), compi...  4.78 us
  transfers between devices with their start and end apart: 5, of which 4 were waited for; matrix products, arithmetic and copies ran while one was open for 0% of the time, Pallas kernels for 6%

profile of v8, /device:TPU:1, one launch (start us, length us, event | category | flops | bytes accessed | tf_op | source)
XLA Modules:
  0.0 176.3 jit_solution(16681840182231862568)
XLA Ops:
  7.2 2.6 %shard_map.111 = (bf16[256,1408]{1,0:T(8,128)(2,1)}, bf16[256,160]{1,0:T(8,128)(2,1)}, bf16[4,256,160]{2,1,0:T(8,128)(2,1)}) custom-call(s32[1,160]{1,0:T(1,128)} %bitcast.20, s32[1,160]{1,0:T(1,128)} %bitcast.19, bf16[160,512]{1,0:T(8,128)(2,1)} %keys_ref.1, bf16[160,512]{1,0:T(8,128)(2,1)} %values_ref.1), custom_call_target="tpu_custom_call" | custom-call | flops 167772160 | bytes 1572864 | tf_op jit(solution)/shard_map/pallas_call | solution.py:337
  9.8 8.6 %all-to-all-start = ((bf16[32,8,1408]{2,1,0:T(8,128)(2,1)}), bf16[32,8,1408]{2,1,0:T(8,128)(2,1)}, u32[]{:S(2)}, u32[]{:S(2)}) async-start(bf16[32,8,1408]{2,1,0:T(8,128)(2,1)} %bitcast.18), calls=%async_computation | async-start | bytes 1441792 | tf_op jit(solution)/shard_map/all_to_all | solution.py:329
  18.5 0.0 all-gather.2.cloned.1.call-start
  18.5 1.5 shard_map.113.home_ref
  20.0 0.0 copy-start.1
  20.0 4.8 %shard_map.112 = bf16[256,6400]{1,0:T(8,128)(2,1)} custom-call(bf16[160,2560]{1,0:T(8,128)(2,1)} %query_ref.1, bf16[160,2560]{1,0:T(8,128)(2,1)} %grad_ref.1, bf16[256,160]{1,0:T(8,128)(2,1)} %get-tuple-element.21.m1_ref, bf16[4,256,160]{2,1,0:T(8,128)(2,1)} %get-tuple-element.22.m2_ref), custom_call_target="tpu_custom_call" | custom-call | flops 99999997952 | bytes 6553600 | tf_op jit(solution)/shard_map/pallas_call | solution.py:351
  24.8 0.0 copy-done.1
  24.8 0.1 reshape.51
  24.9 0.6 pad_add_fusion.info_ref
  25.5 6.6 %all-to-all-done = bf16[32,8,1408]{2,1,0:T(8,128)(2,1)} async-done(((bf16[32,8,1408]{2,1,0:T(8,128)(2,1)}), bf16[32,8,1408]{2,1,0:T(8,128)(2,1)}, u32[]{:S(2)}, u32[]{:S(2)}) %all-to-all-start) | async-done | bytes 720928 | tf_op jit(solution)/shard_map/all_to_all | solution.py:329
  32.1 2.3 %shard_map.114 = bf16[160,1024]{1,0:T(8,128)(2,1)} custom-call(bf16[256,1408]{1,0:T(8,128)(2,1)} %bitcast.3.recv_ref.landing_ref), custom_call_target="tpu_custom_call" | custom-call | flops 167772160 | bytes 1572864 | tf_op jit(solution)/shard_map/pallas_call | solution.py:362
  34.4 0.0 all-gather.2.cloned.1.call-update
  34.4 0.0 reduce-scatter.2.cloned.1.call-start
  34.4 45.8 %all_to_all.20 = bf16[32,8,6400]{2,1,0:T(8,128)(2,1)} all-to-all(bf16[32,8,6400]{2,1,0:T(8,128)(2,1)} %bitcast.13), channel_id=1, replica_groups=mesh['dp'=32,'pack'=8] {'dp'}, dimensions={0} | all-to-all | bytes 6553600 | tf_op jit(solution)/shard_map/all_to_all | solution.py:329
  80.3 0.0 all-gather.2.cloned.1.call-done.key_ref.value_ref
  80.3 20.9 %shard_map.115 = (bf16[1280,1024]{1,0:T(8,128)(2,1)}, bf16[256,6400]{1,0:T(8,128)(2,1)}) custom-call(s32[7]{0:T(128)} %pad_add_fusion.info_ref, f32[2]{0:T(128)} %bitcast.22, bf16[256,6400]{1,0:T(8,128)(2,1)} %bitcast.15, bf16[256,6400]{1,0:T(8,128)(2,1)} %bitcast.16, bf16[1280,1024]{1,0:T(8,128)(2,1)} %all-gather.2.cloned.1.call-done.key_ref.value_ref, ...), custom_call_target="tpu_custom_call" | custom-call | flops 6291456000 | bytes 8192000 | tf_op jit(solution)/shard_map/pallas_call | solution.py:381
  101.1 0.0 reduce-scatter.2.cloned.1.call-update
  101.2 0.0 copy-start
  101.2 4.3 %all-to-all-start.2 = ((bf16[32,8,6400]{2,1,0:T(8,128)(2,1)}), bf16[32,8,6400]{2,1,0:T(8,128)(2,1)S(1)}, u32[]{:S(2)}, u32[]{:S(2)}) async-start(bf16[32,8,6400]{2,1,0:T(8,128)(2,1)} %bitcast.14), calls=%async_computation.2 | async-start | bytes 6553600 | tf_op jit(solution)/shard_map/all_to_all | solution.py:329
  105.4 35.4 %reduce-scatter.2.cloned.1.call-done.source_ref = bf16[160,1024]{1,0:T(8,128)(2,1)} async-done(((bf16[1280,1024]{1,0:T(8,128)(2,1)}), bf16[160,1024]{1,0:T(8,128)(2,1)}) %reduce-scatter.2.cloned.1.call-update) | async-done | bytes 327696 | tf_op jit(solution)/shard_map/reduce_scatter | solution.py:417
  140.8 2.3 %shard_map.116 = bf16[256,1280]{1,0:T(8,128)(2,1)} custom-call(bf16[160,1024]{1,0:T(8,128)(2,1)} %reduce-scatter.2.cloned.1.call-done.source_ref, bf16[256,1408]{1,0:T(8,128)(2,1)} %bitcast.3.recv_ref.landing_ref), custom_call_target="tpu_custom_call" | custom-call | flops 167772160 | bytes 1310720 | tf_op jit(solution)/shard_map/pallas_call | solution.py:418
  143.2 3.5 %all-to-all-done.2 = bf16[32,8,6400]{2,1,0:T(8,128)(2,1)S(1)} async-done(((bf16[32,8,6400]{2,1,0:T(8,128)(2,1)}), bf16[32,8,6400]{2,1,0:T(8,128)(2,1)S(1)}, u32[]{:S(2)}, u32[]{:S(2)}) %all-to-all-start.2) | async-done | bytes 3276832 | tf_op jit(solution)/shard_map/all_to_all | solution.py:329
  146.6 7.7 %all-to-all-start.3 = ((bf16[32,8,1280]{2,1,0:T(8,128)(2,1)}), bf16[32,8,1280]{2,1,0:T(8,128)(2,1)}, u32[]{:S(2)}, u32[]{:S(2)}) async-start(bf16[32,8,1280]{2,1,0:T(8,128)(2,1)} %bitcast.17), calls=%async_computation.4 | async-start | bytes 1310720 | tf_op jit(solution)/shard_map/all_to_all | solution.py:329
  154.3 0.0 copy-done
  154.3 2.2 %shard_map.117 = (bf16[160,2560]{1,0:T(8,128)(2,1)}, bf16[160,2560]{1,0:T(8,128)(2,1)}) custom-call(bf16[256,6400]{1,0:T(8,128)(2,1)S(1)} %bitcast.12, s32[160,128]{1,0:T(8,128)S(1)} %copy-done), custom_call_target="tpu_custom_call" | custom-call | flops 99999997952 | bytes 6553600 | tf_op jit(solution)/shard_map/pallas_call | solution.py:429
  156.5 10.8 %all-to-all-done.3 = bf16[32,8,1280]{2,1,0:T(8,128)(2,1)} async-done(((bf16[32,8,1280]{2,1,0:T(8,128)(2,1)}), bf16[32,8,1280]{2,1,0:T(8,128)(2,1)}, u32[]{:S(2)}, u32[]{:S(2)}) %all-to-all-start.3) | async-done | bytes 655392 | tf_op jit(solution)/shard_map/all_to_all | solution.py:329
  167.3 2.2 %shard_map.118 = (bf16[160,512]{1,0:T(8,128)(2,1)}, bf16[160,512]{1,0:T(8,128)(2,1)}) custom-call(bf16[256,1280]{1,0:T(8,128)(2,1)} %bitcast.11.recv_ref, s32[160,128]{1,0:T(8,128)S(1)} %copy-done), custom_call_target="tpu_custom_call" | custom-call | flops 167772160 | bytes 1048576 | tf_op jit(solution)/shard_map/pallas_call | solution.py:435
Async XLA Ops:
  9.8 22.3 %all-to-all-start = ((bf16[32,8,1408]{2,1,0:T(8,128)(2,1)}), bf16[32,8,1408]{2,1,0:T(8,128)(2,1)}, u32[]{:S(2)}, u32[]{:S(2)}) async-start(bf16[32,8,1408]{2,1,0:T(8,128)(2,1)} %bitcast.18), calls=%async_computation | async-start | bytes 1441792 | tf_op jit(solution)/shard_map/all_to_all | solution.py:329
  18.5 61.8 %all-gather.2.cloned.1.call-start = ((), (), s32[]{:S(2)}) async-start(), calls=%async_computation.5 | async-start | bytes 2949120 | tf_op jit(solution)/shard_map/all_gather | solution.py:368
  20.0 4.8 %copy-start.1 = (s32[1,2,3]{2,1,0:T(2,128)S(1)}, s32[1,2,3]{2,1,0:T(2,128)}, u32[]{:S(2)}) copy-start(s32[1,2,3]{2,1,0:T(2,128)} %param.13) | copy-start | bytes 76
  34.4 106.5 %reduce-scatter.2.cloned.1.call-start = ((), (), s32[]{:S(2)}) async-start(), calls=%async_computation.6 | async-start | bytes 2949120 | tf_op jit(solution)/shard_map/reduce_scatter | solution.py:417
  101.2 53.2 %copy-start = (s32[160,128]{1,0:T(8,128)S(1)}, s32[160,128]{1,0:T(8,128)}, u32[]{:S(2)}) copy-start(s32[160,128]{1,0:T(8,128)} %shard_map.113.home_ref) | copy-start | bytes 245764
  101.2 45.5 %all-to-all-start.2 = ((bf16[32,8,6400]{2,1,0:T(8,128)(2,1)}), bf16[32,8,6400]{2,1,0:T(8,128)(2,1)S(1)}, u32[]{:S(2)}, u32[]{:S(2)}) async-start(bf16[32,8,6400]{2,1,0:T(8,128)(2,1)} %bitcast.14), calls=%async_computation.2 | async-start | bytes 6553600 | tf_op jit(solution)/shard_map/all_to_all | solution.py:329
  146.6 20.7 %all-to-all-start.3 = ((bf16[32,8,1280]{2,1,0:T(8,128)(2,1)}), bf16[32,8,1280]{2,1,0:T(8,128)(2,1)}, u32[]{:S(2)}, u32[]{:S(2)}) async-start(bf16[32,8,1280]{2,1,0:T(8,128)(2,1)} %bitcast.17), calls=%async_computation.4 | async-start | bytes 1310720 | tf_op jit(solution)/shard_map/all_to_all | solution.py:329
Sparse Core Ops, SparseCore 0:
  34.5 38.3 all-gather.1
  101.3 39.5 reduce-scatter.1
